TPU v7x, 32 devices: a whole 2x2x4 slice. The times are simulated.
32 devices in a mesh: tm: 16 (over z, x, core), head: 2 (over y).
Axes of the slice: x: 2, y: 2, z: 4, core: 2. Of those that a mesh axis runs over, the one named last changes fastest.
Arguments:
- frames: bfloat16 [16, 512, 1152], P('tm', None, 'head'), may hold values from -6 to 6
- modulation: float32 [3, 1152], replicated, may hold values from -4 to 4
- w_qkv: bfloat16 [3, 1152, 1152], P(None, None, 'head'), may hold values from -1 to 1
- w_out: bfloat16 [1152, 1152], P('head'), may hold values from -0.375 to 0.375
- conv_taps: float32 [3, 1152], P(None, 'head'), may hold values from -3 to 3
- anchors: int32 [1], replicated, may hold values from 0 to 15
Outputs:
- block_out: bfloat16 [16, 512, 1152], P('tm', None, 'head')
All inputs are finite; a program needn't handle non-finite values.
Results may differ from a plain program's by a relative error of at most 0.011.
Values may be sent and summed in bfloat16 or wider, within the bound.
No kernel may reach another device: no remote copies, remote signals or barrier semaphores. Data moves between devices by JAX's collectives and lax.ppermute only.
A program may use at most 64 MiB of HBM per device.

v0:
```python
import jax
import jax.numpy as jnp
from jax import lax
from jax.sharding import PartitionSpec as P

HS = 72
SEG = 16


EPSILON = 1e-06


def swapped(block, axis, stride):
    count = lax.axis_size(axis)
    route = []
    for low in range(count):
        high = low | 1 << stride
        if high != low and high < count:
            route += [(low, high), (high, low)]
    return lax.ppermute(block, axis, route)


def extended(x, sides, width):
    for axis, dim in sides:
        size, length = (lax.axis_size(axis), x.shape[dim])
        up = [(i, (i + 1) % size) for i in range(size - 1)]
        down = [(j, i) for i, j in up]
        last = lax.slice_in_dim(x, length - width, length, axis=dim)
        leading = lax.slice_in_dim(x, 0, width, axis=dim)
        before = lax.ppermute(last, axis, up)
        after = lax.ppermute(leading, axis, down)
        x = jnp.concatenate([before, x, after], axis=dim)
    return x


def modulate(frame_rows, modulation):
    values = frame_rows.astype(jnp.float32)
    average = jnp.mean(values, axis=-1, keepdims=True)
    centred = values - average
    variance = jnp.mean(centred * centred, axis=-1, keepdims=True)
    normed = centred * lax.rsqrt(variance + EPSILON)
    return (normed * (1.0 + modulation[1]) + modulation[0]).astype(jnp.bfloat16)


def attend_block(queries, key_rows, value_rows):
    scores = jnp.einsum(
        "qhs,khs->hqk", queries, key_rows, preferred_element_type=jnp.float32
    ) * HS ** (-0.5)
    row_max = jnp.max(scores, axis=-1, keepdims=True)
    weights = jnp.exp(scores - row_max)
    weights = (weights / jnp.sum(weights, axis=-1, keepdims=True)).astype(jnp.bfloat16)
    return jnp.einsum(
        "hqk,khs->qhs", weights, value_rows, preferred_element_type=jnp.float32
    ).astype(jnp.bfloat16)


def local(frames, modulation, w_qkv, w_out, conv_taps, anchors):
    local_frames, tokens, width_dev = frames.shape
    group_size = SEG // local_frames
    tm_pos = lax.axis_index("tm")
    head_pos = lax.axis_index("head")
    gathered = lax.all_gather(frames, "head", axis=2, tiled=True)
    normed = modulate(gathered, modulation)
    projections = jnp.einsum(
        "fpd,cde->cfpe", normed, w_qkv, preferred_element_type=jnp.float32
    ).astype(jnp.bfloat16)
    segment = tm_pos * local_frames // SEG
    anchor_frame = segment * SEG + lax.dynamic_index_in_dim(anchors, segment, 0, keepdims=False)
    is_owner = anchor_frame // local_frames == tm_pos
    anchor_local = anchor_frame % local_frames
    own_part = lax.dynamic_index_in_dim(projections[1:], anchor_local, 1, keepdims=False)
    routed = jnp.where(is_owner, own_part, jnp.zeros_like(own_part))
    for bit_pos in range(group_size.bit_length() - 1):
        routed = routed + swapped(routed, "tm", bit_pos)
    heads_dev = width_dev // HS
    block_rows = min(512, tokens)
    anchor_keys = routed[0].reshape(tokens, heads_dev, HS)
    anchor_values = routed[1].reshape(tokens, heads_dev, HS)

    def frame_attention(pieces):
        queries, own_keys, own_values = pieces
        key_rows = jnp.concatenate([own_keys.reshape(tokens, heads_dev, HS), anchor_keys], axis=0)
        value_rows = jnp.concatenate(
            [own_values.reshape(tokens, heads_dev, HS), anchor_values], axis=0
        )
        query_blocks = queries.reshape(tokens // block_rows, block_rows, heads_dev, HS)

        def one_block(block_queries):
            return attend_block(block_queries, key_rows, value_rows)

        outputs = lax.map(one_block, query_blocks)
        return outputs.reshape(tokens, width_dev)

    attended = lax.map(frame_attention, (projections[0], projections[1], projections[2]))
    partial_terms = jnp.einsum("fpe,ed->fpd", attended, w_out, preferred_element_type=jnp.float32)
    summed = lax.psum_scatter(partial_terms, "head", scatter_dimension=2, tiled=True)
    gate_dev = lax.dynamic_slice_in_dim(modulation[2], head_pos * width_dev, width_dev)
    hidden = (frames.astype(jnp.float32) + gate_dev * summed).astype(jnp.bfloat16)
    padded = extended(hidden, (("tm", 0),), 1).astype(jnp.float32)
    block_out = (
        padded[1:-1]
        + conv_taps[0] * padded[:-2]
        + conv_taps[1] * padded[1:-1]
        + conv_taps[2] * padded[2:]
    )
    return block_out.astype(jnp.bfloat16)


def solution(mesh):
    in_specs = (
        P("tm", None, "head"),
        P(),
        P(None, None, "head"),
        P("head", None),
        P(None, "head"),
        P(),
    )
    out_specs = P("tm", None, "head")
    return jax.shard_map(local, mesh=mesh, in_specs=in_specs, out_specs=out_specs, check_vma=False)
```

profile of v0, /device:TPU:25, one launch (start us, length us, event | category | flops | bytes accessed | tf_op | source)
XLA Modules:
  0.0 277.5 jit_solution(15589532638199122154)
XLA Ops:
  6.5 0.0 copy-start
  6.5 0.0 all-gather.2.cloned.1.call-start
  6.5 0.7 all-gather.2.cloned.1.call-update
  7.3 0.0 all-reduce.3.cloned.1.call-start
  8.0 0.9 add_reduce_fusion
  8.8 23.9 %all-gather.2.cloned.1.call-done = bf16[1,512,1152]{1,2,0:T(8,128)(2,1)} async-done(((bf16[1,512,576]{1,2,0:T(8,128)(2,1)}), bf16[1,512,1152]{1,2,0:T(8,128)(2,1)}) %all-gather.2.cloned.1.call-update) | async-done | bytes 1179664 | tf_op jit(solution)/shard_map/all_gather | solution.py:62
  32.7 0.0 copy-start.1
  32.7 1.6 convert_reduce_fusion
  34.3 0.0 copy-done.1
  34.3 0.4 fusion.8
  34.7 4.7 %convert_bitcast_fusion = bf16[3,1,512,576]{2,3,0,1:T(8,128)(2,1)S(1)} fusion(bf16[3,1152,576]{1,2,0:T(8,128)(2,1)} %param.8, bf16[1,512,1152]{1,2,0:T(8,128)(2,1)S(1)} %copy-done.1, f32[1152]{0:T(1024)S(1)} %get-tuple-element.38, f32[1152]{0:T(1024)S(1)} %get-tuple-element.37, f32[512]{0:T(512)S(1)} %add_rsqrt_fusion, f32[512]{0:T(512)S(1)} %broadcast_multiply_fusion), kind=kOutput, calls=%fused_computation.18 | convolution fusion | flops 2042855424 | bytes 6943744 | tf_op jit(solution)/shard_map/fpd,cde->cfpe/dot_general | solution.py:64
  39.4 0.1 fusion.21
  39.5 0.7 collective-permute-start
  40.2 2.5 collective-permute-done
  42.7 0.1 fusion.46
  42.8 1.3 collective-permute-start.1
  44.1 26.0 %collective-permute-done.1 = bf16[2,512,576]{1,2,0:T(8,128)(2,1)S(1)} collective-permute-done((bf16[2,512,576]{1,2,0:T(8,128)(2,1)S(1)}, bf16[2,512,576]{1,2,0:T(8,128)(2,1)S(1)}, u32[]{:S(2)}, u32[]{:S(2)}) %collective-permute-start.1) | collective-permute-done | bytes 1179680 | tf_op jit(solution)/shard_map/ppermute | solution.py:20
  70.1 0.4 add.90
  70.4 0.3 collective-permute-start.2
  70.8 26.0 %collective-permute-done.2 = bf16[2,512,576]{1,2,0:T(8,128)(2,1)S(1)} collective-permute-done((bf16[2,512,576]{1,2,0:T(8,128)(2,1)S(1)}, bf16[2,512,576]{1,2,0:T(8,128)(2,1)S(1)}, u32[]{:S(2)}, u32[]{:S(2)}) %collective-permute-start.2) | collective-permute-done | bytes 1179680 | tf_op jit(solution)/shard_map/ppermute | solution.py:20
  96.8 0.4 add.91
  97.1 0.3 collective-permute-start.3
  97.4 0.1 fusion.38
  97.6 53.7 %collective-permute-done.3 = bf16[2,512,576]{1,2,0:T(8,128)(2,1)S(1)} collective-permute-done((bf16[2,512,576]{1,2,0:T(8,128)(2,1)S(1)}, bf16[2,512,576]{1,2,0:T(8,128)(2,1)S(1)}, u32[]{:S(2)}, u32[]{:S(2)}) %collective-permute-start.3) | collective-permute-done | bytes 1179680 | tf_op jit(solution)/shard_map/ppermute | solution.py:20
  151.2 0.4 add.92
  151.6 1.1 fusion.39
  152.7 9.5 %fusion.40 = (f32[8,512]{1,0:T(8,128)S(1)}, f32[8,512,1024]{2,1,0:T(8,128)}) fusion(bf16[512,8,72]{0,2,1:T(8,128)(2,1)S(1)} %bitcast.35, bf16[512,8,72]{0,2,1:T(8,128)(2,1)} %bitcast.37, bf16[512,8,72]{0,2,1:T(8,128)(2,1)S(1)} %bitcast.34), kind=kOutput, calls=%fused_computation.56 | convolution fusion | flops 618923008 | bytes 18563072 | tf_op jit(solution)/shard_map/while/body/eval_jaxpr/while/body/eval_jaxpr/sub | solution.py:50
  162.2 8.7 %fusion.14 = bf16[8,72,512]{2,1,0:T(8,128)(2,1)S(1)} fusion(f32[8,512,1024]{2,1,0:T(8,128)} %get-tuple-element.58, f32[8,512]{1,0:T(8,128)S(1)} %get-tuple-element.57, bf16[512,8,72]{0,2,1:T(8,128)(2,1)} %bitcast.36, bf16[512,8,72]{0,2,1:T(8,128)(2,1)S(1)} %bitcast.33), kind=kOutput, calls=%fused_computation.19 | convolution fusion | flops 615022592 | bytes 18563072 | tf_op jit(solution)/shard_map/while/body/eval_jaxpr/while/body/eval_jaxpr/hqk,khs->qhs/dot_general | solution.py:52
  170.9 0.0 copy-done
  170.9 2.6 convolution_bitcast_fusion
  173.5 6.4 %copy.19 = f32[1,512,1152]{1,0,2:T(1,128)} copy(f32[1,512,1152]{2,1,0:T(8,128)} %convolution_bitcast_fusion) | data formatting | bytes 4718592 | tf_op jit(solution)/shard_map/fpe,ed->fpd/dot_general | solution.py:95
  179.9 0.0 all-reduce.3.cloned.1.call-update
  179.9 0.0 copy-start.2
  179.9 0.6 copy-done.4
  180.6 0.6 dynamic-slice.1
  181.8 0.1 dynamic-slice_reduce_fusion
  181.9 66.7 %all-reduce.3.cloned.1.call-done = f32[1,512,1152]{1,0,2:T(1,128)} async-done(((f32[1,512,1152]{1,0,2:T(1,128)}), f32[1,512,1152]{1,0,2:T(1,128)}) %all-reduce.3.cloned.1.call-update) | async-done | bytes 2359312
  248.5 2.1 constant_dynamic-slice_fusion
  250.6 0.0 copy-done.2
  250.6 0.0 copy-start.3
  250.7 0.2 fusion.26
  250.9 3.7 %collective-permute-start.4 = (bf16[1,512,576]{1,2,0:T(8,128)(2,1)S(1)}, bf16[1,512,576]{1,2,0:T(8,128)(2,1)S(1)}, u32[]{:S(2)}, u32[]{:S(2)}) collective-permute-start(bf16[1,512,576]{1,2,0:T(8,128)(2,1)S(1)} %fusion.26), channel_id=1, source_target_pairs={{0,2},{2,4},{4,6},{6,8},{8,10},{10,12},{12,14},{14,16},{16,18},{18... | collective-permute-start | bytes 1769480 | tf_op jit(solution)/shard_map/ppermute | solution.py:30
  254.5 1.9 collective-permute-start.5
  256.5 0.0 copy-done.3
  256.5 4.8 %collective-permute-done.4 = bf16[1,512,576]{1,2,0:T(8,128)(2,1)S(1)} collective-permute-done((bf16[1,512,576]{1,2,0:T(8,128)(2,1)S(1)}, bf16[1,512,576]{1,2,0:T(8,128)(2,1)S(1)}, u32[]{:S(2)}, u32[]{:S(2)}) %collective-permute-start.4) | collective-permute-done | bytes 589856 | tf_op jit(solution)/shard_map/ppermute | solution.py:30
  261.3 7.9 %collective-permute-done.5 = bf16[1,512,576]{1,2,0:T(8,128)(2,1)S(1)} collective-permute-done((bf16[1,512,576]{1,2,0:T(8,128)(2,1)S(1)}, bf16[1,512,576]{1,2,0:T(8,128)(2,1)S(1)}, u32[]{:S(2)}, u32[]{:S(2)}) %collective-permute-start.5) | collective-permute-done | bytes 589856 | tf_op jit(solution)/shard_map/ppermute | solution.py:31
  269.3 0.3 maximum_convert_fusion
  269.5 1.2 fusion.18
  (4 shorter events, 0.0 us)
Async XLA Ops:
  6.5 164.4 %copy-start = (bf16[576,1152]{1,0:T(8,128)(2,1)S(1)}, bf16[576,1152]{1,0:T(8,128)(2,1)}, u32[]{:S(2)}) copy-start(bf16[576,1152]{1,0:T(8,128)(2,1)} %param.9) | copy-start | bytes 3981316
  6.5 26.2 %all-gather.2.cloned.1.call-start = ((), (), s32[]{:S(2)}) async-start(), calls=%async_computation | async-start | bytes 1769472 | tf_op jit(solution)/shard_map/all_gather | solution.py:62
  7.3 241.3 %all-reduce.3.cloned.1.call-start = ((), (), s32[]{:S(2)}) async-start(), calls=%async_computation.1 | async-start | bytes 4718592
  32.7 1.6 copy-start.1
  39.5 3.2 %collective-permute-start = (bf16[2,512,576]{1,2,0:T(8,128)(2,1)S(1)}, bf16[2,512,576]{1,2,0:T(8,128)(2,1)S(1)}, u32[]{:S(2)}, u32[]{:S(2)}) collective-permute-start(bf16[2,512,576]{1,2,0:T(8,128)(2,1)S(1)} %fusion.21), channel_id=1, source_target_pairs={{0,2},{2,0},{4,6},{6,4},{8,10},{10,8},{12,14},{14,12},{16,18},{18,... | collective-permute-start | bytes 3538952 | tf_op jit(solution)/shard_map/ppermute | solution.py:20
  42.8 27.2 %collective-permute-start.1 = (bf16[2,512,576]{1,2,0:T(8,128)(2,1)S(1)}, bf16[2,512,576]{1,2,0:T(8,128)(2,1)S(1)}, u32[]{:S(2)}, u32[]{:S(2)}) collective-permute-start(bf16[2,512,576]{1,2,0:T(8,128)(2,1)S(1)} %fusion.46), channel_id=1, source_target_pairs={{0,4},{4,0},{2,6},{6,2},{8,12},{12,8},{10,14},{14,10},{16,20},{20,... | collective-permute-start | bytes 3538952 | tf_op jit(solution)/shard_map/ppermute | solution.py:20
  70.4 26.3 %collective-permute-start.2 = (bf16[2,512,576]{1,2,0:T(8,128)(2,1)S(1)}, bf16[2,512,576]{1,2,0:T(8,128)(2,1)S(1)}, u32[]{:S(2)}, u32[]{:S(2)}) collective-permute-start(bf16[2,512,576]{1,2,0:T(8,128)(2,1)S(1)} %add.90), channel_id=1, source_target_pairs={{0,8},{8,0},{2,10},{10,2},{4,12},{12,4},{6,14},{14,6},{16,24},{24,... | collective-permute-start | bytes 3538952 | tf_op jit(solution)/shard_map/ppermute | solution.py:20
  97.1 54.1 %collective-permute-start.3 = (bf16[2,512,576]{1,2,0:T(8,128)(2,1)S(1)}, bf16[2,512,576]{1,2,0:T(8,128)(2,1)S(1)}, u32[]{:S(2)}, u32[]{:S(2)}) collective-permute-start(bf16[2,512,576]{1,2,0:T(8,128)(2,1)S(1)} %add.91), channel_id=1, source_target_pairs={{0,16},{16,0},{2,18},{18,2},{4,20},{20,4},{6,22},{22,6},{8,24},{24... | collective-permute-start | bytes 3538952 | tf_op jit(solution)/shard_map/ppermute | solution.py:20
  179.9 0.7 copy-start.4
  179.9 70.7 %copy-start.2 = (bf16[1,512,576]{1,2,0:T(8,128)(2,1)S(1)}, bf16[1,512,576]{1,2,0:T(8,128)(2,1)}, u32[]{:S(2)}) copy-start(bf16[1,512,576]{1,2,0:T(8,128)(2,1)} %param.6) | copy-start | bytes 1769476
  250.6 5.8 %copy-start.3 = (f32[3,576]{1,0:T(4,128)S(1)}, f32[3,576]{1,0:T(4,128)}, u32[]{:S(2)}) copy-start(f32[3,576]{1,0:T(4,128)} %param.10) | copy-start | bytes 20740
  250.9 10.5 %collective-permute-start.4 = (bf16[1,512,576]{1,2,0:T(8,128)(2,1)S(1)}, bf16[1,512,576]{1,2,0:T(8,128)(2,1)S(1)}, u32[]{:S(2)}, u32[]{:S(2)}) collective-permute-start(bf16[1,512,576]{1,2,0:T(8,128)(2,1)S(1)} %fusion.26), channel_id=1, source_target_pairs={{0,2},{2,4},{4,6},{6,8},{8,10},{10,12},{12,14},{14,16},{16,18},{18... | collective-permute-start | bytes 1769480 | tf_op jit(solution)/shard_map/ppermute | solution.py:30
  254.5 14.7 %collective-permute-start.5 = (bf16[1,512,576]{1,2,0:T(8,128)(2,1)S(1)}, bf16[1,512,576]{1,2,0:T(8,128)(2,1)S(1)}, u32[]{:S(2)}, u32[]{:S(2)}) collective-permute-start(bf16[1,512,576]{1,2,0:T(8,128)(2,1)S(1)} %fusion.26), channel_id=1, source_target_pairs={{2,0},{4,2},{6,4},{8,6},{10,8},{12,10},{14,12},{16,14},{18,16},{20... | collective-permute-start | bytes 1769480 | tf_op jit(solution)/shard_map/ppermute | solution.py:31
Sparse Core Ops, SparseCore 0:
  8.9 23.7 all-gather.1
  180.0 68.4 all-reduce.2
where the time goes:
time: 278 us
  waiting for transfers between devices  212 us (76%)
  matrix products  25.5 us (9%)
  between operations  14.8 us (5%)
  local copies, waits for them, and re-layouts  11 us (4%)
  starting transfers between devices  8.25 us (3%)
  other arithmetic  5.76 us (2%)
    ppermute x4, waiting for transfers between devices, swapped(): return lax.ppermute(block, axis, route)  108 us
    unnamed x3, waiting for transfers between devices  67.4 us
    all_gather x1, waiting for transfers between devices, local(): gathered = lax.all_gather(frames, 'head', axis=2, tiled=True)  23.9 us
    sub x1, matrix products, attend_block(): weights = jnp.exp(scores - row_max)  9.51 us
    dot_general x1, matrix products, attend_block(): jnp.einsum('hqk,khs->qhs', weights, value_rows, preferred_element_type=jn...  8.71 us
    ppermute x1, waiting for transfers between devices, extended(): after = lax.ppermute(leading, axis, down)  7.94 us
    dot_general x1, local copies, waits for them, and re-layouts, local(): jnp.einsum('fpe,ed->fpd', attended, w_out, preferred_element_type=jnp.flo...  6.39 us
  transfers between devices with their start and end apart: 8, of which 8 were waited for; matrix products, arithmetic and copies ran while one was open for 1% of the time, Pallas kernels for 0%

commit v1 on v0

v1 whole, which is shorter than its diff:
```python
import functools

import jax
import jax.numpy as jnp
from jax import lax
from jax.experimental import pallas as pl
from jax.experimental.pallas import tpu as pltpu
from jax.sharding import PartitionSpec as P

HS = 72
SEG = 16
LANES = 128
EPSILON = 1e-06
LOG2_E = 1.4426950408889634

IN_CHUNKS = 2
OUT_CHUNKS = 4


def exchanged(block, bit):
    count = lax.axis_size("tm")
    return lax.ppermute(block, "tm", [(i, i ^ bit) for i in range(count)])


def shifted(block, bit, shift):
    frames, heads = lax.axis_size("tm"), lax.axis_size("head")
    route = [
        (f * heads + h, (f ^ bit) * heads + (h + shift) % heads)
        for f in range(frames)
        for h in range(heads)
    ]
    return lax.ppermute(block, ("tm", "head"), route)


def project_kernel(blocks, parts, scales, order_ref, *refs):
    pieces = refs[: blocks * parts]
    modulation_ref, w_ref = refs[blocks * parts : blocks * parts + 2]
    outs = refs[blocks * parts + 2 :]
    first = w_ref.shape[0] - len(outs)
    order = [order_ref[j] for j in range(parts)]
    start = 0
    for block in range(blocks):
        values = [ref[...].astype(jnp.float32) for ref in pieces[block * parts : (block + 1) * parts]]
        rows = values[0].shape[0]
        features = sum(v.shape[1] for v in values)
        average = sum(jnp.sum(v, axis=1, keepdims=True) for v in values) / features
        centred = [v - average for v in values]
        variance = sum(jnp.sum(c * c, axis=1, keepdims=True) for c in centred) / features
        scale = lax.rsqrt(variance + EPSILON)
        normed = [
            (c * scale * (1.0 + modulation_ref[1, k]) + modulation_ref[0, k]).astype(jnp.bfloat16)
            for c, k in zip(centred, order)
        ]
        for index, (out, factor) in enumerate(zip(outs, scales)):
            total = sum(
                jnp.dot(n, w_ref[first + index, k], preferred_element_type=jnp.float32)
                for n, k in zip(normed, order)
            )
            is_value = index == len(outs) - 1
            if factor is not None:
                total = total * factor
            total = total.astype(jnp.bfloat16)
            lane = lax.broadcasted_iota(jnp.int32, (rows, LANES), 1)
            filler = jnp.where(lane == HS, 1.0 if is_value else 0.0, 0.0).astype(jnp.bfloat16)
            for head in range(out.shape[0]):
                out[head, pl.ds(start, rows), :] = filler
                out[head, pl.ds(start, rows), 0:HS] = total[:, head * HS : (head + 1) * HS]
        start += rows


def project(blocks, order, modulation, w_qkv, with_queries):
    parts = len(blocks[0])
    tokens = sum(block[0].shape[0] for block in blocks)
    heads = w_qkv.shape[-1] // HS
    count = 3 if with_queries else 2
    scales = [HS ** (-0.5) * LOG2_E, None, None][3 - count :]
    out = jax.ShapeDtypeStruct((heads, tokens, LANES), jnp.bfloat16)
    vmem = pl.BlockSpec(memory_space=pltpu.VMEM)
    flat = [piece for block in blocks for piece in block]
    width = w_qkv.shape[1] * w_qkv.shape[2]
    return pl.pallas_call(
        functools.partial(project_kernel, len(blocks), parts, scales),
        out_shape=[out] * count,
        in_specs=[pl.BlockSpec(memory_space=pltpu.SMEM)] + [vmem] * (len(flat) + 2),
        out_specs=[vmem] * count,
        compiler_params=pltpu.CompilerParams(vmem_limit_bytes=40 * 2**20),
        cost_estimate=pl.CostEstimate(
            flops=2 * tokens * width * w_qkv.shape[-1] * count,
            bytes_accessed=count * (w_qkv.size // 3 + tokens * heads * LANES) * 2,
            transcendentals=0,
        ),
    )(order, *flat, modulation, w_qkv)


def attend_kernel(
    parts, head_ref, q_ref, ko_ref, vo_ref, ka_ref, va_ref, w_ref, own_ref, send_ref, attended
):
    heads = q_ref.shape[0]
    contract = (((1,), (1,)), ((), ()))
    for head in range(heads):
        queries = q_ref[head]
        own = lax.dot_general(queries, ko_ref[head], contract, preferred_element_type=jnp.float32)
        anchor = lax.dot_general(queries, ka_ref[head], contract, preferred_element_type=jnp.float32)
        top = jnp.maximum(
            jnp.max(own, axis=1, keepdims=True), jnp.max(anchor, axis=1, keepdims=True)
        )
        own = jnp.exp2(own - top).astype(jnp.bfloat16)
        anchor = jnp.exp2(anchor - top).astype(jnp.bfloat16)
        total = jnp.dot(own, vo_ref[head], preferred_element_type=jnp.float32)
        total += jnp.dot(anchor, va_ref[head], preferred_element_type=jnp.float32)
        result = total[:, :HS] / total[:, HS : HS + 1]
        attended[:, head * HS : (head + 1) * HS] = result.astype(jnp.bfloat16)
    terms = jnp.dot(attended[...], w_ref[...], preferred_element_type=jnp.float32)
    width = own_ref.shape[1]
    me = head_ref[0]
    for part in range(parts):
        columns = terms[:, part * width : (part + 1) * width]
        step = lax.rem(part - me + parts, parts)

        @pl.when(step == 0)
        def _():
            own_ref[...] = columns

        @pl.when(step != 0)
        def _():
            send_ref[lax.max(step - 1, 0)] = columns.astype(jnp.bfloat16)


def attend(me, parts, queries, own_kv, anchor_kv, w_out, chunk, chunks):
    heads, tokens, _ = queries.shape
    rows = tokens // chunks
    width = w_out.shape[1] // parts
    vmem = pl.BlockSpec(memory_space=pltpu.VMEM)

    def whole(x):
        return pl.BlockSpec(x.shape, lambda i: (0,) * x.ndim)

    keys = 2 * tokens
    return pl.pallas_call(
        functools.partial(attend_kernel, parts),
        grid=(1,),
        out_shape=[
            jax.ShapeDtypeStruct((rows, width), jnp.float32),
            jax.ShapeDtypeStruct((parts - 1, rows, width), jnp.bfloat16),
        ],
        in_specs=[
            pl.BlockSpec(memory_space=pltpu.SMEM),
            pl.BlockSpec((heads, rows, LANES), lambda i: (0, chunk, 0)),
        ]
        + [whole(x) for x in (*own_kv, *anchor_kv, w_out)],
        out_specs=[
            pl.BlockSpec((rows, width), lambda i: (0, 0)),
            pl.BlockSpec((parts - 1, rows, width), lambda i: (0, 0, 0)),
        ],
        scratch_shapes=[pltpu.VMEM((rows, heads * HS), jnp.bfloat16)],
        compiler_params=pltpu.CompilerParams(vmem_limit_bytes=40 * 2**20),
        cost_estimate=pl.CostEstimate(
            flops=4 * heads * rows * keys * LANES + 2 * rows * w_out.size,
            bytes_accessed=8 * heads * tokens * LANES + 2 * w_out.size,
            transcendentals=heads * rows * keys,
        ),
    )(me, queries, *own_kv, *anchor_kv, w_out)


def anchor_rows(frame, anchor):
    tokens = frame.shape[0]
    heads = lax.axis_size("head")
    index = lax.axis_index("tm") % SEG
    half, quarter = tokens // 2, tokens // 4

    def bit(value, number):
        return (value >> number) & 1

    def same(number):
        return bit(index, number) == bit(anchor, number)

    core, side = bit(index, 0), bit(index, 1)
    kept = lax.dynamic_slice_in_dim(frame, core * half, half, 0)
    sent = lax.dynamic_slice_in_dim(frame, (1 - core) * half, half, 0)
    block = jnp.where(same(0), kept, exchanged(sent, 1))
    kept = lax.dynamic_slice_in_dim(block, side * quarter, quarter, 0)
    sent = lax.dynamic_slice_in_dim(block, (1 - side) * quarter, quarter, 0)
    block = jnp.where(same(1), kept, exchanged(sent, 2))
    for number in range(2, SEG.bit_length() - 1):
        block = jnp.where(same(number), block, exchanged(block, 1 << number))
    rows = []
    for across in (0, 2):
        rows.append(
            [block if across == 0 and step == 0 else shifted(block, across, step) for step in range(heads)]
        )
    return rows + [[exchanged(piece, 1) for piece in row] for row in rows]


def local(frames, modulation, w_qkv, w_out, conv_taps, anchors):
    frame = frames[0]
    tokens, width = frame.shape
    parts = lax.axis_size("head")
    place, me = lax.axis_index("tm"), lax.axis_index("head")
    anchor = lax.dynamic_index_in_dim(anchors, place // SEG, 0, keepdims=False)
    order = ((me - jnp.arange(parts)) % parts).astype(jnp.int32)
    me_ref = me.astype(jnp.int32).reshape(1)
    by_part = modulation.reshape(3, parts, width)
    w_parts = w_qkv.reshape(3, parts, width, width)

    rows = tokens // IN_CHUNKS
    own_rows = []
    for chunk in range(IN_CHUNKS):
        piece = frame[chunk * rows : (chunk + 1) * rows]
        own_rows.append([piece] + [shifted(piece, 0, step) for step in range(1, parts)])
    far_rows = anchor_rows(frame, anchor)
    queries, *own_kv = project(own_rows, order, by_part, w_parts, True)
    anchor_kv = project(far_rows, order, by_part, w_parts, False)

    gate = lax.dynamic_index_in_dim(by_part[2], me, 0, keepdims=False)
    rows = tokens // OUT_CHUNKS
    count = lax.axis_size("tm")
    odd = [(i, i + 1) for i in range(1, count - 1, 2)]
    odd = odd + [(j, i) for i, j in odd]
    outs = []
    is_even = place % 2 == 0
    tap_near = jnp.where(is_even, conv_taps[2], conv_taps[0])
    tap_far = jnp.where(is_even, conv_taps[0], conv_taps[2])
    for chunk in range(OUT_CHUNKS):
        total, send = attend(me_ref, parts, queries, own_kv, anchor_kv, w_out, chunk, OUT_CHUNKS)
        for step in range(1, parts):
            total = total + shifted(send[step - 1], 0, step).astype(jnp.float32)
        piece = frame[chunk * rows : (chunk + 1) * rows].astype(jnp.float32)
        hidden = (piece + gate * total).astype(jnp.bfloat16)
        near = exchanged(hidden, 1).astype(jnp.float32)
        far = lax.ppermute(hidden, "tm", odd).astype(jnp.float32)
        hidden = hidden.astype(jnp.float32)
        out = hidden + conv_taps[1] * hidden + tap_near * near + tap_far * far
        outs.append(out.astype(jnp.bfloat16))
    return jnp.concatenate(outs, axis=0)[None]


def solution(mesh):
    in_specs = (
        P("tm", None, "head"),
        P(),
        P(None, None, "head"),
        P("head", None),
        P(None, "head"),
        P(),
    )
    out_specs = P("tm", None, "head")
    return jax.shard_map(local, mesh=mesh, in_specs=in_specs, out_specs=out_specs, check_vma=False)
```

time: 278 us -> 106 us (0.38)
  waiting for transfers between devices: 212 us -> 35.4 us
  matrix products: 25.5 us -> 0 us
  Pallas kernels: 0 us -> 23.8 us
  starting transfers between devices: 8.25 us -> 30.2 us
  between operations: 14.8 us -> 0.96 us
  other arithmetic: 5.76 us -> 0.89 us
    ppermute x6 -> x25, waiting for transfers between devices: 121 us -> 35.4 us  [the longest x12 16.4 us: exchanged(): return lax.ppermute(block, 'tm', [(i, i ^ bit) for i in range(count)])]
    unnamed x3 -> x0, waiting for transfers between devices: 67.4 us -> none
    all_gather x1 -> x0, waiting for transfers between devices: 23.9 us -> none  [local(): gathered = lax.all_gather(frames, 'head', axis=2, tiled=True)]
    pallas_call x0 -> x6, Pallas kernels: none -> 23.8 us  [the longest x4 14.4 us: attend(): pl.pallas_call(functools.partial(attend_kernel, parts), grid=(1,), out_sh...]
    ppermute x6 -> x25, starting transfers between devices: 8.21 us -> 30.2 us  [the longest x12 13.4 us: exchanged(): return lax.ppermute(block, 'tm', [(i, i ^ bit) for i in range(count)])]
    dot_general x3 -> x0, matrix products: 16 us -> none  [the longest x1 8.71 us: attend_block(): jnp.einsum('hqk,khs->qhs', weights, value_rows, preferred_element_type=jn...]
    sub x1 -> x0, matrix products: 9.51 us -> none  [attend_block(): weights = jnp.exp(scores - row_max)]
    unnamed x12 -> x19, local copies, waits for them, and re-layouts: 3.31 us -> 9.91 us
  transfers between devices with their start and end apart: 8 -> 25, of which waited for: 8 -> 10; matrix products, arithmetic and copies ran while one was open for 1% -> 8% of each run, Pallas kernels for 0% -> 5%
where the time goes in v1:
time: 106 us; the launch traced here: 104 us
  waiting for transfers between devices  35.4 us (33%)
  starting transfers between devices  30.2 us (28%)
  Pallas kernels  23.8 us (22%)
  local copies, waits for them, and re-layouts  13 us (12%)
    ppermute x12, waiting for transfers between devices, exchanged(): return lax.ppermute(block, 'tm', [(i, i ^ bit) for i in range(count)])  16.4 us
    pallas_call x4, Pallas kernels, attend(): pl.pallas_call(functools.partial(attend_kernel, parts), grid=(1,), out_sh...  14.4 us
    ppermute x12, starting transfers between devices, exchanged(): return lax.ppermute(block, 'tm', [(i, i ^ bit) for i in range(count)])  13.4 us
    ppermute x9, waiting for transfers between devices, shifted(): return lax.ppermute(block, ('tm', 'head'), route)  12.6 us
    unnamed x19, local copies, waits for them, and re-layouts  9.91 us
    ppermute x4, starting transfers between devices, local(): far = lax.ppermute(hidden, 'tm', odd).astype(jnp.float32)  9.57 us
    pallas_call x2, Pallas kernels, project(): pl.pallas_call(functools.partial(project_kernel, len(blocks), parts, scal...  9.46 us
    ppermute x9, starting transfers between devices, shifted(): return lax.ppermute(block, ('tm', 'head'), route)  7.31 us
  transfers between devices with their start and end apart: 25, of which 10 were waited for; matrix products, arithmetic and copies ran while one was open for 8% of the time, Pallas kernels for 5%

profile of v1, /device:TPU:25, one launch (start us, length us, event | category | flops | bytes accessed | tf_op | source)
XLA Modules:
  0.0 104.3 jit_solution(4753752636664908694)
XLA Ops:
  0.0 1.3 %constant_dynamic-slice_fusion.2 = (bf16[1,256,576]{1,2,0:T(8,128)(2,1)S(1)}, bf16[1,256,576]{1,2,0:T(8,128)(2,1)S(1)}, bf16[1,256,576]{1,2,0:T(8,128)(2,1)S(1)}, bf16[1,256,576]{1,2,0:T(8,128)(2,1)S(1)}) fusion(bf16[1,512,576]{1,2,0:T(8,128)(2,1)} %param.6, s32[]{:T(128)S(6)} %select_n.86, s32[]{:T(128)S(6)} %select_n.87), kind=kLoop, calls=%fused_computation.41 | loop fusion | bytes 2359304 | tf_op jit(solution)/shard_map/dynamic_slice | solution.py:178
  1.3 0.2 copy.12
  1.5 0.7 collective-permute-start.2
  2.3 0.2 copy.11
  3.1 0.4 collective-permute-done.2
  3.6 1.3 %collective-permute-start.3 = (bf16[128,576]{1,0:T(8,128)(2,1)S(1)}, bf16[128,576]{1,0:T(8,128)(2,1)S(1)}, u32[]{:S(2)}, u32[]{:S(2)}) collective-permute-start(bf16[128,576]{1,0:T(8,128)(2,1)S(1)} %constant_dynamic-slice_fusion), channel_id=1, source_target_pairs={{0,4},{2,6},{4,0},{6,2},{8,12},{10,14},{12,8},{14,10},{16,20},{18,... | collective-permute-start | bytes 442376 | tf_op jit(solution)/shard_map/ppermute | solution.py:22
  4.9 4.2 %collective-permute-done.3 = bf16[128,576]{1,0:T(8,128)(2,1)S(1)} collective-permute-done((bf16[128,576]{1,0:T(8,128)(2,1)S(1)}, bf16[128,576]{1,0:T(8,128)(2,1)S(1)}, u32[]{:S(2)}, u32[]{:S(2)}) %collective-permute-start.3) | collective-permute-done | bytes 147488 | tf_op jit(solution)/shard_map/ppermute | solution.py:22
  9.1 0.2 collective-permute-start.4
  9.3 4.3 %collective-permute-done.4 = bf16[128,576]{1,0:T(8,128)(2,1)S(1)} collective-permute-done((bf16[128,576]{1,0:T(8,128)(2,1)S(1)}, bf16[128,576]{1,0:T(8,128)(2,1)S(1)}, u32[]{:S(2)}, u32[]{:S(2)}) %collective-permute-start.4) | collective-permute-done | bytes 147488 | tf_op jit(solution)/shard_map/ppermute | solution.py:22
  13.8 0.2 copy.18
  14.0 1.3 %collective-permute-start = (bf16[256,576]{1,0:T(8,128)(2,1)S(1)}, bf16[256,576]{1,0:T(8,128)(2,1)S(1)}, u32[]{:S(2)}, u32[]{:S(2)}) collective-permute-start(bf16[256,576]{1,0:T(8,128)(2,1)S(1)} %bitcast.31), channel_id=1, source_target_pairs={{0,1},{1,0},{2,3},{3,2},{4,5},{5,4},{6,7},{7,6},{8,9},{9,8},{10,11... | collective-permute-start | bytes 884744 | tf_op jit(solution)/shard_map/ppermute | solution.py:32
  15.3 0.2 copy.19
  15.5 0.3 collective-permute-start.1
  15.8 7.5 %collective-permute-done.5 = bf16[128,576]{1,0:T(8,128)(2,1)S(1)} collective-permute-done((bf16[128,576]{1,0:T(8,128)(2,1)S(1)}, bf16[128,576]{1,0:T(8,128)(2,1)S(1)}, u32[]{:S(2)}, u32[]{:S(2)}) %collective-permute-start.5) | collective-permute-done | bytes 147488 | tf_op jit(solution)/shard_map/ppermute | solution.py:22
  23.3 1.3 %collective-permute-start.6 = (bf16[128,576]{1,0:T(8,128)(2,1)S(1)}, bf16[128,576]{1,0:T(8,128)(2,1)S(1)}, u32[]{:S(2)}, u32[]{:S(2)}) collective-permute-start(bf16[128,576]{1,0:T(8,128)(2,1)S(1)} %broadcast_select_fusion.1.refs_0_), channel_id=1, source_target_pairs={{0,1},{1,0},{2,3},{3,2},{4,5},{5,4},{6,7},{7,6},{8,9},{9,8},{10,11... | collective-permute-start | bytes 442376 | tf_op jit(solution)/shard_map/ppermute | solution.py:32
  24.6 1.2 %collective-permute-start.7 = (bf16[128,576]{1,0:T(8,128)(2,1)S(1)}, bf16[128,576]{1,0:T(8,128)(2,1)S(1)}, u32[]{:S(2)}, u32[]{:S(2)}) collective-permute-start(bf16[128,576]{1,0:T(8,128)(2,1)S(1)} %broadcast_select_fusion.1.refs_0_), channel_id=1, source_target_pairs={{0,4},{1,5},{2,6},{3,7},{4,0},{5,1},{6,2},{7,3},{8,12},{9,13},{10,... | collective-permute-start | bytes 442376 | tf_op jit(solution)/shard_map/ppermute | solution.py:32
  25.8 0.2 collective-permute-start.8
  26.1 6.6 %copy.10 = bf16[3,1152,576]{2,1,0:T(8,128)(2,1)} copy(bf16[3,1152,576]{1,2,0:T(8,128)(2,1)} %param.8) | data formatting | bytes 7962624 | tf_op args[2]
  32.8 2.3 %collective-permute-start.9 = (bf16[128,576]{1,0:T(8,128)(2,1)S(1)}, bf16[128,576]{1,0:T(8,128)(2,1)S(1)}, u32[]{:S(2)}, u32[]{:S(2)}) collective-permute-start(bf16[128,576]{1,0:T(8,128)(2,1)S(1)} %broadcast_select_fusion.1.refs_0_), channel_id=1, source_target_pairs={{0,2},{2,0},{4,6},{6,4},{8,10},{10,8},{12,14},{14,12},{16,18},{18,... | collective-permute-start | bytes 442376 | tf_op jit(solution)/shard_map/ppermute | solution.py:22
  35.1 3.1 %collective-permute-start.10 = (bf16[128,576]{1,0:T(8,128)(2,1)S(1)}, bf16[128,576]{1,0:T(8,128)(2,1)S(1)}, u32[]{:S(2)}, u32[]{:S(2)}) collective-permute-start(bf16[128,576]{1,0:T(8,128)(2,1)S(1)} %collective-permute-done.6.refs_1_), channel_id=1, source_target_pairs={{0,2},{2,0},{4,6},{6,4},{8,10},{10,8},{12,14},{14,12},{16,18},{18,... | collective-permute-start | bytes 442376 | tf_op jit(solution)/shard_map/ppermute | solution.py:22
  38.3 0.5 collective-permute-start.12
  38.8 2.3 %copy-done.1 = bf16[3,1152,576]{2,1,0:T(8,128)(2,1)S(1)} copy-done((bf16[3,1152,576]{2,1,0:T(8,128)(2,1)S(1)}, bf16[3,1152,576]{2,1,0:T(8,128)(2,1)}, u32[]{:S(2)}) %copy-start.1) | copy-done | bytes 3981336
  41.0 5.3 %shard_map.64 = (bf16[8,512,128]{2,1,0:T(8,128)(2,1)S(1)}, bf16[8,512,128]{2,1,0:T(8,128)(2,1)S(1)}, bf16[8,512,128]{2,1,0:T(8,128)(2,1)S(1)}) custom-call(s32[2]{0:T(128)S(1)} %and_select_fusion.order_ref, bf16[256,576]{1,0:T(8,128)(2,1)S(1)} %bitcast.32, bf16[256,576]{1,0:T(8,128)(2,1)S(1)} %collective-permute-done.refs_1_, bf16[256,576]{1,0:T(8,128)(2,1)S(1)} %bitcast.34, ...), custom_call_target="tpu_custom_call" | custom-call | flops 2038431744 | bytes 7127040 | tf_op jit(solution)/shard_map/pallas_call | solution.py:81
  46.4 4.2 %shard_map.65 = (bf16[8,512,128]{2,1,0:T(8,128)(2,1)S(1)}, bf16[8,512,128]{2,1,0:T(8,128)(2,1)S(1)}) custom-call(s32[2]{0:T(128)S(1)} %and_select_fusion.order_ref, bf16[128,576]{1,0:T(8,128)(2,1)S(1)} %broadcast_select_fusion.1.refs_0_, bf16[128,576]{1,0:T(8,128)(2,1)S(1)} %collective-permute-done.6.refs_1_, ...), custom_call_target="tpu_custom_call" | custom-call | flops 1358954496 | bytes 4751360 | tf_op jit(solution)/shard_map/pallas_call | solution.py:81
  50.6 3.7 %shard_map.69 = (f32[128,576]{1,0:T(8,128)S(1)}, bf16[1,128,576]{2,1,0:T(8,128)(2,1)S(1)}) custom-call(s32[1]{0:T(128)} %bitcast.1.head_ref, bf16[8,512,128]{2,1,0:T(8,128)(2,1)S(1)} %get-tuple-element.18.q_ref, bf16[8,512,128]{2,1,0:T(8,128)(2,1)S(1)} %get-tuple-element.19.ko_ref, bf16[8,512,128]{2,1,0:T(8,128)(2,1)S(1)} %get-tuple-element.20.vo_ref, ...), custom_call_target="tpu_custom_call" | custom-call | flops 706740224 | bytes 5521408 | tf_op jit(solution)/shard_map/pallas_call | solution.py:139
  54.3 3.5 %shard_map.68 = (f32[128,576]{1,0:T(8,128)S(1)}, bf16[1,128,576]{2,1,0:T(8,128)(2,1)S(1)}) custom-call(s32[1]{0:T(128)} %bitcast.1.head_ref, bf16[8,512,128]{2,1,0:T(8,128)(2,1)S(1)} %get-tuple-element.18.q_ref, bf16[8,512,128]{2,1,0:T(8,128)(2,1)S(1)} %get-tuple-element.19.ko_ref, bf16[8,512,128]{2,1,0:T(8,128)(2,1)S(1)} %get-tuple-element.20.vo_ref, ...), custom_call_target="tpu_custom_call" | custom-call | flops 706740224 | bytes 5521408 | tf_op jit(solution)/shard_map/pallas_call | solution.py:139
  57.9 3.5 %shard_map.67 = (f32[128,576]{1,0:T(8,128)S(1)}, bf16[1,128,576]{2,1,0:T(8,128)(2,1)S(1)}) custom-call(s32[1]{0:T(128)} %bitcast.1.head_ref, bf16[8,512,128]{2,1,0:T(8,128)(2,1)S(1)} %get-tuple-element.18.q_ref, bf16[8,512,128]{2,1,0:T(8,128)(2,1)S(1)} %get-tuple-element.19.ko_ref, bf16[8,512,128]{2,1,0:T(8,128)(2,1)S(1)} %get-tuple-element.20.vo_ref, ...), custom_call_target="tpu_custom_call" | custom-call | flops 706740224 | bytes 5521408 | tf_op jit(solution)/shard_map/pallas_call | solution.py:139
  61.4 3.5 %shard_map.66 = (f32[128,576]{1,0:T(8,128)S(1)}, bf16[1,128,576]{2,1,0:T(8,128)(2,1)S(1)}) custom-call(s32[1]{0:T(128)} %bitcast.1.head_ref, bf16[8,512,128]{2,1,0:T(8,128)(2,1)S(1)} %get-tuple-element.18.q_ref, bf16[8,512,128]{2,1,0:T(8,128)(2,1)S(1)} %get-tuple-element.19.ko_ref, bf16[8,512,128]{2,1,0:T(8,128)(2,1)S(1)} %get-tuple-element.20.vo_ref, ...), custom_call_target="tpu_custom_call" | custom-call | flops 706740224 | bytes 5521408 | tf_op jit(solution)/shard_map/pallas_call | solution.py:139
  65.0 1.4 %collective-permute-start.22 = (bf16[128,576]{1,0:T(8,128)(2,1)S(1)}, bf16[128,576]{1,0:T(8,128)(2,1)S(1)}, u32[]{:S(2)}, u32[]{:S(2)}) collective-permute-start(bf16[128,576]{1,0:T(8,128)(2,1)S(1)} %bitcast.38), channel_id=1, source_target_pairs={{0,1},{1,0},{2,3},{3,2},{4,5},{5,4},{6,7},{7,6},{8,9},{9,8},{10,11... | collective-permute-start | bytes 442376 | tf_op jit(solution)/shard_map/ppermute | solution.py:32
  66.5 1.4 %collective-permute-start.16 = (bf16[128,576]{1,0:T(8,128)(2,1)S(1)}, bf16[128,576]{1,0:T(8,128)(2,1)S(1)}, u32[]{:S(2)}, u32[]{:S(2)}) collective-permute-start(bf16[128,576]{1,0:T(8,128)(2,1)S(1)} %bitcast.36), channel_id=1, source_target_pairs={{0,1},{1,0},{2,3},{3,2},{4,5},{5,4},{6,7},{7,6},{8,9},{9,8},{10,11... | collective-permute-start | bytes 442376 | tf_op jit(solution)/shard_map/ppermute | solution.py:32
  68.3 0.2 copy.20
  68.8 2.0 %collective-permute-done.22 = bf16[128,576]{1,0:T(8,128)(2,1)S(1)} collective-permute-done((bf16[128,576]{1,0:T(8,128)(2,1)S(1)}, bf16[128,576]{1,0:T(8,128)(2,1)S(1)}, u32[]{:S(2)}, u32[]{:S(2)}) %collective-permute-start.22) | collective-permute-done | bytes 147488 | tf_op jit(solution)/shard_map/ppermute | solution.py:32
  70.8 3.5 %collective-permute-done.19 = bf16[128,576]{1,0:T(8,128)(2,1)S(1)} collective-permute-done((bf16[128,576]{1,0:T(8,128)(2,1)S(1)}, bf16[128,576]{1,0:T(8,128)(2,1)S(1)}, u32[]{:S(2)}, u32[]{:S(2)}) %collective-permute-start.19) | collective-permute-done | bytes 147488 | tf_op jit(solution)/shard_map/ppermute | solution.py:32
  74.3 3.5 %collective-permute-done.16 = bf16[128,576]{1,0:T(8,128)(2,1)S(1)} collective-permute-done((bf16[128,576]{1,0:T(8,128)(2,1)S(1)}, bf16[128,576]{1,0:T(8,128)(2,1)S(1)}, u32[]{:S(2)}, u32[]{:S(2)}) %collective-permute-start.16) | collective-permute-done | bytes 147488 | tf_op jit(solution)/shard_map/ppermute | solution.py:32
  77.8 3.5 %collective-permute-done.13 = bf16[128,576]{1,0:T(8,128)(2,1)S(1)} collective-permute-done((bf16[128,576]{1,0:T(8,128)(2,1)S(1)}, bf16[128,576]{1,0:T(8,128)(2,1)S(1)}, u32[]{:S(2)}, u32[]{:S(2)}) %collective-permute-start.13) | collective-permute-done | bytes 147488 | tf_op jit(solution)/shard_map/ppermute | solution.py:32
  81.3 0.2 fusion.15
  81.6 0.9 collective-permute-start.14
  82.5 3.0 %collective-permute-start.15 = (bf16[128,576]{1,0:T(8,128)(2,1)S(1)}, bf16[128,576]{1,0:T(8,128)(2,1)S(1)}, u32[]{:S(2)}, u32[]{:S(2)}) collective-permute-start(bf16[128,576]{1,0:T(8,128)(2,1)S(1)} %get-tuple-element.46), channel_id=1, source_target_pairs={{2,4},{6,8},{10,12},{14,16},{18,20},{22,24},{26,28},{4,2},{8,6},{1... | collective-permute-start | bytes 442376 | tf_op jit(solution)/shard_map/ppermute | solution.py:230
  85.5 0.4 collective-permute-start.17
  86.0 2.2 %collective-permute-start.18 = (bf16[128,576]{1,0:T(8,128)(2,1)S(1)}, bf16[128,576]{1,0:T(8,128)(2,1)S(1)}, u32[]{:S(2)}, u32[]{:S(2)}) collective-permute-start(bf16[128,576]{1,0:T(8,128)(2,1)S(1)} %get-tuple-element.47), channel_id=1, source_target_pairs={{2,4},{6,8},{10,12},{14,16},{18,20},{22,24},{26,28},{4,2},{8,6},{1... | collective-permute-start | bytes 442376 | tf_op jit(solution)/shard_map/ppermute | solution.py:230
  88.2 1.0 collective-permute-start.20
  89.2 2.5 %collective-permute-start.21 = (bf16[128,576]{1,0:T(8,128)(2,1)S(1)}, bf16[128,576]{1,0:T(8,128)(2,1)S(1)}, u32[]{:S(2)}, u32[]{:S(2)}) collective-permute-start(bf16[128,576]{1,0:T(8,128)(2,1)S(1)} %get-tuple-element.48), channel_id=1, source_target_pairs={{2,4},{6,8},{10,12},{14,16},{18,20},{22,24},{26,28},{4,2},{8,6},{1... | collective-permute-start | bytes 442376 | tf_op jit(solution)/shard_map/ppermute | solution.py:230
  91.7 2.7 %collective-permute-start.23 = (bf16[128,576]{1,0:T(8,128)(2,1)S(1)}, bf16[128,576]{1,0:T(8,128)(2,1)S(1)}, u32[]{:S(2)}, u32[]{:S(2)}) collective-permute-start(bf16[128,576]{1,0:T(8,128)(2,1)S(1)} %get-tuple-element.49), channel_id=1, source_target_pairs={{0,2},{2,0},{4,6},{6,4},{8,10},{10,8},{12,14},{14,12},{16,18},{18,... | collective-permute-start | bytes 442376 | tf_op jit(solution)/shard_map/ppermute | solution.py:22
  94.3 1.9 %collective-permute-start.24 = (bf16[128,576]{1,0:T(8,128)(2,1)S(1)}, bf16[128,576]{1,0:T(8,128)(2,1)S(1)}, u32[]{:S(2)}, u32[]{:S(2)}) collective-permute-start(bf16[128,576]{1,0:T(8,128)(2,1)S(1)} %get-tuple-element.49), channel_id=1, source_target_pairs={{2,4},{6,8},{10,12},{14,16},{18,20},{22,24},{26,28},{4,2},{8,6},{1... | collective-permute-start | bytes 442376 | tf_op jit(solution)/shard_map/ppermute | solution.py:230
  96.3 1.6 %collective-permute-done.21 = bf16[128,576]{1,0:T(8,128)(2,1)S(1)} collective-permute-done((bf16[128,576]{1,0:T(8,128)(2,1)S(1)}, bf16[128,576]{1,0:T(8,128)(2,1)S(1)}, u32[]{:S(2)}, u32[]{:S(2)}) %collective-permute-start.21) | collective-permute-done | bytes 147488 | tf_op jit(solution)/shard_map/ppermute | solution.py:230
  97.9 4.8 %collective-permute-done.24 = bf16[128,576]{1,0:T(8,128)(2,1)S(1)} collective-permute-done((bf16[128,576]{1,0:T(8,128)(2,1)S(1)}, bf16[128,576]{1,0:T(8,128)(2,1)S(1)}, u32[]{:S(2)}, u32[]{:S(2)}) %collective-permute-start.24) | collective-permute-done | bytes 147488 | tf_op jit(solution)/shard_map/ppermute | solution.py:230
  102.7 0.4 fusion.2
  103.2 1.1 %copy.16 = bf16[1,512,576]{1,2,0:T(8,128)(2,1)} copy(bf16[1,512,576]{2,1,0:T(8,128)(2,1)S(1)} %maximum_bitcast_fusion) | data formatting | bytes 1179648 | tf_op jit(solution)/shard_map/broadcast_in_dim | solution.py:234
  (46 shorter events, 1.4 us)
Async XLA Ops:
  1.5 2.0 %collective-permute-start.2 = (bf16[256,576]{1,0:T(8,128)(2,1)S(1)}, bf16[256,576]{1,0:T(8,128)(2,1)S(1)}, u32[]{:S(2)}, u32[]{:S(2)}) collective-permute-start(bf16[256,576]{1,0:T(8,128)(2,1)S(1)} %bitcast.39), channel_id=1, source_target_pairs={{0,2},{2,0},{4,6},{6,4},{8,10},{10,8},{12,14},{14,12},{16,18},{18,... | collective-permute-start | bytes 884744 | tf_op jit(solution)/shard_map/ppermute | solution.py:22
  3.6 5.5 %collective-permute-start.3 = (bf16[128,576]{1,0:T(8,128)(2,1)S(1)}, bf16[128,576]{1,0:T(8,128)(2,1)S(1)}, u32[]{:S(2)}, u32[]{:S(2)}) collective-permute-start(bf16[128,576]{1,0:T(8,128)(2,1)S(1)} %constant_dynamic-slice_fusion), channel_id=1, source_target_pairs={{0,4},{2,6},{4,0},{6,2},{8,12},{10,14},{12,8},{14,10},{16,20},{18,... | collective-permute-start | bytes 442376 | tf_op jit(solution)/shard_map/ppermute | solution.py:22
  4.9 21.2 %copy-start.4 = (f32[3,1152]{1,0:T(4,128)S(1)}, f32[3,1152]{1,0:T(4,128)}, u32[]{:S(2)}) copy-start(f32[3,1152]{1,0:T(4,128)} %param.7) | copy-start | bytes 41476
  9.1 4.6 %collective-permute-start.4 = (bf16[128,576]{1,0:T(8,128)(2,1)S(1)}, bf16[128,576]{1,0:T(8,128)(2,1)S(1)}, u32[]{:S(2)}, u32[]{:S(2)}) collective-permute-start(bf16[128,576]{1,0:T(8,128)(2,1)S(1)} %dynamic-slice_select_fusion), channel_id=1, source_target_pairs={{0,8},{2,10},{4,12},{6,14},{8,0},{10,2},{12,4},{14,6},{16,24},{18,... | collective-permute-start | bytes 442376 | tf_op jit(solution)/shard_map/ppermute | solution.py:22
  13.7 9.6 %collective-permute-start.5 = (bf16[128,576]{1,0:T(8,128)(2,1)S(1)}, bf16[128,576]{1,0:T(8,128)(2,1)S(1)}, u32[]{:S(2)}, u32[]{:S(2)}) collective-permute-start(bf16[128,576]{1,0:T(8,128)(2,1)S(1)} %broadcast_select_fusion), channel_id=1, source_target_pairs={{0,16},{2,18},{4,20},{6,22},{8,24},{10,26},{12,28},{14,30},{16,0},... | collective-permute-start | bytes 442376 | tf_op jit(solution)/shard_map/ppermute | solution.py:22
  14.0 18.8 %collective-permute-start = (bf16[256,576]{1,0:T(8,128)(2,1)S(1)}, bf16[256,576]{1,0:T(8,128)(2,1)S(1)}, u32[]{:S(2)}, u32[]{:S(2)}) collective-permute-start(bf16[256,576]{1,0:T(8,128)(2,1)S(1)} %bitcast.31), channel_id=1, source_target_pairs={{0,1},{1,0},{2,3},{3,2},{4,5},{5,4},{6,7},{7,6},{8,9},{9,8},{10,11... | collective-permute-start | bytes 884744 | tf_op jit(solution)/shard_map/ppermute | solution.py:32
  15.5 23.2 %collective-permute-start.1 = (bf16[256,576]{1,0:T(8,128)(2,1)S(1)}, bf16[256,576]{1,0:T(8,128)(2,1)S(1)}, u32[]{:S(2)}, u32[]{:S(2)}) collective-permute-start(bf16[256,576]{1,0:T(8,128)(2,1)S(1)} %bitcast.33), channel_id=1, source_target_pairs={{0,1},{1,0},{2,3},{3,2},{4,5},{5,4},{6,7},{7,6},{8,9},{9,8},{10,11... | collective-permute-start | bytes 884744 | tf_op jit(solution)/shard_map/ppermute | solution.py:32
  23.3 11.8 %collective-permute-start.6 = (bf16[128,576]{1,0:T(8,128)(2,1)S(1)}, bf16[128,576]{1,0:T(8,128)(2,1)S(1)}, u32[]{:S(2)}, u32[]{:S(2)}) collective-permute-start(bf16[128,576]{1,0:T(8,128)(2,1)S(1)} %broadcast_select_fusion.1.refs_0_), channel_id=1, source_target_pairs={{0,1},{1,0},{2,3},{3,2},{4,5},{5,4},{6,7},{7,6},{8,9},{9,8},{10,11... | collective-permute-start | bytes 442376 | tf_op jit(solution)/shard_map/ppermute | solution.py:32
  24.6 13.6 %collective-permute-start.7 = (bf16[128,576]{1,0:T(8,128)(2,1)S(1)}, bf16[128,576]{1,0:T(8,128)(2,1)S(1)}, u32[]{:S(2)}, u32[]{:S(2)}) collective-permute-start(bf16[128,576]{1,0:T(8,128)(2,1)S(1)} %broadcast_select_fusion.1.refs_0_), channel_id=1, source_target_pairs={{0,4},{1,5},{2,6},{3,7},{4,0},{5,1},{6,2},{7,3},{8,12},{9,13},{10,... | collective-permute-start | bytes 442376 | tf_op jit(solution)/shard_map/ppermute | solution.py:32
  25.8 12.4 %collective-permute-start.8 = (bf16[128,576]{1,0:T(8,128)(2,1)S(1)}, bf16[128,576]{1,0:T(8,128)(2,1)S(1)}, u32[]{:S(2)}, u32[]{:S(2)}) collective-permute-start(bf16[128,576]{1,0:T(8,128)(2,1)S(1)} %broadcast_select_fusion.1.refs_0_), channel_id=1, source_target_pairs={{0,5},{1,4},{2,7},{3,6},{4,1},{5,0},{6,3},{7,2},{8,13},{9,12},{10,... | collective-permute-start | bytes 442376 | tf_op jit(solution)/shard_map/ppermute | solution.py:32
  32.8 13.5 %collective-permute-start.9 = (bf16[128,576]{1,0:T(8,128)(2,1)S(1)}, bf16[128,576]{1,0:T(8,128)(2,1)S(1)}, u32[]{:S(2)}, u32[]{:S(2)}) collective-permute-start(bf16[128,576]{1,0:T(8,128)(2,1)S(1)} %broadcast_select_fusion.1.refs_0_), channel_id=1, source_target_pairs={{0,2},{2,0},{4,6},{6,4},{8,10},{10,8},{12,14},{14,12},{16,18},{18,... | collective-permute-start | bytes 442376 | tf_op jit(solution)/shard_map/ppermute | solution.py:22
  35.1 11.2 %collective-permute-start.10 = (bf16[128,576]{1,0:T(8,128)(2,1)S(1)}, bf16[128,576]{1,0:T(8,128)(2,1)S(1)}, u32[]{:S(2)}, u32[]{:S(2)}) collective-permute-start(bf16[128,576]{1,0:T(8,128)(2,1)S(1)} %collective-permute-done.6.refs_1_), channel_id=1, source_target_pairs={{0,2},{2,0},{4,6},{6,4},{8,10},{10,8},{12,14},{14,12},{16,18},{18,... | collective-permute-start | bytes 442376 | tf_op jit(solution)/shard_map/ppermute | solution.py:22
  38.3 8.1 %collective-permute-start.11 = (bf16[128,576]{1,0:T(8,128)(2,1)S(1)}, bf16[128,576]{1,0:T(8,128)(2,1)S(1)}, u32[]{:S(2)}, u32[]{:S(2)}) collective-permute-start(bf16[128,576]{1,0:T(8,128)(2,1)S(1)} %collective-permute-done.7.refs_2_), channel_id=1, source_target_pairs={{0,2},{2,0},{4,6},{6,4},{8,10},{10,8},{12,14},{14,12},{16,18},{18,... | collective-permute-start | bytes 442376 | tf_op jit(solution)/shard_map/ppermute | solution.py:22
  38.3 8.1 %collective-permute-start.12 = (bf16[128,576]{1,0:T(8,128)(2,1)S(1)}, bf16[128,576]{1,0:T(8,128)(2,1)S(1)}, u32[]{:S(2)}, u32[]{:S(2)}) collective-permute-start(bf16[128,576]{1,0:T(8,128)(2,1)S(1)} %collective-permute-done.8.refs_3_), channel_id=1, source_target_pairs={{0,2},{2,0},{4,6},{6,4},{8,10},{10,8},{12,14},{14,12},{16,18},{18,... | collective-permute-start | bytes 442376 | tf_op jit(solution)/shard_map/ppermute | solution.py:22
  38.8 2.3 %copy-start.1 = (bf16[3,1152,576]{2,1,0:T(8,128)(2,1)S(1)}, bf16[3,1152,576]{2,1,0:T(8,128)(2,1)}, u32[]{:S(2)}) copy-start(bf16[3,1152,576]{2,1,0:T(8,128)(2,1)} %copy.10) | copy-start | bytes 11943940
  41.0 5.3 %copy-start.2 = (bf16[3,1152,576]{2,1,0:T(8,128)(2,1)S(1)}, bf16[3,1152,576]{2,1,0:T(8,128)(2,1)}, u32[]{:S(2)}) copy-start(bf16[3,1152,576]{2,1,0:T(8,128)(2,1)} %copy.10) | copy-start | bytes 11943940
  46.3 4.3 %copy-start = (bf16[576,1152]{1,0:T(8,128)(2,1)S(1)}, bf16[576,1152]{1,0:T(8,128)(2,1)}, u32[]{:S(2)}) copy-start(bf16[576,1152]{1,0:T(8,128)(2,1)} %w_ref.7) | copy-start | bytes 3981316
  61.4 6.6 %copy-start.3 = (bf16[1,512,576]{1,2,0:T(8,128)(2,1)S(1)}, bf16[1,512,576]{1,2,0:T(8,128)(2,1)}, u32[]{:S(2)}) copy-start(bf16[1,512,576]{1,2,0:T(8,128)(2,1)} %param.6) | copy-start | bytes 1769476
  65.0 5.8 %collective-permute-start.22 = (bf16[128,576]{1,0:T(8,128)(2,1)S(1)}, bf16[128,576]{1,0:T(8,128)(2,1)S(1)}, u32[]{:S(2)}, u32[]{:S(2)}) collective-permute-start(bf16[128,576]{1,0:T(8,128)(2,1)S(1)} %bitcast.38), channel_id=1, source_target_pairs={{0,1},{1,0},{2,3},{3,2},{4,5},{5,4},{6,7},{7,6},{8,9},{9,8},{10,11... | collective-permute-start | bytes 442376 | tf_op jit(solution)/shard_map/ppermute | solution.py:32
  66.4 7.9 %collective-permute-start.19 = (bf16[128,576]{1,0:T(8,128)(2,1)S(1)}, bf16[128,576]{1,0:T(8,128)(2,1)S(1)}, u32[]{:S(2)}, u32[]{:S(2)}) collective-permute-start(bf16[128,576]{1,0:T(8,128)(2,1)S(1)} %bitcast.37), channel_id=1, source_target_pairs={{0,1},{1,0},{2,3},{3,2},{4,5},{5,4},{6,7},{7,6},{8,9},{9,8},{10,11... | collective-permute-start | bytes 442376 | tf_op jit(solution)/shard_map/ppermute | solution.py:32
  66.5 11.3 %collective-permute-start.16 = (bf16[128,576]{1,0:T(8,128)(2,1)S(1)}, bf16[128,576]{1,0:T(8,128)(2,1)S(1)}, u32[]{:S(2)}, u32[]{:S(2)}) collective-permute-start(bf16[128,576]{1,0:T(8,128)(2,1)S(1)} %bitcast.36), channel_id=1, source_target_pairs={{0,1},{1,0},{2,3},{3,2},{4,5},{5,4},{6,7},{7,6},{8,9},{9,8},{10,11... | collective-permute-start | bytes 442376 | tf_op jit(solution)/shard_map/ppermute | solution.py:32
  67.9 13.4 %collective-permute-start.13 = (bf16[128,576]{1,0:T(8,128)(2,1)S(1)}, bf16[128,576]{1,0:T(8,128)(2,1)S(1)}, u32[]{:S(2)}, u32[]{:S(2)}) collective-permute-start(bf16[128,576]{1,0:T(8,128)(2,1)S(1)} %bitcast.35), channel_id=1, source_target_pairs={{0,1},{1,0},{2,3},{3,2},{4,5},{5,4},{6,7},{7,6},{8,9},{9,8},{10,11... | collective-permute-start | bytes 442376 | tf_op jit(solution)/shard_map/ppermute | solution.py:32
  81.3 14.9 %copy-start.5 = (f32[3,576]{1,0:T(4,128)S(1)}, f32[3,576]{1,0:T(4,128)}, u32[]{:S(2)}) copy-start(f32[3,576]{1,0:T(4,128)} %param.10) | copy-start | bytes 20740
  81.6 7.6 %collective-permute-start.14 = (bf16[128,576]{1,0:T(8,128)(2,1)S(1)}, bf16[128,576]{1,0:T(8,128)(2,1)S(1)}, u32[]{:S(2)}, u32[]{:S(2)}) collective-permute-start(bf16[128,576]{1,0:T(8,128)(2,1)S(1)} %get-tuple-element.46), channel_id=1, source_target_pairs={{0,2},{2,0},{4,6},{6,4},{8,10},{10,8},{12,14},{14,12},{16,18},{18,... | collective-permute-start | bytes 442376 | tf_op jit(solution)/shard_map/ppermute | solution.py:22
  82.5 9.1 %collective-permute-start.15 = (bf16[128,576]{1,0:T(8,128)(2,1)S(1)}, bf16[128,576]{1,0:T(8,128)(2,1)S(1)}, u32[]{:S(2)}, u32[]{:S(2)}) collective-permute-start(bf16[128,576]{1,0:T(8,128)(2,1)S(1)} %get-tuple-element.46), channel_id=1, source_target_pairs={{2,4},{6,8},{10,12},{14,16},{18,20},{22,24},{26,28},{4,2},{8,6},{1... | collective-permute-start | bytes 442376 | tf_op jit(solution)/shard_map/ppermute | solution.py:230
  85.5 8.8 %collective-permute-start.17 = (bf16[128,576]{1,0:T(8,128)(2,1)S(1)}, bf16[128,576]{1,0:T(8,128)(2,1)S(1)}, u32[]{:S(2)}, u32[]{:S(2)}) collective-permute-start(bf16[128,576]{1,0:T(8,128)(2,1)S(1)} %get-tuple-element.47), channel_id=1, source_target_pairs={{0,2},{2,0},{4,6},{6,4},{8,10},{10,8},{12,14},{14,12},{16,18},{18,... | collective-permute-start | bytes 442376 | tf_op jit(solution)/shard_map/ppermute | solution.py:22
  86.0 10.3 %collective-permute-start.18 = (bf16[128,576]{1,0:T(8,128)(2,1)S(1)}, bf16[128,576]{1,0:T(8,128)(2,1)S(1)}, u32[]{:S(2)}, u32[]{:S(2)}) collective-permute-start(bf16[128,576]{1,0:T(8,128)(2,1)S(1)} %get-tuple-element.47), channel_id=1, source_target_pairs={{2,4},{6,8},{10,12},{14,16},{18,20},{22,24},{26,28},{4,2},{8,6},{1... | collective-permute-start | bytes 442376 | tf_op jit(solution)/shard_map/ppermute | solution.py:230
  88.2 8.2 %collective-permute-start.20 = (bf16[128,576]{1,0:T(8,128)(2,1)S(1)}, bf16[128,576]{1,0:T(8,128)(2,1)S(1)}, u32[]{:S(2)}, u32[]{:S(2)}) collective-permute-start(bf16[128,576]{1,0:T(8,128)(2,1)S(1)} %get-tuple-element.48), channel_id=1, source_target_pairs={{0,2},{2,0},{4,6},{6,4},{8,10},{10,8},{12,14},{14,12},{16,18},{18,... | collective-permute-start | bytes 442376 | tf_op jit(solution)/shard_map/ppermute | solution.py:22
  89.2 8.8 %collective-permute-start.21 = (bf16[128,576]{1,0:T(8,128)(2,1)S(1)}, bf16[128,576]{1,0:T(8,128)(2,1)S(1)}, u32[]{:S(2)}, u32[]{:S(2)}) collective-permute-start(bf16[128,576]{1,0:T(8,128)(2,1)S(1)} %get-tuple-element.48), channel_id=1, source_target_pairs={{2,4},{6,8},{10,12},{14,16},{18,20},{22,24},{26,28},{4,2},{8,6},{1... | collective-permute-start | bytes 442376 | tf_op jit(solution)/shard_map/ppermute | solution.py:230
  91.7 6.3 %collective-permute-start.23 = (bf16[128,576]{1,0:T(8,128)(2,1)S(1)}, bf16[128,576]{1,0:T(8,128)(2,1)S(1)}, u32[]{:S(2)}, u32[]{:S(2)}) collective-permute-start(bf16[128,576]{1,0:T(8,128)(2,1)S(1)} %get-tuple-element.49), channel_id=1, source_target_pairs={{0,2},{2,0},{4,6},{6,4},{8,10},{10,8},{12,14},{14,12},{16,18},{18,... | collective-permute-start | bytes 442376 | tf_op jit(solution)/shard_map/ppermute | solution.py:22
  94.3 8.4 %collective-permute-start.24 = (bf16[128,576]{1,0:T(8,128)(2,1)S(1)}, bf16[128,576]{1,0:T(8,128)(2,1)S(1)}, u32[]{:S(2)}, u32[]{:S(2)}) collective-permute-start(bf16[128,576]{1,0:T(8,128)(2,1)S(1)} %get-tuple-element.49), channel_id=1, source_target_pairs={{2,4},{6,8},{10,12},{14,16},{18,20},{22,24},{26,28},{4,2},{8,6},{1... | collective-permute-start | bytes 442376 | tf_op jit(solution)/shard_map/ppermute | solution.py:230

commit v2 on v0

v2 whole, which is shorter than its diff:
```python
import functools

import jax
import jax.numpy as jnp
from jax import lax
from jax.experimental import pallas as pl
from jax.experimental.pallas import tpu as pltpu
from jax.sharding import PartitionSpec as P

HS = 72
SEG = 16
LANES = 128
VALUE_ROWS = 80
EPSILON = 1e-06
LOG2_E = 1.4426950408889634

OUT_CHUNKS = 2
IN_CHUNKS = 1
CONV_FLOPS = 10**10
VMEM_BYTES = 32 * 2**20
VMEM = pl.BlockSpec(memory_space=pltpu.VMEM)
SMEM = pl.BlockSpec(memory_space=pltpu.SMEM)
HBM = pl.BlockSpec(memory_space=pltpu.HBM)


def outside(x):
    return pltpu.with_memory_space_constraint(x, pltpu.HBM)


def exchanged(block, bit):
    count = lax.axis_size("tm")
    return lax.ppermute(block, "tm", [(i, i ^ bit) for i in range(count)])


def shifted(block, bit, shift):
    frames, heads = lax.axis_size("tm"), lax.axis_size("head")
    route = [
        (f * heads + h, (f ^ bit) * heads + (h + shift) % heads)
        for f in range(frames)
        for h in range(heads)
    ]
    return lax.ppermute(block, ("tm", "head"), route)


def project_kernel(blocks, parts, factor, order_ref, modulation_ref, w_hbm, *refs):
    pieces = refs[: blocks * parts]
    *query_ref, key_ref, value_ref, x_ref, shift_ref, scale_ref, w_ref, w_sem = refs[blocks * parts :]
    features, tokens = x_ref.shape
    width = features // parts
    step = tokens // blocks
    heads = key_ref.shape[0]
    count = w_ref.shape[0]
    loads = [
        pltpu.make_async_copy(w_hbm.at[3 - count + c], w_ref.at[c], w_sem.at[c]) for c in range(count)
    ]
    for load in loads:
        load.start()
    for block in range(blocks):
        for part in range(parts):
            start = pl.multiple_of(order_ref[part] * width, 32)
            x_ref[pl.ds(start, width), block * step : (block + 1) * step] = pieces[
                block * parts + part
            ][...]
    columns = jnp.concatenate([modulation_ref[...], jnp.zeros((5, features), jnp.float32)]).T
    shift_ref[...] = jnp.broadcast_to(columns[:, 0:1], (features, LANES))
    scale_ref[...] = jnp.broadcast_to(1.0 + columns[:, 1:2], (features, LANES))
    for start in range(0, tokens, LANES):
        values = x_ref[:, start : start + LANES].astype(jnp.float32)
        centred = values - jnp.sum(values, axis=0, keepdims=True) / features
        variance = jnp.sum(centred * centred, axis=0, keepdims=True) / features
        normed = centred * lax.rsqrt(variance + EPSILON)
        x_ref[:, start : start + LANES] = (normed * scale_ref[...] + shift_ref[...]).astype(jnp.bfloat16)

    row = lax.broadcasted_iota(jnp.int32, (VALUE_ROWS - HS, tokens), 0)
    ones = jnp.where(row == 0, 1.0, 0.0).astype(jnp.bfloat16)
    group = 2
    for c in range(count):
        loads[c].wait()
        for first in range(0, heads, group):
            total = jnp.dot(
                w_ref[c, first * HS : (first + group) * HS],
                x_ref[...],
                preferred_element_type=jnp.float32,
            )
            for head in range(first, first + group):
                rows = total[(head - first) * HS : (head - first + 1) * HS]
                if c == count - 1:
                    value_ref[head, 0:HS, :] = rows.astype(jnp.bfloat16)
                    value_ref[head, HS:, :] = ones
                elif c == count - 2:
                    key_ref[head, :, 0:HS] = rows.T.astype(jnp.bfloat16)
                    key_ref[head, :, HS:] = jnp.zeros((tokens, LANES - HS), jnp.bfloat16)
                else:
                    query_ref[0][head, 0:HS, :] = (rows * factor).astype(jnp.bfloat16)
                    query_ref[0][head, HS:, :] = jnp.zeros((LANES - HS, tokens), jnp.bfloat16)


def project(blocks, order, modulation, w_qkv, with_queries):
    parts = len(blocks[0])
    tokens = sum(block[0].shape[1] for block in blocks)
    _, width, features = w_qkv.shape
    heads = width // HS
    count = 3 if with_queries else 2
    queries = jax.ShapeDtypeStruct((heads, LANES, tokens), jnp.bfloat16)
    keys = jax.ShapeDtypeStruct((heads, tokens, LANES), jnp.bfloat16)
    values = jax.ShapeDtypeStruct((heads, VALUE_ROWS, tokens), jnp.bfloat16)
    flat = [piece for block in blocks for piece in block]
    return pl.pallas_call(
        functools.partial(project_kernel, len(blocks), parts, HS ** (-0.5) * LOG2_E),
        out_shape=[queries, keys, values][3 - count :],
        in_specs=[SMEM, VMEM, HBM] + [VMEM] * len(flat),
        out_specs=[VMEM] * count,
        scratch_shapes=[
            pltpu.VMEM((features, tokens), jnp.bfloat16),
            pltpu.VMEM((features, LANES), jnp.float32),
            pltpu.VMEM((features, LANES), jnp.float32),
            pltpu.VMEM((count, width, features), jnp.bfloat16),
            pltpu.SemaphoreType.DMA((count,)),
        ],
        compiler_params=pltpu.CompilerParams(vmem_limit_bytes=VMEM_BYTES),
        cost_estimate=pl.CostEstimate(
            flops=2 * tokens * features * width * count,
            bytes_accessed=count * 2 * (features * width + tokens * heads * LANES),
            transcendentals=0,
        ),
    )(order, modulation, outside(w_qkv), *flat)


def attend_kernel(parts, start, me_ref, *refs):
    sources = refs[:8]
    own_ref, send_ref = refs[8:10]
    buffers = refs[10:18]
    attended, terms, scores, weights, sems = refs[18:]
    q_ref, *keys_values = buffers[:7]
    w_ref = buffers[7]
    keys, values = keys_values[0::2], keys_values[1::2]
    heads = q_ref.shape[0]
    width, rows = own_ref.shape
    firsts = (0, 1) if heads < 4 else (0, 1, 3)
    loads = []
    for first, last in zip(firsts, (*firsts[1:], heads)):
        span = pl.ds(first, last - first)
        loads.append([])
        for i, (source, buffer) in enumerate(zip(sources[:7], buffers[:7])):
            part = source.at[span]
            if i == 0:
                part = source.at[span, :, pl.ds(start, rows)]
            loads[-1].append(
                pltpu.make_async_copy(part, buffer.at[span], sems.at[first, i])
            )
    load_w = pltpu.make_async_copy(sources[7], w_ref, sems.at[0, 7])
    for group in loads:
        for load in group:
            load.start()
    load_w.start()
    spans, total = [], 0
    for ref in keys:
        spans.append((total, total + ref.shape[1]))
        total += ref.shape[1]

    def score(head):
        if head in firsts:
            for load in loads[firsts.index(head)]:
                load.wait()
        for ref, (low, high) in zip(keys, spans):
            scores[head % 2, low:high] = jnp.dot(
                ref[head], q_ref[head], preferred_element_type=jnp.float32
            )

    def weigh(head):
        values = scores[head % 2]
        top = jnp.max(values, axis=0, keepdims=True)
        weights[head % 2] = jnp.exp2(values - top).astype(jnp.bfloat16)

    def collect(head):
        total = sum(
            jnp.dot(ref[head], weights[head % 2, low:high], preferred_element_type=jnp.float32)
            for ref, (low, high) in zip(values, spans)
        )
        attended[head * HS : (head + 1) * HS, :] = total[:HS] / total[HS : HS + 1]

    for head in range(heads + 2):
        if head < heads:
            score(head)
        if head >= 2:
            collect(head - 2)
        if 1 <= head <= heads:
            weigh(head - 1)
    load_w.wait()
    terms[...] = jnp.dot(
        w_ref[...], attended[...].astype(jnp.bfloat16), preferred_element_type=jnp.float32
    )
    me = me_ref[0]
    own_ref[...] = terms[pl.ds(pl.multiple_of(me * width, 32), width), :]
    for step in range(1, parts):
        other = lax.rem(me + step, parts)
        send_ref[step - 1] = terms[pl.ds(pl.multiple_of(other * width, 32), width), :].astype(
            jnp.bfloat16
        )


def attend(me, parts, queries, kvs, w_out, start, rows):
    heads, _, tokens = queries.shape
    features, width = w_out.shape
    keys = 2 * tokens
    arrays = [queries, *kvs[0], *kvs[1], *kvs[2], w_out]
    buffers = [pltpu.VMEM((heads, LANES, rows), jnp.bfloat16)]
    buffers += [pltpu.VMEM(x.shape, x.dtype) for x in arrays[1:]]
    return pl.pallas_call(
        functools.partial(attend_kernel, parts, start),
        out_shape=[
            jax.ShapeDtypeStruct((features // parts, rows), jnp.float32),
            jax.ShapeDtypeStruct((parts - 1, features // parts, rows), jnp.bfloat16),
        ],
        in_specs=[SMEM] + [HBM] * 8,
        out_specs=[VMEM] * 2,
        scratch_shapes=buffers
        + [
            pltpu.VMEM((heads * HS, rows), jnp.float32),
            pltpu.VMEM((features, rows), jnp.float32),
            pltpu.VMEM((2, keys, rows), jnp.float32),
            pltpu.VMEM((2, keys, rows), jnp.bfloat16),
            pltpu.SemaphoreType.DMA((heads, 8)),
        ],
        compiler_params=pltpu.CompilerParams(vmem_limit_bytes=VMEM_BYTES),
        cost_estimate=pl.CostEstimate(
            flops=4 * heads * rows * keys * LANES + 2 * rows * w_out.size,
            bytes_accessed=8 * heads * tokens * LANES + 2 * w_out.size,
            transcendentals=heads * rows * keys,
        ),
    )(me, *[outside(x) for x in arrays])


def tied(x, *others):
    return lax.optimization_barrier((x, *others))[0]


def conv_kernel(start, hidden_ref, near_ref, far_ref, taps_ref, *refs):
    out_hbm, out_ref, sem = refs[-3:]
    width, rows = out_ref.shape
    hidden = hidden_ref[...].astype(jnp.float32)
    total = hidden + taps_ref[:, 1:2] * hidden
    total += taps_ref[:, 0:1] * near_ref[...].astype(jnp.float32)
    total += taps_ref[:, 2:3] * far_ref[...].astype(jnp.float32)
    out_ref[...] = total.astype(jnp.bfloat16)
    store = pltpu.make_async_copy(out_ref, out_hbm.at[:, start : start + rows], sem)
    store.start()
    store.wait()


def convolved(hidden, near, far, taps, start, tokens, out):
    width, rows = hidden.shape
    before = [] if out is None else [out]
    return pl.pallas_call(
        functools.partial(conv_kernel, start),
        out_shape=jax.ShapeDtypeStruct((width, tokens), jnp.bfloat16),
        in_specs=[VMEM] * 4 + [HBM] * len(before),
        out_specs=HBM,
        scratch_shapes=[pltpu.VMEM((width, rows), jnp.bfloat16), pltpu.SemaphoreType.DMA],
        input_output_aliases={4: 0} if before else {},
        compiler_params=pltpu.CompilerParams(vmem_limit_bytes=VMEM_BYTES),
        cost_estimate=pl.CostEstimate(flops=CONV_FLOPS, bytes_accessed=8 * width * rows, transcendentals=0),
    )(hidden, near, far, taps, *before)


def local(frames, modulation, w_qkv, w_out, conv_taps, anchors):
    frame = frames[0].T
    width, tokens = frame.shape
    parts, count = lax.axis_size("head"), lax.axis_size("tm")
    place, me = lax.axis_index("tm"), lax.axis_index("head")
    anchor = lax.dynamic_index_in_dim(anchors, place // SEG, 0, keepdims=False)
    order = ((me - jnp.arange(parts)) % parts).astype(jnp.int32)
    me_ref = me.astype(jnp.int32).reshape(1)
    w_qkv = jnp.swapaxes(w_qkv, 1, 2)
    index = place % SEG

    def bit(number):
        return (index >> number) & 1

    def same(number):
        return bit(number) == (anchor >> number) & 1

    rows = tokens // IN_CHUNKS
    own = []
    for start in range(0, tokens, rows):
        piece = frame[:, start : start + rows]
        if own:
            piece = tied(piece, *own[-1])
        own.append([piece] + [shifted(piece, 0, step) for step in range(1, parts)])

    block = frame
    for number in range(SEG.bit_length() - 1):
        kept = sent = block
        if number < 2:
            half = block.shape[1] // 2
            low, high = block[:, :half], block[:, half:]
            kept = jnp.where(bit(number) == 0, low, high)
            sent = jnp.where(bit(number) == 0, high, low)
        came = exchanged(sent, 1 << number)
        if number == 1:
            w_out = tied(w_out, sent).T
            came = tied(came, w_out)
        block = jnp.where(same(number), kept, came)
    block, own = lax.optimization_barrier((block, own))
    near = [block] + [shifted(block, 0, step) for step in range(1, parts)]
    across = [shifted(block, 2, step) for step in range(parts)]
    queries, *own_kv = project(own, order, modulation, w_qkv, True)
    near = [tied(near[0], queries)] + near[1:]
    near_kv = project([near, across], order, modulation, w_qkv, False)
    kvs = [own_kv, near_kv, [exchanged(x, 1) for x in near_kv]]

    gate = lax.dynamic_slice_in_dim(modulation[2], me * width, width, 0)[:, None]
    rows = tokens // OUT_CHUNKS
    odd = []
    for h in range(parts):
        for f in range(1, count - 1, 2):
            here, there = f * parts + h, (f + 1) * parts + h
            odd += [(here, there), (there, here)]
        for f in (0, count - 1):
            odd.append((f * parts + h, f * parts + (h + 1) % parts))
    is_even = place % 2 == 0
    tap_near = jnp.where(is_even, conv_taps[2], conv_taps[0])
    tap_far = jnp.where(is_even, conv_taps[0], conv_taps[2])
    tap_far = jnp.where((place == 0) | (place == count - 1), 0.0, tap_far)
    taps = jnp.stack([tap_near, conv_taps[1], tap_far]).T
    totals, received = [], []
    for chunk in range(OUT_CHUNKS):
        turn = me_ref
        total, send = attend(turn, parts, queries, kvs, w_out, chunk * rows, rows)
        totals.append(total)
        received.append([shifted(send[step - 1], 0, step) for step in range(1, parts)])
    out, sent = None, []
    for chunk in range(OUT_CHUNKS):
        total = tied(totals[chunk], totals[-1], *sent)
        for part in received[chunk]:
            total = total + part.astype(jnp.float32)
        piece = frame[:, chunk * rows : (chunk + 1) * rows].astype(jnp.float32)
        hidden = (piece + gate * total).astype(jnp.bfloat16)
        sent = [hidden]
        close, far = exchanged(hidden, 1), lax.ppermute(hidden, ("tm", "head"), odd)
        out = convolved(hidden, close, far, taps, chunk * rows, tokens, out)
    return out.T[None]


def solution(mesh):
    in_specs = (
        P("tm", None, "head"),
        P(),
        P(None, None, "head"),
        P("head", None),
        P(None, "head"),
        P(),
    )
    out_specs = P("tm", None, "head")
    return jax.shard_map(local, mesh=mesh, in_specs=in_specs, out_specs=out_specs, check_vma=False)
```

time: 278 us -> 75.3 us (0.27)
  waiting for transfers between devices: 212 us -> 27.6 us
  matrix products: 25.5 us -> 0 us
  Pallas kernels: 0 us -> 21.7 us
  between operations: 14.8 us -> 0.85 us
  starting transfers between devices: 8.25 us -> 17.5 us
  local copies, waits for them, and re-layouts: 11 us -> 3.85 us
  other arithmetic: 5.76 us -> 2.69 us
    ppermute x6 -> x16, waiting for transfers between devices: 121 us -> 27.6 us  [the longest x8 15.5 us: exchanged(): return lax.ppermute(block, 'tm', [(i, i ^ bit) for i in range(count)])]
    unnamed x3 -> x0, waiting for transfers between devices: 67.4 us -> none
    all_gather x1 -> x0, waiting for transfers between devices: 23.9 us -> none  [local(): gathered = lax.all_gather(frames, 'head', axis=2, tiled=True)]
    pallas_call x0 -> x6, Pallas kernels: none -> 21.7 us  [the longest x2 11.3 us: attend(): pl.pallas_call(functools.partial(attend_kernel, parts, start), out_shape=...]
    dot_general x3 -> x0, matrix products: 16 us -> none  [the longest x1 8.71 us: attend_block(): jnp.einsum('hqk,khs->qhs', weights, value_rows, preferred_element_type=jn...]
    sub x1 -> x0, matrix products: 9.51 us -> none  [attend_block(): weights = jnp.exp(scores - row_max)]
    ppermute x6 -> x16, starting transfers between devices: 8.21 us -> 17.5 us  [the longest x8 8.63 us: exchanged(): return lax.ppermute(block, 'tm', [(i, i ^ bit) for i in range(count)])]
    dot_general x1 -> x0, local copies, waits for them, and re-layouts: 6.39 us -> none  [local(): jnp.einsum('fpe,ed->fpd', attended, w_out, preferred_element_type=jnp.flo...]
  transfers between devices with their start and end apart: 8 -> 16, of which waited for: 8 -> 10; matrix products, arithmetic and copies ran while one was open for 1% -> 3% of each run, Pallas kernels for 0% -> 16%
where the time goes in v2:
time: 75.3 us; the launch traced here: 74.2 us
  waiting for transfers between devices  27.6 us (37%)
  Pallas kernels  21.7 us (29%)
  starting transfers between devices  17.5 us (23%)
  local copies, waits for them, and re-layouts  3.85 us (5%)
  other arithmetic  2.69 us (4%)
  between operations  0.85 us (1%)
    ppermute x8, waiting for transfers between devices, exchanged(): return lax.ppermute(block, 'tm', [(i, i ^ bit) for i in range(count)])  15.5 us
    pallas_call x2, Pallas kernels, attend(): pl.pallas_call(functools.partial(attend_kernel, parts, start), out_shape=...  11.3 us
    ppermute x8, starting transfers between devices, exchanged(): return lax.ppermute(block, 'tm', [(i, i ^ bit) for i in range(count)])  8.63 us
    pallas_call x2, Pallas kernels, project(): pl.pallas_call(functools.partial(project_kernel, len(blocks), parts, HS *...  8.21 us
    ppermute x2, waiting for transfers between devices, local(): lax.ppermute(hidden, ('tm', 'head'), odd)  6.18 us
    ppermute x6, waiting for transfers between devices, shifted(): return lax.ppermute(block, ('tm', 'head'), route)  5.89 us
    ppermute x6, starting transfers between devices, shifted(): return lax.ppermute(block, ('tm', 'head'), route)  5.42 us
    ppermute x2, starting transfers between devices, local(): lax.ppermute(hidden, ('tm', 'head'), odd)  3.47 us
  transfers between devices with their start and end apart: 16, of which 10 were waited for; matrix products, arithmetic and copies ran while one was open for 3% of the time, Pallas kernels for 16%

profile of v2, /device:TPU:25, one launch (start us, length us, event | category | flops | bytes accessed | tf_op | source)
XLA Modules:
  0.0 74.2 jit_solution(8840701812450607237)
XLA Ops:
  0.0 1.2 %broadcast_select_fusion = bf16[576,256]{1,0:T(8,128)(2,1)S(1)} fusion(pred[]{:T(512)S(6)} %eq.39, bf16[576,512]{1,0:T(8,128)(2,1)} %bitcast.16), kind=kLoop, calls=%fused_computation.3 | loop fusion | flops 147456 | bytes 884737 | tf_op jit(solution)/shard_map/jit(_where)/select_n | solution.py:298
  1.2 0.7 collective-permute-start
  2.6 0.6 collective-permute-done
  3.1 1.1 %select_select_fusion = bf16[576,256]{1,0:T(8,128)(2,1)S(1)} fusion(bf16[576,256]{1,0:T(8,128)(2,1)S(1)} %collective-permute-done, pred[]{:T(512)S(6)} %eq.39, pred[]{:T(512)S(6)} %eq.38, bf16[576,512]{1,0:T(8,128)(2,1)} %bitcast.17), kind=kLoop, calls=%fused_computation.2 | loop fusion | flops 294912 | bytes 1179650 | tf_op jit(solution)/shard_map/jit(_where)/select_n | solution.py:303
  4.3 1.3 %collective-permute-start.1 = (bf16[576,128]{1,0:T(8,128)(2,1)S(1)}, bf16[576,128]{1,0:T(8,128)(2,1)S(1)}, u32[]{:S(2)}, u32[]{:S(2)}) collective-permute-start(bf16[576,128]{1,0:T(8,128)(2,1)S(1)} %broadcast_select_fusion.1), channel_id=1, source_target_pairs={{0,4},{2,6},{4,0},{6,2},{8,12},{10,14},{12,8},{14,10},{16,20},{18,... | collective-permute-start | bytes 442376 | tf_op jit(solution)/shard_map/ppermute | solution.py:32
  5.6 1.7 %copy.14 = bf16[576,1152]{0,1:T(8,128)(2,1)} copy(bf16[576,1152]{1,0:T(8,128)(2,1)S(1)} %copy-done.8) | data formatting | bytes 2654208 | tf_op jit(solution)/shard_map/optimization_barrier | solution.py:235
  7.2 2.2 %collective-permute-done.1 = bf16[576,128]{1,0:T(8,128)(2,1)S(1)} collective-permute-done((bf16[576,128]{1,0:T(8,128)(2,1)S(1)}, bf16[576,128]{1,0:T(8,128)(2,1)S(1)}, u32[]{:S(2)}, u32[]{:S(2)}) %collective-permute-start.1) | collective-permute-done | bytes 147488 | tf_op jit(solution)/shard_map/ppermute | solution.py:32
  9.4 0.2 collective-permute-start.2
  9.7 1.2 %collective-permute-start.4 = (bf16[576,512]{1,0:T(8,128)(2,1)S(1)}, bf16[576,512]{1,0:T(8,128)(2,1)S(1)}, u32[]{:S(2)}, u32[]{:S(2)}) collective-permute-start(bf16[576,512]{1,0:T(8,128)(2,1)S(1)} %bitcast.18), channel_id=1, source_target_pairs={{0,1},{1,0},{2,3},{3,2},{4,5},{5,4},{6,7},{7,6},{8,9},{9,8},{10,11... | collective-permute-start | bytes 1769480 | tf_op jit(solution)/shard_map/ppermute | solution.py:42
  10.9 2.6 %collective-permute-done.2 = bf16[576,128]{1,0:T(8,128)(2,1)S(1)} collective-permute-done((bf16[576,128]{1,0:T(8,128)(2,1)S(1)}, bf16[576,128]{1,0:T(8,128)(2,1)S(1)}, u32[]{:S(2)}, u32[]{:S(2)}) %collective-permute-start.2) | collective-permute-done | bytes 147488 | tf_op jit(solution)/shard_map/ppermute | solution.py:32
  13.5 0.1 collective-permute-start.3
  13.6 8.3 %collective-permute-done.3 = bf16[576,128]{1,0:T(8,128)(2,1)S(1)} collective-permute-done((bf16[576,128]{1,0:T(8,128)(2,1)S(1)}, bf16[576,128]{1,0:T(8,128)(2,1)S(1)}, u32[]{:S(2)}, u32[]{:S(2)}) %collective-permute-start.3) | collective-permute-done | bytes 147488 | tf_op jit(solution)/shard_map/ppermute | solution.py:32
  22.0 1.0 %collective-permute-done.4.refs_1_ = bf16[576,512]{1,0:T(8,128)(2,1)S(1)} collective-permute-done((bf16[576,512]{1,0:T(8,128)(2,1)S(1)}, bf16[576,512]{1,0:T(8,128)(2,1)S(1)}, u32[]{:S(2)}, u32[]{:S(2)}) %collective-permute-start.4) | collective-permute-done | bytes 589856 | tf_op jit(solution)/shard_map/ppermute | solution.py:42
  23.0 1.2 %collective-permute-start.5 = (bf16[576,128]{1,0:T(8,128)(2,1)S(1)}, bf16[576,128]{1,0:T(8,128)(2,1)S(1)}, u32[]{:S(2)}, u32[]{:S(2)}) collective-permute-start(bf16[576,128]{1,0:T(8,128)(2,1)S(1)} %broadcast_select_fusion.3.refs_0_), channel_id=1, source_target_pairs={{0,1},{1,0},{2,3},{3,2},{4,5},{5,4},{6,7},{7,6},{8,9},{9,8},{10,11... | collective-permute-start | bytes 442376 | tf_op jit(solution)/shard_map/ppermute | solution.py:42
  24.2 1.2 %collective-permute-start.6 = (bf16[576,128]{1,0:T(8,128)(2,1)S(1)}, bf16[576,128]{1,0:T(8,128)(2,1)S(1)}, u32[]{:S(2)}, u32[]{:S(2)}) collective-permute-start(bf16[576,128]{1,0:T(8,128)(2,1)S(1)} %broadcast_select_fusion.3.refs_0_), channel_id=1, source_target_pairs={{0,4},{1,5},{2,6},{3,7},{4,0},{5,1},{6,2},{7,3},{8,12},{9,13},{10,... | collective-permute-start | bytes 442376 | tf_op jit(solution)/shard_map/ppermute | solution.py:42
  25.5 0.2 collective-permute-start.7
  25.7 5.0 %shard_map.64 = (bf16[8,128,512]{2,1,0:T(8,128)(2,1)S(1)}, bf16[8,512,128]{2,1,0:T(8,128)(2,1)S(1)}, bf16[8,80,512]{2,1,0:T(8,128)(2,1)S(1)}) custom-call(s32[2]{0:T(128)S(1)} %and_select_fusion.order_ref, f32[3,1152]{1,0:T(4,128)S(1)} %copy-done.6, bf16[3,576,1152]{2,1,0:T(8,128)(2,1)} %bitcast.28, bf16[576,512]{1,0:T(8,128)(2,1)S(1)} %bitcast.19, ...), custom_call_target="tpu_custom_call" | custom-call | flops 2038431744 | bytes 7127040 | tf_op jit(solution)/shard_map/pallas_call | solution.py:108
  30.6 1.0 %copy-done.1 = bf16[8,128,512]{2,1,0:T(8,128)(2,1)} copy-done((bf16[8,128,512]{2,1,0:T(8,128)(2,1)}, bf16[8,128,512]{2,1,0:T(8,128)(2,1)S(1)}, u32[]{:S(2)}) %copy-start.1) | copy-done | bytes 1048600
  31.6 0.0 collective-permute-done.5.refs_1_
  31.6 0.0 collective-permute-done.6.refs_2_
  31.6 0.0 collective-permute-done.7.refs_3_
  31.6 3.2 %shard_map.65 = (bf16[8,256,128]{2,1,0:T(8,128)(2,1)S(1)}, bf16[8,80,256]{2,1,0:T(8,128)(2,1)S(1)}) custom-call(s32[2]{0:T(128)S(1)} %and_select_fusion.order_ref, f32[3,1152]{1,0:T(4,128)S(1)} %copy-done.6, bf16[3,576,1152]{2,1,0:T(8,128)(2,1)} %bitcast.29, bf16[576,128]{1,0:T(8,128)(2,1)S(1)} %broadcast_select_fusion.3.refs_0_, ...), custom_call_target="tpu_custom_call" | custom-call | flops 679477248 | bytes 3702784 | tf_op jit(solution)/shard_map/pallas_call | solution.py:108
  34.9 0.0 copy-start.4
  34.9 3.3 %collective-permute-start.8 = (bf16[8,256,128]{2,1,0:T(8,128)(2,1)S(1)}, bf16[8,256,128]{2,1,0:T(8,128)(2,1)S(1)}, u32[]{:S(2)}, u32[]{:S(2)}) collective-permute-start(bf16[8,256,128]{2,1,0:T(8,128)(2,1)S(1)} %get-tuple-element.31.refs_3_), channel_id=1, source_target_pairs={{0,2},{2,0},{4,6},{6,4},{8,10},{10,8},{12,14},{14,12},{16,18},{18,... | collective-permute-start | bytes 1572872 | tf_op jit(solution)/shard_map/ppermute | solution.py:32
  38.2 0.1 collective-permute-start.9
  38.3 0.1 dynamic-slice_reduce_fusion
  38.4 1.8 %collective-permute-done.9.refs_6_ = bf16[8,80,256]{2,1,0:T(8,128)(2,1)S(1)} collective-permute-done((bf16[8,80,256]{2,1,0:T(8,128)(2,1)S(1)}, bf16[8,80,256]{2,1,0:T(8,128)(2,1)S(1)}, u32[]{:S(2)}, u32[]{:S(2)}) %collective-permute-start.9) | collective-permute-done | bytes 327712 | tf_op jit(solution)/shard_map/ppermute | solution.py:32
  40.2 0.0 collective-permute-done.8.refs_5_
  40.3 0.7 copy-done.9
  41.0 0.2 copy-done.7
  41.2 5.7 %shard_map.67 = (f32[576,256]{1,0:T(8,128)S(1)}, bf16[1,576,256]{2,1,0:T(8,128)(2,1)S(1)}) custom-call(s32[1]{0:T(128)} %bitcast.2.me_ref, bf16[8,128,512]{2,1,0:T(8,128)(2,1)} %copy-done.1, bf16[8,512,128]{2,1,0:T(8,128)(2,1)} %copy-done.2, bf16[8,80,512]{2,1,0:T(8,128)(2,1)} %copy-done.3, bf16[8,256,128]{2,1,0:T(8,128)(2,1)} %copy-done.4, ...), custom_call_target="tpu_custom_call" | custom-call | flops 1413480448 | bytes 5521408 | tf_op jit(solution)/shard_map/pallas_call | solution.py:209
  46.9 1.2 %collective-permute-start.10 = (bf16[576,256]{1,0:T(8,128)(2,1)S(1)}, bf16[576,256]{1,0:T(8,128)(2,1)S(1)}, u32[]{:S(2)}, u32[]{:S(2)}) collective-permute-start(bf16[576,256]{1,0:T(8,128)(2,1)S(1)} %bitcast.25), channel_id=1, source_target_pairs={{0,1},{1,0},{2,3},{3,2},{4,5},{5,4},{6,7},{7,6},{8,9},{9,8},{10,11... | collective-permute-start | bytes 884744 | tf_op jit(solution)/shard_map/ppermute | solution.py:42
  48.1 5.7 %shard_map.66 = (f32[576,256]{1,0:T(8,128)S(1)}, bf16[1,576,256]{2,1,0:T(8,128)(2,1)S(1)}) custom-call(s32[1]{0:T(128)} %bitcast.2.me_ref, bf16[8,128,512]{2,1,0:T(8,128)(2,1)} %copy-done.1, bf16[8,512,128]{2,1,0:T(8,128)(2,1)} %copy-done.2, bf16[8,80,512]{2,1,0:T(8,128)(2,1)} %copy-done.3, bf16[8,256,128]{2,1,0:T(8,128)(2,1)} %copy-done.4, ...), custom_call_target="tpu_custom_call" | custom-call | flops 1413480448 | bytes 5521408 | tf_op jit(solution)/shard_map/pallas_call | solution.py:209
  53.8 0.3 collective-permute-start.11
  54.1 1.1 %collective-permute-done.10 = bf16[576,256]{1,0:T(8,128)(2,1)S(1)} collective-permute-done((bf16[576,256]{1,0:T(8,128)(2,1)S(1)}, bf16[576,256]{1,0:T(8,128)(2,1)S(1)}, u32[]{:S(2)}, u32[]{:S(2)}) %collective-permute-start.10) | collective-permute-done | bytes 294944 | tf_op jit(solution)/shard_map/ppermute | solution.py:42
  55.2 0.1 add_convert_fusion.1.hidden_ref
  55.3 1.3 %collective-permute-start.14 = (bf16[576,256]{1,0:T(8,128)(2,1)S(1)}, bf16[576,256]{1,0:T(8,128)(2,1)S(1)}, u32[]{:S(2)}, u32[]{:S(2)}) collective-permute-start(bf16[576,256]{1,0:T(8,128)(2,1)S(1)} %add_convert_fusion.1.hidden_ref), channel_id=1, source_target_pairs={{0,2},{2,0},{4,6},{6,4},{8,10},{10,8},{12,14},{14,12},{16,18},{18,... | collective-permute-start | bytes 884744 | tf_op jit(solution)/shard_map/ppermute | solution.py:32
  56.6 1.2 %collective-permute-start.15 = (bf16[576,256]{1,0:T(8,128)(2,1)S(1)}, bf16[576,256]{1,0:T(8,128)(2,1)S(1)}, u32[]{:S(2)}, u32[]{:S(2)}) collective-permute-start(bf16[576,256]{1,0:T(8,128)(2,1)S(1)} %add_convert_fusion.1.hidden_ref), channel_id=1, source_target_pairs={{2,4},{4,2},{6,8},{8,6},{10,12},{12,10},{14,16},{16,14},{18,20},{2... | collective-permute-start | bytes 884744 | tf_op jit(solution)/shard_map/ppermute | solution.py:340
  57.8 0.2 copy.15
  57.9 3.8 %collective-permute-done.11 = bf16[576,256]{1,0:T(8,128)(2,1)S(1)} collective-permute-done((bf16[576,256]{1,0:T(8,128)(2,1)S(1)}, bf16[576,256]{1,0:T(8,128)(2,1)S(1)}, u32[]{:S(2)}, u32[]{:S(2)}) %collective-permute-start.11) | collective-permute-done | bytes 294944 | tf_op jit(solution)/shard_map/ppermute | solution.py:42
  61.8 0.1 add_convert_fusion.hidden_ref
  61.9 1.6 %collective-permute-start.12 = (bf16[576,256]{1,0:T(8,128)(2,1)S(1)}, bf16[576,256]{1,0:T(8,128)(2,1)S(1)}, u32[]{:S(2)}, u32[]{:S(2)}) collective-permute-start(bf16[576,256]{1,0:T(8,128)(2,1)S(1)} %add_convert_fusion.hidden_ref), channel_id=1, source_target_pairs={{0,2},{2,0},{4,6},{6,4},{8,10},{10,8},{12,14},{14,12},{16,18},{18,... | collective-permute-start | bytes 884744 | tf_op jit(solution)/shard_map/ppermute | solution.py:32
  63.5 2.3 %collective-permute-start.13 = (bf16[576,256]{1,0:T(8,128)(2,1)S(1)}, bf16[576,256]{1,0:T(8,128)(2,1)S(1)}, u32[]{:S(2)}, u32[]{:S(2)}) collective-permute-start(bf16[576,256]{1,0:T(8,128)(2,1)S(1)} %add_convert_fusion.hidden_ref), channel_id=1, source_target_pairs={{2,4},{4,2},{6,8},{8,6},{10,12},{12,10},{14,16},{16,14},{18,20},{2... | collective-permute-start | bytes 884744 | tf_op jit(solution)/shard_map/ppermute | solution.py:340
  65.8 0.1 collective-permute-done.15.far_ref
  65.9 1.1 %shard_map.68.refs_0_ = bf16[576,512]{1,0:T(8,128)(2,1)} custom-call(bf16[576,256]{1,0:T(8,128)(2,1)S(1)} %add_convert_fusion.1.hidden_ref, bf16[576,256]{1,0:T(8,128)(2,1)S(1)} %collective-permute-done.14.near_ref, bf16[576,256]{1,0:T(8,128)(2,1)S(1)} %collective-permute-done.15.far_ref, f32[576,3]{1,0:T(8,128)S(1)} %bitcast.22), custom_call_target="tpu_custom_call" | custom-call | flops 10000000000 | bytes 1179648 | tf_op jit(solution)/shard_map/pallas_call | solution.py:254
  67.0 0.0 collective-permute-done.12.near_ref
  67.0 6.1 %collective-permute-done.13.far_ref = bf16[576,256]{1,0:T(8,128)(2,1)S(1)} collective-permute-done((bf16[576,256]{1,0:T(8,128)(2,1)S(1)}, bf16[576,256]{1,0:T(8,128)(2,1)S(1)}, u32[]{:S(2)}, u32[]{:S(2)}) %collective-permute-start.13) | collective-permute-done | bytes 294944 | tf_op jit(solution)/shard_map/ppermute | solution.py:340
  73.1 1.1 %shard_map.69 = bf16[576,512]{1,0:T(8,128)(2,1)} custom-call(bf16[576,256]{1,0:T(8,128)(2,1)S(1)} %add_convert_fusion.hidden_ref, bf16[576,256]{1,0:T(8,128)(2,1)S(1)} %collective-permute-done.12.near_ref, bf16[576,256]{1,0:T(8,128)(2,1)S(1)} %collective-permute-done.13.far_ref, f32[576,3]{1,0:T(8,128)S(1)} %bitcast.23, ...), custom_call_target="tpu_custom_call", output_to_operand_aliasing={{}: (4, {})} | custom-call | flops 10000000000 | bytes 1179648 | tf_op jit(solution)/shard_map/pallas_call | solution.py:254
  (27 shorter events, 0.2 us)
Async XLA Ops:
  0.0 5.5 %copy-start.8 = (bf16[576,1152]{1,0:T(8,128)(2,1)S(1)}, bf16[576,1152]{1,0:T(8,128)(2,1)}, u32[]{:S(2)}) copy-start(bf16[576,1152]{1,0:T(8,128)(2,1)} %param.9) | copy-start | bytes 3981316
  1.2 1.9 %collective-permute-start = (bf16[576,256]{1,0:T(8,128)(2,1)S(1)}, bf16[576,256]{1,0:T(8,128)(2,1)S(1)}, u32[]{:S(2)}, u32[]{:S(2)}) collective-permute-start(bf16[576,256]{1,0:T(8,128)(2,1)S(1)} %broadcast_select_fusion), channel_id=1, source_target_pairs={{0,2},{2,0},{4,6},{6,4},{8,10},{10,8},{12,14},{14,12},{16,18},{18,... | collective-permute-start | bytes 884744 | tf_op jit(solution)/shard_map/ppermute | solution.py:32
  4.3 5.1 %collective-permute-start.1 = (bf16[576,128]{1,0:T(8,128)(2,1)S(1)}, bf16[576,128]{1,0:T(8,128)(2,1)S(1)}, u32[]{:S(2)}, u32[]{:S(2)}) collective-permute-start(bf16[576,128]{1,0:T(8,128)(2,1)S(1)} %broadcast_select_fusion.1), channel_id=1, source_target_pairs={{0,4},{2,6},{4,0},{6,2},{8,12},{10,14},{12,8},{14,10},{16,20},{18,... | collective-permute-start | bytes 442376 | tf_op jit(solution)/shard_map/ppermute | solution.py:32
  5.5 4.1 %copy-start = (bf16[1,512,576]{1,2,0:T(8,128)(2,1)S(1)}, bf16[1,512,576]{1,2,0:T(8,128)(2,1)}, u32[]{:S(2)}) copy-start(bf16[1,512,576]{1,2,0:T(8,128)(2,1)} %param.6) | copy-start | bytes 1769476
  5.5 20.1 %copy-start.6 = (f32[3,1152]{1,0:T(4,128)S(1)}, f32[3,1152]{1,0:T(4,128)}, u32[]{:S(2)}) copy-start(f32[3,1152]{1,0:T(4,128)} %modulation_ref.3) | copy-start | bytes 41476
  9.4 4.1 %collective-permute-start.2 = (bf16[576,128]{1,0:T(8,128)(2,1)S(1)}, bf16[576,128]{1,0:T(8,128)(2,1)S(1)}, u32[]{:S(2)}, u32[]{:S(2)}) collective-permute-start(bf16[576,128]{1,0:T(8,128)(2,1)S(1)} %select_select_fusion.1), channel_id=1, source_target_pairs={{0,8},{2,10},{4,12},{6,14},{8,0},{10,2},{12,4},{14,6},{16,24},{18,... | collective-permute-start | bytes 442376 | tf_op jit(solution)/shard_map/ppermute | solution.py:32
  9.7 13.3 %collective-permute-start.4 = (bf16[576,512]{1,0:T(8,128)(2,1)S(1)}, bf16[576,512]{1,0:T(8,128)(2,1)S(1)}, u32[]{:S(2)}, u32[]{:S(2)}) collective-permute-start(bf16[576,512]{1,0:T(8,128)(2,1)S(1)} %bitcast.18), channel_id=1, source_target_pairs={{0,1},{1,0},{2,3},{3,2},{4,5},{5,4},{6,7},{7,6},{8,9},{9,8},{10,11... | collective-permute-start | bytes 1769480 | tf_op jit(solution)/shard_map/ppermute | solution.py:42
  13.5 8.5 %collective-permute-start.3 = (bf16[576,128]{1,0:T(8,128)(2,1)S(1)}, bf16[576,128]{1,0:T(8,128)(2,1)S(1)}, u32[]{:S(2)}, u32[]{:S(2)}) collective-permute-start(bf16[576,128]{1,0:T(8,128)(2,1)S(1)} %broadcast_select_fusion.2), channel_id=1, source_target_pairs={{0,16},{2,18},{4,20},{6,22},{8,24},{10,26},{12,28},{14,30},{16,0},... | collective-permute-start | bytes 442376 | tf_op jit(solution)/shard_map/ppermute | solution.py:32
  23.0 8.6 %collective-permute-start.5 = (bf16[576,128]{1,0:T(8,128)(2,1)S(1)}, bf16[576,128]{1,0:T(8,128)(2,1)S(1)}, u32[]{:S(2)}, u32[]{:S(2)}) collective-permute-start(bf16[576,128]{1,0:T(8,128)(2,1)S(1)} %broadcast_select_fusion.3.refs_0_), channel_id=1, source_target_pairs={{0,1},{1,0},{2,3},{3,2},{4,5},{5,4},{6,7},{7,6},{8,9},{9,8},{10,11... | collective-permute-start | bytes 442376 | tf_op jit(solution)/shard_map/ppermute | solution.py:42
  24.2 7.4 %collective-permute-start.6 = (bf16[576,128]{1,0:T(8,128)(2,1)S(1)}, bf16[576,128]{1,0:T(8,128)(2,1)S(1)}, u32[]{:S(2)}, u32[]{:S(2)}) collective-permute-start(bf16[576,128]{1,0:T(8,128)(2,1)S(1)} %broadcast_select_fusion.3.refs_0_), channel_id=1, source_target_pairs={{0,4},{1,5},{2,6},{3,7},{4,0},{5,1},{6,2},{7,3},{8,12},{9,13},{10,... | collective-permute-start | bytes 442376 | tf_op jit(solution)/shard_map/ppermute | solution.py:42
  25.5 6.2 %collective-permute-start.7 = (bf16[576,128]{1,0:T(8,128)(2,1)S(1)}, bf16[576,128]{1,0:T(8,128)(2,1)S(1)}, u32[]{:S(2)}, u32[]{:S(2)}) collective-permute-start(bf16[576,128]{1,0:T(8,128)(2,1)S(1)} %broadcast_select_fusion.3.refs_0_), channel_id=1, source_target_pairs={{0,5},{1,4},{2,7},{3,6},{4,1},{5,0},{6,3},{7,2},{8,13},{9,12},{10,... | collective-permute-start | bytes 442376 | tf_op jit(solution)/shard_map/ppermute | solution.py:42
  30.6 1.0 %copy-start.1 = (bf16[8,128,512]{2,1,0:T(8,128)(2,1)}, bf16[8,128,512]{2,1,0:T(8,128)(2,1)S(1)}, u32[]{:S(2)}) copy-start(bf16[8,128,512]{2,1,0:T(8,128)(2,1)S(1)} %get-tuple-element.26.refs_0_) | copy-start | bytes 3145732
  31.6 3.3 %copy-start.2 = (bf16[8,512,128]{2,1,0:T(8,128)(2,1)}, bf16[8,512,128]{2,1,0:T(8,128)(2,1)S(1)}, u32[]{:S(2)}) copy-start(bf16[8,512,128]{2,1,0:T(8,128)(2,1)S(1)} %get-tuple-element.27.refs_1_) | copy-start | bytes 3145732
  31.6 3.3 %copy-start.3 = (bf16[8,80,512]{2,1,0:T(8,128)(2,1)}, bf16[8,80,512]{2,1,0:T(8,128)(2,1)S(1)}, u32[]{:S(2)}) copy-start(bf16[8,80,512]{2,1,0:T(8,128)(2,1)S(1)} %get-tuple-element.28.refs_2_) | copy-start | bytes 1966084
  34.9 5.4 %copy-start.4 = (bf16[8,256,128]{2,1,0:T(8,128)(2,1)}, bf16[8,256,128]{2,1,0:T(8,128)(2,1)S(1)}, u32[]{:S(2)}) copy-start(bf16[8,256,128]{2,1,0:T(8,128)(2,1)S(1)} %get-tuple-element.31.refs_3_) | copy-start | bytes 1572868
  34.9 5.3 %copy-start.5 = (bf16[8,80,256]{2,1,0:T(8,128)(2,1)}, bf16[8,80,256]{2,1,0:T(8,128)(2,1)S(1)}, u32[]{:S(2)}) copy-start(bf16[8,80,256]{2,1,0:T(8,128)(2,1)S(1)} %get-tuple-element.32.refs_4_) | copy-start | bytes 983044
  34.9 5.3 %collective-permute-start.8 = (bf16[8,256,128]{2,1,0:T(8,128)(2,1)S(1)}, bf16[8,256,128]{2,1,0:T(8,128)(2,1)S(1)}, u32[]{:S(2)}, u32[]{:S(2)}) collective-permute-start(bf16[8,256,128]{2,1,0:T(8,128)(2,1)S(1)} %get-tuple-element.31.refs_3_), channel_id=1, source_target_pairs={{0,2},{2,0},{4,6},{6,4},{8,10},{10,8},{12,14},{14,12},{16,18},{18,... | collective-permute-start | bytes 1572872 | tf_op jit(solution)/shard_map/ppermute | solution.py:32
  38.2 2.0 %collective-permute-start.9 = (bf16[8,80,256]{2,1,0:T(8,128)(2,1)S(1)}, bf16[8,80,256]{2,1,0:T(8,128)(2,1)S(1)}, u32[]{:S(2)}, u32[]{:S(2)}) collective-permute-start(bf16[8,80,256]{2,1,0:T(8,128)(2,1)S(1)} %get-tuple-element.32.refs_4_), channel_id=1, source_target_pairs={{0,2},{2,0},{4,6},{6,4},{8,10},{10,8},{12,14},{14,12},{16,18},{18,... | collective-permute-start | bytes 983048 | tf_op jit(solution)/shard_map/ppermute | solution.py:32
  40.2 0.7 copy-start.9
  40.2 1.0 %copy-start.7 = (bf16[8,256,128]{2,1,0:T(8,128)(2,1)}, bf16[8,256,128]{2,1,0:T(8,128)(2,1)S(1)}, u32[]{:S(2)}) copy-start(bf16[8,256,128]{2,1,0:T(8,128)(2,1)S(1)} %collective-permute-done.8.refs_5_) | copy-start | bytes 1572868
  41.2 6.9 %copy-start.10 = (f32[3,576]{1,0:T(4,128)S(1)}, f32[3,576]{1,0:T(4,128)}, u32[]{:S(2)}) copy-start(f32[3,576]{1,0:T(4,128)} %param.10) | copy-start | bytes 20740
  46.9 8.3 %collective-permute-start.10 = (bf16[576,256]{1,0:T(8,128)(2,1)S(1)}, bf16[576,256]{1,0:T(8,128)(2,1)S(1)}, u32[]{:S(2)}, u32[]{:S(2)}) collective-permute-start(bf16[576,256]{1,0:T(8,128)(2,1)S(1)} %bitcast.25), channel_id=1, source_target_pairs={{0,1},{1,0},{2,3},{3,2},{4,5},{5,4},{6,7},{7,6},{8,9},{9,8},{10,11... | collective-permute-start | bytes 884744 | tf_op jit(solution)/shard_map/ppermute | solution.py:42
  53.8 8.0 %collective-permute-start.11 = (bf16[576,256]{1,0:T(8,128)(2,1)S(1)}, bf16[576,256]{1,0:T(8,128)(2,1)S(1)}, u32[]{:S(2)}, u32[]{:S(2)}) collective-permute-start(bf16[576,256]{1,0:T(8,128)(2,1)S(1)} %bitcast.24), channel_id=1, source_target_pairs={{0,1},{1,0},{2,3},{3,2},{4,5},{5,4},{6,7},{7,6},{8,9},{9,8},{10,11... | collective-permute-start | bytes 884744 | tf_op jit(solution)/shard_map/ppermute | solution.py:42
  55.3 10.5 %collective-permute-start.14 = (bf16[576,256]{1,0:T(8,128)(2,1)S(1)}, bf16[576,256]{1,0:T(8,128)(2,1)S(1)}, u32[]{:S(2)}, u32[]{:S(2)}) collective-permute-start(bf16[576,256]{1,0:T(8,128)(2,1)S(1)} %add_convert_fusion.1.hidden_ref), channel_id=1, source_target_pairs={{0,2},{2,0},{4,6},{6,4},{8,10},{10,8},{12,14},{14,12},{16,18},{18,... | collective-permute-start | bytes 884744 | tf_op jit(solution)/shard_map/ppermute | solution.py:32
  56.6 9.3 %collective-permute-start.15 = (bf16[576,256]{1,0:T(8,128)(2,1)S(1)}, bf16[576,256]{1,0:T(8,128)(2,1)S(1)}, u32[]{:S(2)}, u32[]{:S(2)}) collective-permute-start(bf16[576,256]{1,0:T(8,128)(2,1)S(1)} %add_convert_fusion.1.hidden_ref), channel_id=1, source_target_pairs={{2,4},{4,2},{6,8},{8,6},{10,12},{12,10},{14,16},{16,14},{18,20},{2... | collective-permute-start | bytes 884744 | tf_op jit(solution)/shard_map/ppermute | solution.py:340
  61.9 5.1 %collective-permute-start.12 = (bf16[576,256]{1,0:T(8,128)(2,1)S(1)}, bf16[576,256]{1,0:T(8,128)(2,1)S(1)}, u32[]{:S(2)}, u32[]{:S(2)}) collective-permute-start(bf16[576,256]{1,0:T(8,128)(2,1)S(1)} %add_convert_fusion.hidden_ref), channel_id=1, source_target_pairs={{0,2},{2,0},{4,6},{6,4},{8,10},{10,8},{12,14},{14,12},{16,18},{18,... | collective-permute-start | bytes 884744 | tf_op jit(solution)/shard_map/ppermute | solution.py:32
  63.5 9.6 %collective-permute-start.13 = (bf16[576,256]{1,0:T(8,128)(2,1)S(1)}, bf16[576,256]{1,0:T(8,128)(2,1)S(1)}, u32[]{:S(2)}, u32[]{:S(2)}) collective-permute-start(bf16[576,256]{1,0:T(8,128)(2,1)S(1)} %add_convert_fusion.hidden_ref), channel_id=1, source_target_pairs={{2,4},{4,2},{6,8},{8,6},{10,12},{12,10},{14,16},{16,14},{18,20},{2... | collective-permute-start | bytes 884744 | tf_op jit(solution)/shard_map/ppermute | solution.py:340

commit v3 on v2

v3 whole, which is shorter than its diff:
```python
import functools

import jax
import jax.numpy as jnp
from jax import lax
from jax.experimental import pallas as pl
from jax.experimental.pallas import tpu as pltpu
from jax.sharding import PartitionSpec as P

HS = 72
SEG = 16
LANES = 128
VALUE_ROWS = 80
EPSILON = 1e-06
LOG2_E = 1.4426950408889634

CUTS = (0, 2, 4)
CONV_FLOPS = 10**10
VMEM_BYTES = 24 * 2**20
VMEM = pl.BlockSpec(memory_space=pltpu.VMEM)
SMEM = pl.BlockSpec(memory_space=pltpu.SMEM)
HBM = pl.BlockSpec(memory_space=pltpu.HBM)


def outside(x):
    return pltpu.with_memory_space_constraint(x, pltpu.HBM)


def exchanged(block, bit):
    count = lax.axis_size("tm")
    return lax.ppermute(block, "tm", [(i, i ^ bit) for i in range(count)])


def shifted(block, bit, shift):
    frames, heads = lax.axis_size("tm"), lax.axis_size("head")
    route = [
        (f * heads + h, (f ^ bit) * heads + (h + shift) % heads)
        for f in range(frames)
        for h in range(heads)
    ]
    return lax.ppermute(block, ("tm", "head"), route)


def project_kernel(blocks, parts, factor, order_ref, modulation_ref, w_hbm, *refs):
    pieces = refs[: blocks * parts]
    *query_ref, key_ref, value_ref, x_ref, shift_ref, scale_ref, w_ref, w_sem = refs[blocks * parts :]
    features, tokens = x_ref.shape
    width = features // parts
    heads = key_ref.shape[0]
    count = w_ref.shape[0]
    loads = [
        pltpu.make_async_copy(w_hbm.at[3 - count + c], w_ref.at[c], w_sem.at[c]) for c in range(count)
    ]
    for load in loads:
        load.start()
    first = 0
    for block in range(blocks):
        for part, piece in enumerate(pieces[block * parts : (block + 1) * parts]):
            start = pl.multiple_of(order_ref[part] * width, 32)
            x_ref[pl.ds(start, width), first : first + piece.shape[1]] = piece[...]
        first += piece.shape[1]
    columns = as_columns(modulation_ref)
    shift_ref[...] = jnp.broadcast_to(columns[:, 0:1], (features, LANES))
    scale_ref[...] = jnp.broadcast_to(1.0 + columns[:, 1:2], (features, LANES))
    for start in range(0, tokens, LANES):
        values = x_ref[:, start : start + LANES].astype(jnp.float32)
        centred = values - jnp.sum(values, axis=0, keepdims=True) / features
        variance = jnp.sum(centred * centred, axis=0, keepdims=True) / features
        normed = centred * lax.rsqrt(variance + EPSILON)
        x_ref[:, start : start + LANES] = (normed * scale_ref[...] + shift_ref[...]).astype(jnp.bfloat16)

    row = lax.broadcasted_iota(jnp.int32, (VALUE_ROWS - HS, tokens), 0)
    ones = jnp.where(row == 0, 1.0, 0.0).astype(jnp.bfloat16)
    group = 2
    for c in range(count):
        loads[c].wait()
        for first in range(0, heads, group):
            total = jnp.dot(
                w_ref[c, first * HS : (first + group) * HS],
                x_ref[...],
                preferred_element_type=jnp.float32,
            )
            for head in range(first, first + group):
                rows = total[(head - first) * HS : (head - first + 1) * HS]
                if c == count - 1:
                    value_ref[head, 0:HS, :] = rows.astype(jnp.bfloat16)
                    value_ref[head, HS:, :] = ones
                elif c == count - 2:
                    key_ref[head, :, 0:HS] = rows.T.astype(jnp.bfloat16)
                    key_ref[head, :, HS:] = jnp.zeros((tokens, LANES - HS), jnp.bfloat16)
                else:
                    query_ref[0][head, 0:HS, :] = (rows * factor).astype(jnp.bfloat16)
                    query_ref[0][head, HS:, :] = jnp.zeros((LANES - HS, tokens), jnp.bfloat16)


def project(blocks, order, modulation, w_qkv, with_queries):
    parts = len(blocks[0])
    tokens = sum(block[0].shape[1] for block in blocks)
    _, width, features = w_qkv.shape
    heads = width // HS
    count = 3 if with_queries else 2
    queries = jax.ShapeDtypeStruct((heads, LANES, tokens), jnp.bfloat16)
    keys = jax.ShapeDtypeStruct((heads, tokens, LANES), jnp.bfloat16)
    values = jax.ShapeDtypeStruct((heads, VALUE_ROWS, tokens), jnp.bfloat16)
    flat = [piece for block in blocks for piece in block]
    return pl.pallas_call(
        functools.partial(project_kernel, len(blocks), parts, HS ** (-0.5) * LOG2_E),
        out_shape=[queries, keys, values][3 - count :],
        in_specs=[SMEM, VMEM, HBM] + [VMEM] * len(flat),
        out_specs=[VMEM] * count,
        scratch_shapes=[
            pltpu.VMEM((features, tokens), jnp.bfloat16),
            pltpu.VMEM((features, LANES), jnp.float32),
            pltpu.VMEM((features, LANES), jnp.float32),
            pltpu.VMEM((count, width, features), jnp.bfloat16),
            pltpu.SemaphoreType.DMA((count,)),
        ],
        compiler_params=pltpu.CompilerParams(vmem_limit_bytes=VMEM_BYTES),
        cost_estimate=pl.CostEstimate(
            flops=2 * tokens * features * width * count,
            bytes_accessed=count * 2 * (features * width + tokens * heads * LANES),
            transcendentals=0,
        ),
    )(order, modulation, outside(w_qkv), *flat)


def flash(heads, score, weigh, collect):
    for head in range(heads + 2):
        if head < heads:
            score(head)
        if head >= 2:
            collect(head - 2)
        if 1 <= head <= heads:
            weigh(head - 1)


def block_kernel(q_ref, k_ref, v_ref, *refs):
    *before_ref, state_ref, scores, weights, tops = refs
    heads = q_ref.shape[0]

    def score(head):
        scores[head % 2] = jnp.dot(k_ref[head], q_ref[head], preferred_element_type=jnp.float32)

    def weigh(head):
        values = scores[head % 2]
        top = jnp.max(values, axis=0, keepdims=True)
        if before_ref:
            top = jnp.maximum(top, before_ref[0][head, HS + 1 : HS + 2, :])
        tops[head : head + 1, :] = top
        weights[head % 2] = jnp.exp2(values - top).astype(jnp.bfloat16)

    def collect(head):
        total = jnp.dot(v_ref[head], weights[head % 2], preferred_element_type=jnp.float32)
        if before_ref:
            before = before_ref[0][head]
            total += before * jnp.exp2(before[HS + 1 : HS + 2] - tops[head : head + 1, :])
        state_ref[head] = total
        state_ref[head, HS + 1 : HS + 2, :] = tops[head : head + 1, :]

    flash(heads, score, weigh, collect)


def attend_block(queries, keys, values, *state):
    heads, _, tokens = queries.shape
    count = keys.shape[1]
    return pl.pallas_call(
        block_kernel,
        out_shape=jax.ShapeDtypeStruct((heads, VALUE_ROWS, tokens), jnp.float32),
        in_specs=[VMEM] * (3 + len(state)),
        out_specs=VMEM,
        scratch_shapes=[
            pltpu.VMEM((2, count, tokens), jnp.float32),
            pltpu.VMEM((2, count, tokens), jnp.bfloat16),
            pltpu.VMEM((heads, tokens), jnp.float32),
        ],
        compiler_params=pltpu.CompilerParams(vmem_limit_bytes=VMEM_BYTES),
        cost_estimate=pl.CostEstimate(
            flops=4 * heads * tokens * tokens * LANES,
            bytes_accessed=8 * heads * tokens * LANES,
            transcendentals=heads * tokens * tokens,
        ),
    )(queries, keys, values, *state)


def as_columns(rows_ref):
    count, features = rows_ref.shape
    return jnp.concatenate([rows_ref[...], jnp.zeros((8 - count, features), jnp.float32)]).T


def attend_kernel(parts, bounds, blocks, me_ref, modulation_ref, frame_ref, q_ref, state_ref, *refs):
    keys, values = refs[: 2 * blocks : 2], refs[1 : 2 * blocks : 2]
    w_ref = refs[2 * blocks]
    chunks = len(bounds) - 1
    owns, sends = refs[-5 - 2 * chunks : -5 - chunks], refs[-5 - chunks : -5]
    attended, terms, scores, weights, tops = refs[-5:]
    heads = q_ref.shape[0]
    width = frame_ref.shape[0]
    spans, total = [], 0
    for ref in keys:
        spans.append((total, total + ref.shape[1]))
        total += ref.shape[1]

    def score(head):
        for ref, (low, high) in zip(keys, spans):
            scores[head % 2, low:high] = jnp.dot(
                ref[head], q_ref[head], preferred_element_type=jnp.float32
            )

    def weigh(head):
        values = scores[head % 2]
        top = jnp.max(values, axis=0, keepdims=True)
        top = jnp.maximum(top, state_ref[head, HS + 1 : HS + 2, :])
        tops[head : head + 1, :] = top
        weights[head % 2] = jnp.exp2(values - top).astype(jnp.bfloat16)

    def collect(head):
        before = state_ref[head]
        total = before * jnp.exp2(before[HS + 1 : HS + 2] - tops[head : head + 1, :])
        for ref, (low, high) in zip(values, spans):
            total += jnp.dot(
                ref[head], weights[head % 2, low:high], preferred_element_type=jnp.float32
            )
        attended[head * HS : (head + 1) * HS, :] = total[:HS] / total[HS : HS + 1]

    flash(heads, score, weigh, collect)
    gate = as_columns(modulation_ref)[:, 2:3]
    me = me_ref[0]
    terms[...] = gate * jnp.dot(
        w_ref[...], attended[...].astype(jnp.bfloat16), preferred_element_type=jnp.float32
    )
    for start, end, own_ref, send_ref in zip(bounds[:-1], bounds[1:], owns, sends):
        residual = frame_ref[:, start:end].astype(jnp.float32)
        mine = pl.ds(pl.multiple_of(me * width, 32), width)
        own_ref[...] = residual + terms[mine, start:end]
        for step in range(1, parts):
            other = pl.multiple_of(lax.rem(me + step, parts) * width, 32)
            send_ref[step - 1] = terms[pl.ds(other, width), start:end].astype(jnp.bfloat16)


def attend(me, parts, modulation, frame, queries, state, kvs, w_out, bounds):
    heads, _, tokens = queries.shape
    features, width = w_out.shape
    part = features // parts
    keys = sum(k.shape[1] for k, _ in kvs)
    rows = [end - start for start, end in zip(bounds[:-1], bounds[1:])]
    outs = pl.pallas_call(
        functools.partial(attend_kernel, parts, bounds, len(kvs)),
        out_shape=[jax.ShapeDtypeStruct((part, r), jnp.float32) for r in rows]
        + [jax.ShapeDtypeStruct((parts - 1, part, r), jnp.bfloat16) for r in rows],
        in_specs=[SMEM] + [VMEM] * (5 + 2 * len(kvs)),
        out_specs=[VMEM] * (2 * len(rows)),
        scratch_shapes=[
            pltpu.VMEM((heads * HS, tokens), jnp.float32),
            pltpu.VMEM((features, tokens), jnp.float32),
            pltpu.VMEM((2, keys, tokens), jnp.float32),
            pltpu.VMEM((2, keys, tokens), jnp.bfloat16),
            pltpu.VMEM((heads, tokens), jnp.float32),
        ],
        compiler_params=pltpu.CompilerParams(vmem_limit_bytes=VMEM_BYTES),
        cost_estimate=pl.CostEstimate(
            flops=4 * heads * tokens * tokens * LANES + 2 * tokens * w_out.size,
            bytes_accessed=8 * heads * tokens * LANES + 2 * w_out.size,
            transcendentals=heads * tokens * tokens,
        ),
    )(me, modulation, frame, queries, state, *[x for kv in kvs for x in kv], w_out)
    return outs[: len(rows)], outs[len(rows) :]


def conv_kernel(start, taps_ref, hidden_ref, near_ref, far_ref, *refs):
    out_hbm, out_ref, sem = refs[-3:]
    hidden = hidden_ref[...].astype(jnp.float32)
    total = hidden + taps_ref[:, 1:2] * hidden
    total += taps_ref[:, 0:1] * near_ref[...].astype(jnp.float32)
    total += taps_ref[:, 2:3] * far_ref[...].astype(jnp.float32)
    out_ref[...] = total.astype(jnp.bfloat16)
    rows = out_ref.shape[1]
    store = pltpu.make_async_copy(out_ref, out_hbm.at[:, start : start + rows], sem)
    store.start()
    store.wait()


def convolved(taps, hidden, near, far, start, tokens, out):
    width, rows = hidden.shape
    before = [] if out is None else [out]
    return pl.pallas_call(
        functools.partial(conv_kernel, start),
        out_shape=jax.ShapeDtypeStruct((width, tokens), jnp.bfloat16),
        in_specs=[VMEM] * 4 + [HBM] * len(before),
        out_specs=HBM,
        scratch_shapes=[pltpu.VMEM((width, rows), jnp.bfloat16), pltpu.SemaphoreType.DMA],
        input_output_aliases={4: 0} if before else {},
        compiler_params=pltpu.CompilerParams(vmem_limit_bytes=VMEM_BYTES),
        cost_estimate=pl.CostEstimate(
            flops=CONV_FLOPS, bytes_accessed=8 * width * rows, transcendentals=0
        ),
    )(taps, hidden, near, far, *before)


def tied(x, *others):
    return lax.optimization_barrier((x, *others))[0]


def local(frames, modulation, w_qkv, w_out, conv_taps, anchors):
    frame = frames[0].T
    width, tokens = frame.shape
    parts, count = lax.axis_size("head"), lax.axis_size("tm")
    place, me = lax.axis_index("tm"), lax.axis_index("head")
    anchor = lax.dynamic_index_in_dim(anchors, place // SEG, 0, keepdims=False)
    order = ((me - jnp.arange(parts)) % parts).astype(jnp.int32)
    me_ref = me.astype(jnp.int32).reshape(1)
    w_qkv = jnp.swapaxes(w_qkv, 1, 2)
    index = place % SEG

    def bit(number):
        return (index >> number) & 1

    def same(number):
        return bit(number) == (anchor >> number) & 1

    own = [[frame] + [shifted(frame, 0, step) for step in range(1, parts)]]

    def halves(block, number):
        half = block.shape[1] // 2
        low, high = block[:, :half], block[:, half:]
        return jnp.where(bit(number) == 0, low, high), jnp.where(bit(number) == 0, high, low)

    kept, sent = lax.optimization_barrier(halves(frame, 0))
    block = jnp.where(same(0), kept, exchanged(sent, 1))
    kept, sent = halves(block, 1)
    came = lax.cond(anchors[0] >= 0, lambda x: exchanged(x, 2), jnp.zeros_like, sent)
    block = jnp.where(same(1), kept, came)
    for number in range(2, SEG.bit_length() - 1):
        sent = block
        came = exchanged(sent, 1 << number)
        if number == 2:
            w_out = tied(w_out, sent).T
            came = tied(came, w_out)
        if number == 3:
            own[0][0] = tied(own[0][0], sent)
            queries, *own_kv = project(own, order, modulation, w_qkv, True)
            came = tied(came, queries)
        block = jnp.where(same(number), block, came)
    near = [block] + [shifted(block, 0, step) for step in range(1, parts)]
    across = [shifted(block, 2, step) for step in range(parts)]
    state = attend_block(tied(queries, block), *own_kv)
    near[0] = tied(near[0], state)
    near_kv = project([near, across], order, modulation, w_qkv, False)
    far_kv = [exchanged(x, 1) for x in near_kv]
    state = attend_block(queries, *near_kv, state)
    kvs = [[tied(x, state) for x in far_kv]]

    odd = []
    for h in range(parts):
        for f in range(1, count - 1, 2):
            here, there = f * parts + h, (f + 1) * parts + h
            odd += [(here, there), (there, here)]
        for f in (0, count - 1):
            odd.append((f * parts + h, f * parts + (h + 1) % parts))
    is_even = place % 2 == 0
    tap_near = jnp.where(is_even, conv_taps[2], conv_taps[0])
    tap_far = jnp.where(is_even, conv_taps[0], conv_taps[2])
    tap_far = jnp.where((place == 0) | (place == count - 1), 0.0, tap_far)
    taps = jnp.stack([tap_near, conv_taps[1], tap_far]).T
    bounds = [tokens * cut // 4 for cut in CUTS]
    spans = list(zip(bounds[:-1], bounds[1:]))
    totals, sends = attend(me_ref, parts, modulation, frame, queries, state, kvs, w_out, bounds)
    received = [[shifted(send[step - 1], 0, step) for step in range(1, parts)] for send in sends]
    out, sent = None, []
    for chunk, (start, end) in enumerate(spans):
        total = tied(totals[chunk], *sent)
        for part in received[chunk]:
            total = total + part.astype(jnp.float32)
        hidden = total.astype(jnp.bfloat16)
        sent = [hidden]
        close, far = exchanged(hidden, 1), lax.ppermute(hidden, ("tm", "head"), odd)
        out = convolved(taps, hidden, close, far, start, tokens, out)
    return out.T[None]


def solution(mesh):
    in_specs = (
        P("tm", None, "head"),
        P(),
        P(None, None, "head"),
        P("head", None),
        P(None, "head"),
        P(),
    )
    out_specs = P("tm", None, "head")
    return jax.shard_map(local, mesh=mesh, in_specs=in_specs, out_specs=out_specs, check_vma=False)
```

time: 75.3 us -> 70.7 us (0.939); the launches traced: 74.2 us -> 70.4 us
  Pallas kernels: 21.7 us -> 17.8 us
  waiting for transfers between devices: 27.6 us -> 29.3 us
  other arithmetic: 2.69 us -> 1.38 us
  local copies, waits for them, and re-layouts: 3.85 us -> 3.04 us
    ppermute x6, waiting for transfers between devices: 5.89 us -> 15.5 us  [shifted(): return lax.ppermute(block, ('tm', 'head'), route)]
    ppermute x8, waiting for transfers between devices: 15.5 us -> 6.95 us  [exchanged(): return lax.ppermute(block, 'tm', [(i, i ^ bit) for i in range(count)])]
    pallas_call x2 -> x3, Pallas kernels: 11.3 us -> 7.41 us  [the longest x2 4.06 us: attend_block(): pl.pallas_call(block_kernel, out_shape=jax.ShapeDtypeStruct((heads, VALUE...]
    unnamed x22 -> x8, local copies, waits for them, and re-layouts: 1.94 us -> 0.72 us
    select_n x6, other arithmetic: 2.37 us -> 1.21 us  [the longest x2 1.11 us: halves(): jnp.where(bit(number) == 0, high, low)]
  transfers between devices with their start and end apart: 16 -> 16, of which waited for: 10 -> 10; matrix products, arithmetic and copies ran while one was open for 3% -> 4% of each run, Pallas kernels for 16% -> 14%
where the time goes in v3:
time: 70.7 us; the launch traced here: 70.4 us
  waiting for transfers between devices  29.3 us (41%)
  starting transfers between devices  18.1 us (26%)
  Pallas kernels  17.8 us (25%)
  local copies, waits for them, and re-layouts  3.04 us (4%)
  other arithmetic  1.38 us (2%)
  between operations  0.82 us (1%)
    ppermute x6, waiting for transfers between devices, shifted(): return lax.ppermute(block, ('tm', 'head'), route)  15.5 us
    ppermute x8, starting transfers between devices, exchanged(): return lax.ppermute(block, 'tm', [(i, i ^ bit) for i in range(count)])  8.43 us
    pallas_call x2, Pallas kernels, project(): pl.pallas_call(functools.partial(project_kernel, len(blocks), parts, HS *...  8.21 us
    ppermute x8, waiting for transfers between devices, exchanged(): return lax.ppermute(block, 'tm', [(i, i ^ bit) for i in range(count)])  6.95 us
    ppermute x2, waiting for transfers between devices, local(): lax.ppermute(hidden, ('tm', 'head'), odd)  6.84 us
    ppermute x6, starting transfers between devices, shifted(): return lax.ppermute(block, ('tm', 'head'), route)  6.15 us
    pallas_call x2, Pallas kernels, attend_block(): pl.pallas_call(block_kernel, out_shape=jax.ShapeDtypeStruct((heads, VALUE...  4.06 us
    ppermute x2, starting transfers between devices, local(): lax.ppermute(hidden, ('tm', 'head'), odd)  3.54 us
  transfers between devices with their start and end apart: 16, of which 10 were waited for; matrix products, arithmetic and copies ran while one was open for 4% of the time, Pallas kernels for 14%

profile of v3, /device:TPU:25, one launch (start us, length us, event | category | flops | bytes accessed | tf_op | source)
XLA Modules:
  0.0 70.4 jit_solution(9715111998088644547)
XLA Ops:
  0.0 1.1 %broadcast_select_fusion.1 = (bf16[576,256]{1,0:T(8,128)(2,1)S(1)}, bf16[576,256]{1,0:T(8,128)(2,1)S(1)}) fusion(pred[]{:T(512)S(6)} %eq.41, bf16[576,512]{1,0:T(8,128)(2,1)} %bitcast.18), kind=kLoop, calls=%fused_computation.3 | loop fusion | flops 294912 | bytes 1179649 | tf_op jit(solution)/shard_map/jit(_where)/select_n | solution.py:325
  1.1 0.7 %collective-permute-start.1 = (bf16[576,256]{1,0:T(8,128)(2,1)S(1)}, bf16[576,256]{1,0:T(8,128)(2,1)S(1)}, u32[]{:S(2)}, u32[]{:S(2)}) collective-permute-start(bf16[576,256]{1,0:T(8,128)(2,1)S(1)} %get-tuple-element.40), channel_id=1, source_target_pairs={{0,2},{2,0},{4,6},{6,4},{8,10},{10,8},{12,14},{14,12},{16,18},{18,... | collective-permute-start | bytes 884744 | tf_op jit(solution)/shard_map/ppermute | solution.py:31
  1.8 1.3 %collective-permute-start.3 = (bf16[576,512]{1,0:T(8,128)(2,1)}, bf16[576,512]{1,0:T(8,128)(2,1)S(1)}, u32[]{:S(2)}, u32[]{:S(2)}) collective-permute-start(bf16[576,512]{1,0:T(8,128)(2,1)} %bitcast.19), channel_id=1, source_target_pairs={{0,1},{1,0},{2,3},{3,2},{4,5},{5,4},{6,7},{7,6},{8,9},{9,8},{10,11... | collective-permute-start | bytes 1769480 | tf_op jit(solution)/shard_map/ppermute | solution.py:41
  3.8 0.0 collective-permute-done.1
  3.8 5.3 %conditional.1 = (bf16[576,128]{1,0:T(8,128)(2,1)}) conditional(s32[]{:T(128)} %bitcast.9, () %tuple.23, (pred[]{:T(512)}, bf16[576,128]{1,0:T(8,128)(2,1)S(1)}, bf16[576,128]{1,0:T(8,128)(2,1)S(1)}) %tuple.24), branch_computations={%region_0.1_spmd, %region_1.2_spmd} | conditional | flops 73728 | bytes 1032241 | solution.py:330
  3.9 1.3 %collective-permute-start = (bf16[576,128]{1,0:T(8,128)(2,1)S(1)}, bf16[576,128]{1,0:T(8,128)(2,1)}, u32[]{:S(2)}, u32[]{:S(2)}) collective-permute-start(bf16[576,128]{1,0:T(8,128)(2,1)S(1)} %broadcast_select_fusion), channel_id=1, source_target_pairs={{0,4},{2,6},{4,0},{6,2},{8,12},{10,14},{12,8},{14,10},{16,20},{18,... | collective-permute-start | bytes 442376 | tf_op jit(solution)/shard_map/cond/branch_1_fun/ppermute | solution.py:31
  5.2 4.0 %collective-permute-done = bf16[576,128]{1,0:T(8,128)(2,1)} collective-permute-done((bf16[576,128]{1,0:T(8,128)(2,1)S(1)}, bf16[576,128]{1,0:T(8,128)(2,1)}, u32[]{:S(2)}, u32[]{:S(2)}) %collective-permute-start) | collective-permute-done | bytes 147488 | tf_op jit(solution)/shard_map/cond/branch_1_fun/ppermute | solution.py:31
  9.2 0.2 collective-permute-start.2
  9.4 0.0 copy-start.1
  9.4 2.1 %copy.15 = bf16[576,1152]{0,1:T(8,128)(2,1)S(1)} copy(bf16[576,1152]{1,0:T(8,128)(2,1)} %param.11) | data formatting | bytes 2654208 | tf_op jit(solution)/shard_map/optimization_barrier | solution.py:300
  11.6 1.9 %collective-permute-done.2 = bf16[576,128]{1,0:T(8,128)(2,1)S(1)} collective-permute-done((bf16[576,128]{1,0:T(8,128)(2,1)S(1)}, bf16[576,128]{1,0:T(8,128)(2,1)S(1)}, u32[]{:S(2)}, u32[]{:S(2)}) %collective-permute-start.2) | collective-permute-done | bytes 147488 | tf_op jit(solution)/shard_map/ppermute | solution.py:31
  13.6 0.1 collective-permute-start.4
  13.7 3.3 %collective-permute-done.3.refs_1_ = bf16[576,512]{1,0:T(8,128)(2,1)S(1)} collective-permute-done((bf16[576,512]{1,0:T(8,128)(2,1)}, bf16[576,512]{1,0:T(8,128)(2,1)S(1)}, u32[]{:S(2)}, u32[]{:S(2)}) %collective-permute-start.3) | collective-permute-done | bytes 589856 | tf_op jit(solution)/shard_map/ppermute | solution.py:41
  17.0 0.0 copy-done
  17.0 5.0 %shard_map.64 = (bf16[8,128,512]{2,1,0:T(8,128)(2,1)S(1)}, bf16[8,512,128]{2,1,0:T(8,128)(2,1)S(1)}, bf16[8,80,512]{2,1,0:T(8,128)(2,1)S(1)}) custom-call(s32[2]{0:T(128)S(1)} %and_select_fusion.order_ref, f32[3,1152]{1,0:T(4,128)S(1)} %copy-done.1, bf16[3,576,1152]{2,1,0:T(8,128)(2,1)} %bitcast.25, bf16[576,512]{1,0:T(8,128)(2,1)S(1)} %bitcast.20, ...), custom_call_target="tpu_custom_call" | custom-call | flops 2038431744 | bytes 7127040 | tf_op jit(solution)/shard_map/pallas_call | solution.py:106
  21.9 0.4 collective-permute-done.4
  22.4 0.9 %collective-permute-start.5 = (bf16[576,128]{1,0:T(8,128)(2,1)S(1)}, bf16[576,128]{1,0:T(8,128)(2,1)S(1)}, u32[]{:S(2)}, u32[]{:S(2)}) collective-permute-start(bf16[576,128]{1,0:T(8,128)(2,1)S(1)} %broadcast_select_fusion.4.refs_0_), channel_id=1, source_target_pairs={{0,1},{1,0},{2,3},{3,2},{4,5},{5,4},{6,7},{7,6},{8,9},{9,8},{10,11... | collective-permute-start | bytes 442376 | tf_op jit(solution)/shard_map/ppermute | solution.py:41
  23.3 1.7 %collective-permute-start.6 = (bf16[576,128]{1,0:T(8,128)(2,1)S(1)}, bf16[576,128]{1,0:T(8,128)(2,1)S(1)}, u32[]{:S(2)}, u32[]{:S(2)}) collective-permute-start(bf16[576,128]{1,0:T(8,128)(2,1)S(1)} %broadcast_select_fusion.4.refs_0_), channel_id=1, source_target_pairs={{0,4},{1,5},{2,6},{3,7},{4,0},{5,1},{6,2},{7,3},{8,12},{9,13},{10,... | collective-permute-start | bytes 442376 | tf_op jit(solution)/shard_map/ppermute | solution.py:41
  25.0 0.7 %collective-permute-start.7 = (bf16[576,128]{1,0:T(8,128)(2,1)S(1)}, bf16[576,128]{1,0:T(8,128)(2,1)S(1)}, u32[]{:S(2)}, u32[]{:S(2)}) collective-permute-start(bf16[576,128]{1,0:T(8,128)(2,1)S(1)} %broadcast_select_fusion.4.refs_0_), channel_id=1, source_target_pairs={{0,5},{1,4},{2,7},{3,6},{4,1},{5,0},{6,3},{7,2},{8,13},{9,12},{10,... | collective-permute-start | bytes 442376 | tf_op jit(solution)/shard_map/ppermute | solution.py:41
  25.7 2.7 %shard_map.65.refs_0_ = f32[8,80,512]{2,1,0:T(8,128)S(1)} custom-call(bf16[8,128,512]{2,1,0:T(8,128)(2,1)S(1)} %get-tuple-element.46.q_ref, bf16[8,512,128]{2,1,0:T(8,128)(2,1)S(1)} %get-tuple-element.47.k_ref, bf16[8,80,512]{2,1,0:T(8,128)(2,1)S(1)} %get-tuple-element.48.v_ref), custom_call_target="tpu_custom_call" | custom-call | flops 1073741824 | bytes 4194304 | tf_op jit(solution)/shard_map/pallas_call | solution.py:166
  28.5 0.0 collective-permute-done.5.refs_1_
  28.5 0.0 collective-permute-done.6.refs_2_
  28.5 2.7 %collective-permute-done.7.refs_3_ = bf16[576,128]{1,0:T(8,128)(2,1)S(1)} collective-permute-done((bf16[576,128]{1,0:T(8,128)(2,1)S(1)}, bf16[576,128]{1,0:T(8,128)(2,1)S(1)}, u32[]{:S(2)}, u32[]{:S(2)}) %collective-permute-start.7) | collective-permute-done | bytes 147488 | tf_op jit(solution)/shard_map/ppermute | solution.py:41
  31.2 3.2 %shard_map.66 = (bf16[8,256,128]{2,1,0:T(8,128)(2,1)S(1)}, bf16[8,80,256]{2,1,0:T(8,128)(2,1)S(1)}) custom-call(s32[2]{0:T(128)S(1)} %and_select_fusion.order_ref, f32[3,1152]{1,0:T(4,128)S(1)} %copy-done.1, bf16[3,576,1152]{2,1,0:T(8,128)(2,1)} %bitcast.26, bf16[576,128]{1,0:T(8,128)(2,1)S(1)} %broadcast_select_fusion.4.refs_0_, ...), custom_call_target="tpu_custom_call" | custom-call | flops 679477248 | bytes 3702784 | tf_op jit(solution)/shard_map/pallas_call | solution.py:106
  34.4 2.6 %collective-permute-start.8 = (bf16[8,256,128]{2,1,0:T(8,128)(2,1)S(1)}, bf16[8,256,128]{2,1,0:T(8,128)(2,1)S(1)}, u32[]{:S(2)}, u32[]{:S(2)}) collective-permute-start(bf16[8,256,128]{2,1,0:T(8,128)(2,1)S(1)} %get-tuple-element.50.k_ref), channel_id=1, source_target_pairs={{0,2},{2,0},{4,6},{6,4},{8,10},{10,8},{12,14},{14,12},{16,18},{18,... | collective-permute-start | bytes 1572872 | tf_op jit(solution)/shard_map/ppermute | solution.py:31
  37.1 0.1 collective-permute-start.9
  37.2 1.3 %shard_map.67.state_ref = f32[8,80,512]{2,1,0:T(8,128)S(1)} custom-call(bf16[8,128,512]{2,1,0:T(8,128)(2,1)S(1)} %get-tuple-element.46.q_ref, bf16[8,256,128]{2,1,0:T(8,128)(2,1)S(1)} %get-tuple-element.50.k_ref, bf16[8,80,256]{2,1,0:T(8,128)(2,1)S(1)} %get-tuple-element.51.v_ref, f32[8,80,512]{2,1,0:T(8,128)S(1)} %shard_map.65.refs_0_), custom_call_target="tpu_custom_call" | custom-call | flops 1073741824 | bytes 4194304 | tf_op jit(solution)/shard_map/pallas_call | solution.py:166
  38.5 0.6 collective-permute-done.9.refs_1_
  39.1 0.0 collective-permute-done.8.refs_0_
  39.1 3.3 %shard_map.68 = (f32[576,256]{1,0:T(8,128)S(1)}, f32[576,256]{1,0:T(8,128)S(1)}, bf16[1,576,256]{2,1,0:T(8,128)(2,1)}, bf16[1,576,256]{2,1,0:T(8,128)(2,1)S(1)}) custom-call(s32[1]{0:T(128)} %bitcast.1.me_ref, f32[3,1152]{1,0:T(4,128)S(1)} %copy-done.1, bf16[576,512]{1,0:T(8,128)(2,1)S(1)} %bitcast.21, bf16[8,128,512]{2,1,0:T(8,128)(2,1)S(1)} %get-tuple-element.46.q_ref, ...), custom_call_target="tpu_custom_call" | custom-call | flops 1753219072 | bytes 5521408 | tf_op jit(solution)/shard_map/pallas_call | solution.py:246
  42.4 0.7 %copy-done.2 = bf16[1,576,256]{2,1,0:T(8,128)(2,1)} copy-done((bf16[1,576,256]{2,1,0:T(8,128)(2,1)}, bf16[1,576,256]{2,1,0:T(8,128)(2,1)S(1)}, u32[]{:S(2)}) %copy-start.2) | copy-done | bytes 294936
  43.1 0.8 %collective-permute-start.10 = (bf16[576,256]{1,0:T(8,128)(2,1)}, bf16[576,256]{1,0:T(8,128)(2,1)S(1)}, u32[]{:S(2)}, u32[]{:S(2)}) collective-permute-start(bf16[576,256]{1,0:T(8,128)(2,1)} %bitcast.12), channel_id=1, source_target_pairs={{0,1},{1,0},{2,3},{3,2},{4,5},{5,4},{6,7},{7,6},{8,9},{9,8},{10,11... | collective-permute-start | bytes 884744 | tf_op jit(solution)/shard_map/ppermute | solution.py:41
  43.9 0.8 %collective-permute-start.11 = (bf16[576,256]{1,0:T(8,128)(2,1)}, bf16[576,256]{1,0:T(8,128)(2,1)S(1)}, u32[]{:S(2)}, u32[]{:S(2)}) collective-permute-start(bf16[576,256]{1,0:T(8,128)(2,1)} %bitcast.24), channel_id=1, source_target_pairs={{0,1},{1,0},{2,3},{3,2},{4,5},{5,4},{6,7},{7,6},{8,9},{9,8},{10,11... | collective-permute-start | bytes 884744 | tf_op jit(solution)/shard_map/ppermute | solution.py:41
  44.7 6.9 %collective-permute-done.10 = bf16[576,256]{1,0:T(8,128)(2,1)S(1)} collective-permute-done((bf16[576,256]{1,0:T(8,128)(2,1)}, bf16[576,256]{1,0:T(8,128)(2,1)S(1)}, u32[]{:S(2)}, u32[]{:S(2)}) %collective-permute-start.10) | collective-permute-done | bytes 294944 | tf_op jit(solution)/shard_map/ppermute | solution.py:41
  51.6 0.1 add_convert_fusion.1.hidden_ref
  51.6 2.1 %collective-permute-start.14 = (bf16[576,256]{1,0:T(8,128)(2,1)S(1)}, bf16[576,256]{1,0:T(8,128)(2,1)S(1)}, u32[]{:S(2)}, u32[]{:S(2)}) collective-permute-start(bf16[576,256]{1,0:T(8,128)(2,1)S(1)} %add_convert_fusion.1.hidden_ref), channel_id=1, source_target_pairs={{0,2},{2,0},{4,6},{6,4},{8,10},{10,8},{12,14},{14,12},{16,18},{18,... | collective-permute-start | bytes 884744 | tf_op jit(solution)/shard_map/ppermute | solution.py:31
  53.7 1.4 %collective-permute-start.15 = (bf16[576,256]{1,0:T(8,128)(2,1)S(1)}, bf16[576,256]{1,0:T(8,128)(2,1)S(1)}, u32[]{:S(2)}, u32[]{:S(2)}) collective-permute-start(bf16[576,256]{1,0:T(8,128)(2,1)S(1)} %add_convert_fusion.1.hidden_ref), channel_id=1, source_target_pairs={{2,4},{4,2},{6,8},{8,6},{10,12},{12,10},{14,16},{16,14},{18,20},{2... | collective-permute-start | bytes 884744 | tf_op jit(solution)/shard_map/ppermute | solution.py:375
  55.1 0.2 copy.14
  55.3 2.6 %collective-permute-done.11 = bf16[576,256]{1,0:T(8,128)(2,1)S(1)} collective-permute-done((bf16[576,256]{1,0:T(8,128)(2,1)}, bf16[576,256]{1,0:T(8,128)(2,1)S(1)}, u32[]{:S(2)}, u32[]{:S(2)}) %collective-permute-start.11) | collective-permute-done | bytes 294944 | tf_op jit(solution)/shard_map/ppermute | solution.py:41
  57.9 0.1 add_convert_fusion.hidden_ref
  58.0 1.3 %collective-permute-start.12 = (bf16[576,256]{1,0:T(8,128)(2,1)S(1)}, bf16[576,256]{1,0:T(8,128)(2,1)S(1)}, u32[]{:S(2)}, u32[]{:S(2)}) collective-permute-start(bf16[576,256]{1,0:T(8,128)(2,1)S(1)} %add_convert_fusion.hidden_ref), channel_id=1, source_target_pairs={{0,2},{2,0},{4,6},{6,4},{8,10},{10,8},{12,14},{14,12},{16,18},{18,... | collective-permute-start | bytes 884744 | tf_op jit(solution)/shard_map/ppermute | solution.py:31
  59.2 2.2 %collective-permute-start.13 = (bf16[576,256]{1,0:T(8,128)(2,1)S(1)}, bf16[576,256]{1,0:T(8,128)(2,1)S(1)}, u32[]{:S(2)}, u32[]{:S(2)}) collective-permute-start(bf16[576,256]{1,0:T(8,128)(2,1)S(1)} %add_convert_fusion.hidden_ref), channel_id=1, source_target_pairs={{2,4},{4,2},{6,8},{8,6},{10,12},{12,10},{14,16},{16,14},{18,20},{2... | collective-permute-start | bytes 884744 | tf_op jit(solution)/shard_map/ppermute | solution.py:375
  61.4 0.0 collective-permute-done.14.near_ref
  61.4 4.8 %collective-permute-done.15.far_ref = bf16[576,256]{1,0:T(8,128)(2,1)S(1)} collective-permute-done((bf16[576,256]{1,0:T(8,128)(2,1)S(1)}, bf16[576,256]{1,0:T(8,128)(2,1)S(1)}, u32[]{:S(2)}, u32[]{:S(2)}) %collective-permute-start.15) | collective-permute-done | bytes 294944 | tf_op jit(solution)/shard_map/ppermute | solution.py:375
  66.2 1.1 %shard_map.69.refs_0_ = bf16[576,512]{1,0:T(8,128)(2,1)} custom-call(f32[576,3]{1,0:T(8,128)S(1)} %bitcast.22, bf16[576,256]{1,0:T(8,128)(2,1)S(1)} %add_convert_fusion.1.hidden_ref, bf16[576,256]{1,0:T(8,128)(2,1)S(1)} %collective-permute-done.14.near_ref, bf16[576,256]{1,0:T(8,128)(2,1)S(1)} %collective-permute-done.15.far_ref), custom_call_target="tpu_custom_call" | custom-call | flops 10000000000 | bytes 1179648 | tf_op jit(solution)/shard_map/pallas_call | solution.py:285
  67.3 0.0 collective-permute-done.12.near_ref
  67.3 2.1 %collective-permute-done.13.far_ref = bf16[576,256]{1,0:T(8,128)(2,1)S(1)} collective-permute-done((bf16[576,256]{1,0:T(8,128)(2,1)S(1)}, bf16[576,256]{1,0:T(8,128)(2,1)S(1)}, u32[]{:S(2)}, u32[]{:S(2)}) %collective-permute-start.13) | collective-permute-done | bytes 294944 | tf_op jit(solution)/shard_map/ppermute | solution.py:375
  69.4 1.1 %shard_map.70 = bf16[576,512]{1,0:T(8,128)(2,1)} custom-call(f32[576,3]{1,0:T(8,128)S(1)} %bitcast.23, bf16[576,256]{1,0:T(8,128)(2,1)S(1)} %add_convert_fusion.hidden_ref, bf16[576,256]{1,0:T(8,128)(2,1)S(1)} %collective-permute-done.12.near_ref, bf16[576,256]{1,0:T(8,128)(2,1)S(1)} %collective-permute-done.13.far_ref, ...), custom_call_target="tpu_custom_call", output_to_operand_aliasing={{}: (4, {})} | custom-call | flops 10000000000 | bytes 1179648 | tf_op jit(solution)/shard_map/pallas_call | solution.py:285
  (14 shorter events, 0.2 us)
Async XLA Ops:
  1.1 2.7 %collective-permute-start.1 = (bf16[576,256]{1,0:T(8,128)(2,1)S(1)}, bf16[576,256]{1,0:T(8,128)(2,1)S(1)}, u32[]{:S(2)}, u32[]{:S(2)}) collective-permute-start(bf16[576,256]{1,0:T(8,128)(2,1)S(1)} %get-tuple-element.40), channel_id=1, source_target_pairs={{0,2},{2,0},{4,6},{6,4},{8,10},{10,8},{12,14},{14,12},{16,18},{18,... | collective-permute-start | bytes 884744 | tf_op jit(solution)/shard_map/ppermute | solution.py:31
  1.8 15.1 %collective-permute-start.3 = (bf16[576,512]{1,0:T(8,128)(2,1)}, bf16[576,512]{1,0:T(8,128)(2,1)S(1)}, u32[]{:S(2)}, u32[]{:S(2)}) collective-permute-start(bf16[576,512]{1,0:T(8,128)(2,1)} %bitcast.19), channel_id=1, source_target_pairs={{0,1},{1,0},{2,3},{3,2},{4,5},{5,4},{6,7},{7,6},{8,9},{9,8},{10,11... | collective-permute-start | bytes 1769480 | tf_op jit(solution)/shard_map/ppermute | solution.py:41
  3.9 5.3 %collective-permute-start = (bf16[576,128]{1,0:T(8,128)(2,1)S(1)}, bf16[576,128]{1,0:T(8,128)(2,1)}, u32[]{:S(2)}, u32[]{:S(2)}) collective-permute-start(bf16[576,128]{1,0:T(8,128)(2,1)S(1)} %broadcast_select_fusion), channel_id=1, source_target_pairs={{0,4},{2,6},{4,0},{6,2},{8,12},{10,14},{12,8},{14,10},{16,20},{18,... | collective-permute-start | bytes 442376 | tf_op jit(solution)/shard_map/cond/branch_1_fun/ppermute | solution.py:31
  9.2 4.4 %collective-permute-start.2 = (bf16[576,128]{1,0:T(8,128)(2,1)S(1)}, bf16[576,128]{1,0:T(8,128)(2,1)S(1)}, u32[]{:S(2)}, u32[]{:S(2)}) collective-permute-start(bf16[576,128]{1,0:T(8,128)(2,1)S(1)} %select_select_fusion), channel_id=1, source_target_pairs={{0,8},{2,10},{4,12},{6,14},{8,0},{10,2},{12,4},{14,6},{16,24},{18,... | collective-permute-start | bytes 442376 | tf_op jit(solution)/shard_map/ppermute | solution.py:31
  9.4 7.5 %copy-start = (bf16[1,512,576]{1,2,0:T(8,128)(2,1)S(1)}, bf16[1,512,576]{1,2,0:T(8,128)(2,1)}, u32[]{:S(2)}) copy-start(bf16[1,512,576]{1,2,0:T(8,128)(2,1)} %param.8) | copy-start | bytes 1769476
  9.4 7.5 %copy-start.1 = (f32[3,1152]{1,0:T(4,128)S(1)}, f32[3,1152]{1,0:T(4,128)}, u32[]{:S(2)}) copy-start(f32[3,1152]{1,0:T(4,128)} %modulation_ref.5) | copy-start | bytes 41476
  13.6 8.8 %collective-permute-start.4 = (bf16[576,128]{1,0:T(8,128)(2,1)S(1)}, bf16[576,128]{1,0:T(8,128)(2,1)S(1)}, u32[]{:S(2)}, u32[]{:S(2)}) collective-permute-start(bf16[576,128]{1,0:T(8,128)(2,1)S(1)} %broadcast_select_fusion.5), channel_id=1, source_target_pairs={{0,16},{2,18},{4,20},{6,22},{8,24},{10,26},{12,28},{14,30},{16,0},... | collective-permute-start | bytes 442376 | tf_op jit(solution)/shard_map/ppermute | solution.py:31
  22.4 6.1 %collective-permute-start.5 = (bf16[576,128]{1,0:T(8,128)(2,1)S(1)}, bf16[576,128]{1,0:T(8,128)(2,1)S(1)}, u32[]{:S(2)}, u32[]{:S(2)}) collective-permute-start(bf16[576,128]{1,0:T(8,128)(2,1)S(1)} %broadcast_select_fusion.4.refs_0_), channel_id=1, source_target_pairs={{0,1},{1,0},{2,3},{3,2},{4,5},{5,4},{6,7},{7,6},{8,9},{9,8},{10,11... | collective-permute-start | bytes 442376 | tf_op jit(solution)/shard_map/ppermute | solution.py:41
  23.3 5.2 %collective-permute-start.6 = (bf16[576,128]{1,0:T(8,128)(2,1)S(1)}, bf16[576,128]{1,0:T(8,128)(2,1)S(1)}, u32[]{:S(2)}, u32[]{:S(2)}) collective-permute-start(bf16[576,128]{1,0:T(8,128)(2,1)S(1)} %broadcast_select_fusion.4.refs_0_), channel_id=1, source_target_pairs={{0,4},{1,5},{2,6},{3,7},{4,0},{5,1},{6,2},{7,3},{8,12},{9,13},{10,... | collective-permute-start | bytes 442376 | tf_op jit(solution)/shard_map/ppermute | solution.py:41
  25.0 6.2 %collective-permute-start.7 = (bf16[576,128]{1,0:T(8,128)(2,1)S(1)}, bf16[576,128]{1,0:T(8,128)(2,1)S(1)}, u32[]{:S(2)}, u32[]{:S(2)}) collective-permute-start(bf16[576,128]{1,0:T(8,128)(2,1)S(1)} %broadcast_select_fusion.4.refs_0_), channel_id=1, source_target_pairs={{0,5},{1,4},{2,7},{3,6},{4,1},{5,0},{6,3},{7,2},{8,13},{9,12},{10,... | collective-permute-start | bytes 442376 | tf_op jit(solution)/shard_map/ppermute | solution.py:41
  34.4 4.6 %collective-permute-start.8 = (bf16[8,256,128]{2,1,0:T(8,128)(2,1)S(1)}, bf16[8,256,128]{2,1,0:T(8,128)(2,1)S(1)}, u32[]{:S(2)}, u32[]{:S(2)}) collective-permute-start(bf16[8,256,128]{2,1,0:T(8,128)(2,1)S(1)} %get-tuple-element.50.k_ref), channel_id=1, source_target_pairs={{0,2},{2,0},{4,6},{6,4},{8,10},{10,8},{12,14},{14,12},{16,18},{18,... | collective-permute-start | bytes 1572872 | tf_op jit(solution)/shard_map/ppermute | solution.py:31
  37.1 2.0 %collective-permute-start.9 = (bf16[8,80,256]{2,1,0:T(8,128)(2,1)S(1)}, bf16[8,80,256]{2,1,0:T(8,128)(2,1)S(1)}, u32[]{:S(2)}, u32[]{:S(2)}) collective-permute-start(bf16[8,80,256]{2,1,0:T(8,128)(2,1)S(1)} %get-tuple-element.51.v_ref), channel_id=1, source_target_pairs={{0,2},{2,0},{4,6},{6,4},{8,10},{10,8},{12,14},{14,12},{16,18},{18,... | collective-permute-start | bytes 983048 | tf_op jit(solution)/shard_map/ppermute | solution.py:31
  39.1 4.8 %copy-start.3 = (f32[3,576]{1,0:T(4,128)S(1)}, f32[3,576]{1,0:T(4,128)}, u32[]{:S(2)}) copy-start(f32[3,576]{1,0:T(4,128)} %param.12) | copy-start | bytes 20740
  42.4 0.7 %copy-start.2 = (bf16[1,576,256]{2,1,0:T(8,128)(2,1)}, bf16[1,576,256]{2,1,0:T(8,128)(2,1)S(1)}, u32[]{:S(2)}) copy-start(bf16[1,576,256]{2,1,0:T(8,128)(2,1)S(1)} %get-tuple-element.58) | copy-start | bytes 884740
  43.1 8.4 %collective-permute-start.10 = (bf16[576,256]{1,0:T(8,128)(2,1)}, bf16[576,256]{1,0:T(8,128)(2,1)S(1)}, u32[]{:S(2)}, u32[]{:S(2)}) collective-permute-start(bf16[576,256]{1,0:T(8,128)(2,1)} %bitcast.12), channel_id=1, source_target_pairs={{0,1},{1,0},{2,3},{3,2},{4,5},{5,4},{6,7},{7,6},{8,9},{9,8},{10,11... | collective-permute-start | bytes 884744 | tf_op jit(solution)/shard_map/ppermute | solution.py:41
  43.9 14.0 %collective-permute-start.11 = (bf16[576,256]{1,0:T(8,128)(2,1)}, bf16[576,256]{1,0:T(8,128)(2,1)S(1)}, u32[]{:S(2)}, u32[]{:S(2)}) collective-permute-start(bf16[576,256]{1,0:T(8,128)(2,1)} %bitcast.24), channel_id=1, source_target_pairs={{0,1},{1,0},{2,3},{3,2},{4,5},{5,4},{6,7},{7,6},{8,9},{9,8},{10,11... | collective-permute-start | bytes 884744 | tf_op jit(solution)/shard_map/ppermute | solution.py:41
  51.6 9.8 %collective-permute-start.14 = (bf16[576,256]{1,0:T(8,128)(2,1)S(1)}, bf16[576,256]{1,0:T(8,128)(2,1)S(1)}, u32[]{:S(2)}, u32[]{:S(2)}) collective-permute-start(bf16[576,256]{1,0:T(8,128)(2,1)S(1)} %add_convert_fusion.1.hidden_ref), channel_id=1, source_target_pairs={{0,2},{2,0},{4,6},{6,4},{8,10},{10,8},{12,14},{14,12},{16,18},{18,... | collective-permute-start | bytes 884744 | tf_op jit(solution)/shard_map/ppermute | solution.py:31
  53.7 12.5 %collective-permute-start.15 = (bf16[576,256]{1,0:T(8,128)(2,1)S(1)}, bf16[576,256]{1,0:T(8,128)(2,1)S(1)}, u32[]{:S(2)}, u32[]{:S(2)}) collective-permute-start(bf16[576,256]{1,0:T(8,128)(2,1)S(1)} %add_convert_fusion.1.hidden_ref), channel_id=1, source_target_pairs={{2,4},{4,2},{6,8},{8,6},{10,12},{12,10},{14,16},{16,14},{18,20},{2... | collective-permute-start | bytes 884744 | tf_op jit(solution)/shard_map/ppermute | solution.py:375
  58.0 9.3 %collective-permute-start.12 = (bf16[576,256]{1,0:T(8,128)(2,1)S(1)}, bf16[576,256]{1,0:T(8,128)(2,1)S(1)}, u32[]{:S(2)}, u32[]{:S(2)}) collective-permute-start(bf16[576,256]{1,0:T(8,128)(2,1)S(1)} %add_convert_fusion.hidden_ref), channel_id=1, source_target_pairs={{0,2},{2,0},{4,6},{6,4},{8,10},{10,8},{12,14},{14,12},{16,18},{18,... | collective-permute-start | bytes 884744 | tf_op jit(solution)/shard_map/ppermute | solution.py:31
  59.2 10.1 %collective-permute-start.13 = (bf16[576,256]{1,0:T(8,128)(2,1)S(1)}, bf16[576,256]{1,0:T(8,128)(2,1)S(1)}, u32[]{:S(2)}, u32[]{:S(2)}) collective-permute-start(bf16[576,256]{1,0:T(8,128)(2,1)S(1)} %add_convert_fusion.hidden_ref), channel_id=1, source_target_pairs={{2,4},{4,2},{6,8},{8,6},{10,12},{12,10},{14,16},{16,14},{18,20},{2... | collective-permute-start | bytes 884744 | tf_op jit(solution)/shard_map/ppermute | solution.py:375

commit v4 on v3

--- a/solution.py
+++ b/solution.py
@@ -41,18 +41,21 @@
     return lax.ppermute(block, ("tm", "head"), route)
 
 
-def project_kernel(blocks, parts, factor, order_ref, modulation_ref, w_hbm, *refs):
+def project_kernel(blocks, parts, with_queries, factor, order_ref, modulation_ref, w_hbm, *refs):
     pieces = refs[: blocks * parts]
     *query_ref, key_ref, value_ref, x_ref, shift_ref, scale_ref, w_ref, w_sem = refs[blocks * parts :]
     features, tokens = x_ref.shape
     width = features // parts
     heads = key_ref.shape[0]
     count = w_ref.shape[0]
-    loads = [
-        pltpu.make_async_copy(w_hbm.at[3 - count + c], w_ref.at[c], w_sem.at[c]) for c in range(count)
-    ]
-    for load in loads:
-        load.start()
+    loads = []
+    if with_queries:
+        loads = [
+            pltpu.make_async_copy(w_hbm.at[c], w_ref.at[c], w_sem.at[c]) for c in range(count)
+        ]
+    if with_queries:
+        for load in loads:
+            load.start()
     first = 0
     for block in range(blocks):
         for part, piece in enumerate(pieces[block * parts : (block + 1) * parts]):
@@ -73,10 +76,12 @@
     ones = jnp.where(row == 0, 1.0, 0.0).astype(jnp.bfloat16)
     group = 2
     for c in range(count):
-        loads[c].wait()
+        if with_queries:
+            loads[c].wait()
         for first in range(0, heads, group):
+            span = slice(first * HS, (first + group) * HS)
             total = jnp.dot(
-                w_ref[c, first * HS : (first + group) * HS],
+                w_ref[c, span] if with_queries else w_hbm[c + 1, span],
                 x_ref[...],
                 preferred_element_type=jnp.float32,
             )
@@ -104,9 +109,11 @@
     values = jax.ShapeDtypeStruct((heads, VALUE_ROWS, tokens), jnp.bfloat16)
     flat = [piece for block in blocks for piece in block]
     return pl.pallas_call(
-        functools.partial(project_kernel, len(blocks), parts, HS ** (-0.5) * LOG2_E),
+        functools.partial(
+            project_kernel, len(blocks), parts, with_queries, HS ** (-0.5) * LOG2_E
+        ),
         out_shape=[queries, keys, values][3 - count :],
-        in_specs=[SMEM, VMEM, HBM] + [VMEM] * len(flat),
+        in_specs=[SMEM, VMEM, HBM if with_queries else VMEM] + [VMEM] * len(flat),
         out_specs=[VMEM] * count,
         scratch_shapes=[
             pltpu.VMEM((features, tokens), jnp.bfloat16),
@@ -121,7 +128,7 @@
             bytes_accessed=count * 2 * (features * width + tokens * heads * LANES),
             transcendentals=0,
         ),
-    )(order, modulation, outside(w_qkv), *flat)
+    )(order, modulation, outside(w_qkv) if with_queries else w_qkv, *flat)
 
 
 def flash(heads, score, weigh, collect):
@@ -191,8 +198,8 @@
     keys, values = refs[: 2 * blocks : 2], refs[1 : 2 * blocks : 2]
     w_ref = refs[2 * blocks]
     chunks = len(bounds) - 1
-    owns, sends = refs[-5 - 2 * chunks : -5 - chunks], refs[-5 - chunks : -5]
-    attended, terms, scores, weights, tops = refs[-5:]
+    owns, sends = refs[-7 - 2 * chunks : -7 - chunks], refs[-7 - chunks : -7]
+    attended, terms, scores, weights, tops, held, sem = refs[-7:]
     heads = q_ref.shape[0]
     width = frame_ref.shape[0]
     spans, total = [], 0
@@ -228,13 +235,18 @@
     terms[...] = gate * jnp.dot(
         w_ref[...], attended[...].astype(jnp.bfloat16), preferred_element_type=jnp.float32
     )
+    mine = pl.ds(pl.multiple_of(me * width, 32), width)
+    held[...] = frame_ref[:, bounds[-2] :].astype(jnp.float32) + terms[mine, bounds[-2] :]
+    store = pltpu.make_async_copy(held, owns[-1], sem)
+    store.start()
     for start, end, own_ref, send_ref in zip(bounds[:-1], bounds[1:], owns, sends):
-        residual = frame_ref[:, start:end].astype(jnp.float32)
-        mine = pl.ds(pl.multiple_of(me * width, 32), width)
-        own_ref[...] = residual + terms[mine, start:end]
+        if end < bounds[-1]:
+            residual = frame_ref[:, start:end].astype(jnp.float32)
+            own_ref[...] = residual + terms[mine, start:end]
         for step in range(1, parts):
             other = pl.multiple_of(lax.rem(me + step, parts) * width, 32)
             send_ref[step - 1] = terms[pl.ds(other, width), start:end].astype(jnp.bfloat16)
+    store.wait()
 
 
 def attend(me, parts, modulation, frame, queries, state, kvs, w_out, bounds):
@@ -245,16 +257,19 @@
     rows = [end - start for start, end in zip(bounds[:-1], bounds[1:])]
     outs = pl.pallas_call(
         functools.partial(attend_kernel, parts, bounds, len(kvs)),
-        out_shape=[jax.ShapeDtypeStruct((part, r), jnp.float32) for r in rows]
+        out_shape=[jax.ShapeDtypeStruct((part, r), jnp.float32) for r in rows[:-1]]
+        + [pltpu.HBM((part, rows[-1]), jnp.float32)]
         + [jax.ShapeDtypeStruct((parts - 1, part, r), jnp.bfloat16) for r in rows],
         in_specs=[SMEM] + [VMEM] * (5 + 2 * len(kvs)),
-        out_specs=[VMEM] * (2 * len(rows)),
+        out_specs=[VMEM] * (len(rows) - 1) + [HBM] + [VMEM] * len(rows),
         scratch_shapes=[
             pltpu.VMEM((heads * HS, tokens), jnp.float32),
             pltpu.VMEM((features, tokens), jnp.float32),
             pltpu.VMEM((2, keys, tokens), jnp.float32),
             pltpu.VMEM((2, keys, tokens), jnp.bfloat16),
             pltpu.VMEM((heads, tokens), jnp.float32),
+            pltpu.VMEM((part, rows[-1]), jnp.float32),
+            pltpu.SemaphoreType.DMA,
         ],
         compiler_params=pltpu.CompilerParams(vmem_limit_bytes=VMEM_BYTES),
         cost_estimate=pl.CostEstimate(

time: 70.7 us -> 68.9 us (0.975)
  Pallas kernels: 17.8 us -> 16.9 us
    pallas_call x2, Pallas kernels: 8.21 us -> 7.33 us  [project(): pl.pallas_call(functools.partial(project_kernel, len(blocks), parts, with...]
  transfers between devices with their start and end apart: 16 -> 16, of which waited for: 10 -> 10; matrix products, arithmetic and copies ran while one was open for 4% -> 4% of each run, Pallas kernels for 14% -> 15%
where the time goes in v4:
time: 68.9 us; the launch traced here: 68.7 us
  waiting for transfers between devices  29 us (42%)
  starting transfers between devices  18.2 us (26%)
  Pallas kernels  16.9 us (25%)
  local copies, waits for them, and re-layouts  2.34 us (3%)
  other arithmetic  1.38 us (2%)
  between operations  0.84 us (1%)
    ppermute x6, waiting for transfers between devices, shifted(): return lax.ppermute(block, ('tm', 'head'), route)  15.2 us
    ppermute x8, starting transfers between devices, exchanged(): return lax.ppermute(block, 'tm', [(i, i ^ bit) for i in range(count)])  8.46 us
    pallas_call x2, Pallas kernels, project(): pl.pallas_call(functools.partial(project_kernel, len(blocks), parts, with...  7.33 us
    ppermute x8, waiting for transfers between devices, exchanged(): return lax.ppermute(block, 'tm', [(i, i ^ bit) for i in range(count)])  6.94 us
    ppermute x2, waiting for transfers between devices, local(): lax.ppermute(hidden, ('tm', 'head'), odd)  6.84 us
    ppermute x6, starting transfers between devices, shifted(): return lax.ppermute(block, ('tm', 'head'), route)  6.22 us
    pallas_call x2, Pallas kernels, attend_block(): pl.pallas_call(block_kernel, out_shape=jax.ShapeDtypeStruct((heads, VALUE...  4.07 us
    ppermute x2, starting transfers between devices, local(): lax.ppermute(hidden, ('tm', 'head'), odd)  3.55 us
  transfers between devices with their start and end apart: 16, of which 10 were waited for; matrix products, arithmetic and copies ran while one was open for 4% of the time, Pallas kernels for 15%

profile of v4, /device:TPU:25, one launch (start us, length us, event | category | flops | bytes accessed | tf_op | source)
XLA Modules:
  0.0 68.7 jit_solution(5726315042457584959)
XLA Ops:
  0.0 1.1 %broadcast_select_fusion.1 = (bf16[576,256]{1,0:T(8,128)(2,1)S(1)}, bf16[576,256]{1,0:T(8,128)(2,1)S(1)}) fusion(pred[]{:T(512)S(6)} %eq.41, bf16[576,512]{1,0:T(8,128)(2,1)} %bitcast.20), kind=kLoop, calls=%fused_computation.3 | loop fusion | flops 294912 | bytes 1179649 | tf_op jit(solution)/shard_map/jit(_where)/select_n | solution.py:340
  1.1 0.7 %collective-permute-start.1 = (bf16[576,256]{1,0:T(8,128)(2,1)S(1)}, bf16[576,256]{1,0:T(8,128)(2,1)S(1)}, u32[]{:S(2)}, u32[]{:S(2)}) collective-permute-start(bf16[576,256]{1,0:T(8,128)(2,1)S(1)} %get-tuple-element.40), channel_id=1, source_target_pairs={{0,2},{2,0},{4,6},{6,4},{8,10},{10,8},{12,14},{14,12},{16,18},{18,... | collective-permute-start | bytes 884744 | tf_op jit(solution)/shard_map/ppermute | solution.py:31
  1.8 1.3 %collective-permute-start.3 = (bf16[576,512]{1,0:T(8,128)(2,1)}, bf16[576,512]{1,0:T(8,128)(2,1)S(1)}, u32[]{:S(2)}, u32[]{:S(2)}) collective-permute-start(bf16[576,512]{1,0:T(8,128)(2,1)} %bitcast.21), channel_id=1, source_target_pairs={{0,1},{1,0},{2,3},{3,2},{4,5},{5,4},{6,7},{7,6},{8,9},{9,8},{10,11... | collective-permute-start | bytes 1769480 | tf_op jit(solution)/shard_map/ppermute | solution.py:41
  3.8 0.0 collective-permute-done.1
  3.8 5.3 %conditional.1 = (bf16[576,128]{1,0:T(8,128)(2,1)}) conditional(s32[]{:T(128)} %bitcast.9, () %tuple.23, (pred[]{:T(512)}, bf16[576,128]{1,0:T(8,128)(2,1)S(1)}, bf16[576,128]{1,0:T(8,128)(2,1)S(1)}) %tuple.24), branch_computations={%region_0.1_spmd, %region_1.2_spmd} | conditional | flops 73728 | bytes 1032241 | solution.py:345
  3.9 1.3 %collective-permute-start = (bf16[576,128]{1,0:T(8,128)(2,1)S(1)}, bf16[576,128]{1,0:T(8,128)(2,1)}, u32[]{:S(2)}, u32[]{:S(2)}) collective-permute-start(bf16[576,128]{1,0:T(8,128)(2,1)S(1)} %broadcast_select_fusion), channel_id=1, source_target_pairs={{0,4},{2,6},{4,0},{6,2},{8,12},{10,14},{12,8},{14,10},{16,20},{18,... | collective-permute-start | bytes 442376 | tf_op jit(solution)/shard_map/cond/branch_1_fun/ppermute | solution.py:31
  5.2 4.0 %collective-permute-done = bf16[576,128]{1,0:T(8,128)(2,1)} collective-permute-done((bf16[576,128]{1,0:T(8,128)(2,1)S(1)}, bf16[576,128]{1,0:T(8,128)(2,1)}, u32[]{:S(2)}, u32[]{:S(2)}) %collective-permute-start) | collective-permute-done | bytes 147488 | tf_op jit(solution)/shard_map/cond/branch_1_fun/ppermute | solution.py:31
  9.2 0.2 collective-permute-start.2
  9.4 0.0 copy-start.2
  9.4 2.1 %copy.15 = bf16[576,1152]{0,1:T(8,128)(2,1)S(1)} copy(bf16[576,1152]{1,0:T(8,128)(2,1)} %param.11) | data formatting | bytes 2654208 | tf_op jit(solution)/shard_map/optimization_barrier | solution.py:315
  11.6 1.9 %collective-permute-done.2 = bf16[576,128]{1,0:T(8,128)(2,1)S(1)} collective-permute-done((bf16[576,128]{1,0:T(8,128)(2,1)S(1)}, bf16[576,128]{1,0:T(8,128)(2,1)S(1)}, u32[]{:S(2)}, u32[]{:S(2)}) %collective-permute-start.2) | collective-permute-done | bytes 147488 | tf_op jit(solution)/shard_map/ppermute | solution.py:31
  13.6 0.1 collective-permute-start.4
  13.7 3.3 %collective-permute-done.3.refs_1_ = bf16[576,512]{1,0:T(8,128)(2,1)S(1)} collective-permute-done((bf16[576,512]{1,0:T(8,128)(2,1)}, bf16[576,512]{1,0:T(8,128)(2,1)S(1)}, u32[]{:S(2)}, u32[]{:S(2)}) %collective-permute-start.3) | collective-permute-done | bytes 589856 | tf_op jit(solution)/shard_map/ppermute | solution.py:41
  17.0 0.0 copy-done.1
  17.0 5.0 %shard_map.64 = (bf16[8,128,512]{2,1,0:T(8,128)(2,1)S(1)}, bf16[8,512,128]{2,1,0:T(8,128)(2,1)S(1)}, bf16[8,80,512]{2,1,0:T(8,128)(2,1)S(1)}) custom-call(s32[2]{0:T(128)S(1)} %and_select_fusion.order_ref, f32[3,1152]{1,0:T(4,128)S(1)} %copy-done.2, bf16[3,576,1152]{2,1,0:T(8,128)(2,1)} %bitcast.17, bf16[576,512]{1,0:T(8,128)(2,1)S(1)} %bitcast.22, ...), custom_call_target="tpu_custom_call" | custom-call | flops 2038431744 | bytes 7127040 | tf_op jit(solution)/shard_map/pallas_call | solution.py:111
  21.9 0.4 collective-permute-done.4
  22.4 0.9 %collective-permute-start.5 = (bf16[576,128]{1,0:T(8,128)(2,1)S(1)}, bf16[576,128]{1,0:T(8,128)(2,1)S(1)}, u32[]{:S(2)}, u32[]{:S(2)}) collective-permute-start(bf16[576,128]{1,0:T(8,128)(2,1)S(1)} %broadcast_select_fusion.4.refs_0_), channel_id=1, source_target_pairs={{0,1},{1,0},{2,3},{3,2},{4,5},{5,4},{6,7},{7,6},{8,9},{9,8},{10,11... | collective-permute-start | bytes 442376 | tf_op jit(solution)/shard_map/ppermute | solution.py:41
  23.3 1.7 %collective-permute-start.6 = (bf16[576,128]{1,0:T(8,128)(2,1)S(1)}, bf16[576,128]{1,0:T(8,128)(2,1)S(1)}, u32[]{:S(2)}, u32[]{:S(2)}) collective-permute-start(bf16[576,128]{1,0:T(8,128)(2,1)S(1)} %broadcast_select_fusion.4.refs_0_), channel_id=1, source_target_pairs={{0,4},{1,5},{2,6},{3,7},{4,0},{5,1},{6,2},{7,3},{8,12},{9,13},{10,... | collective-permute-start | bytes 442376 | tf_op jit(solution)/shard_map/ppermute | solution.py:41
  25.0 0.7 %collective-permute-start.7 = (bf16[576,128]{1,0:T(8,128)(2,1)S(1)}, bf16[576,128]{1,0:T(8,128)(2,1)S(1)}, u32[]{:S(2)}, u32[]{:S(2)}) collective-permute-start(bf16[576,128]{1,0:T(8,128)(2,1)S(1)} %broadcast_select_fusion.4.refs_0_), channel_id=1, source_target_pairs={{0,5},{1,4},{2,7},{3,6},{4,1},{5,0},{6,3},{7,2},{8,13},{9,12},{10,... | collective-permute-start | bytes 442376 | tf_op jit(solution)/shard_map/ppermute | solution.py:41
  25.7 2.8 %shard_map.65.refs_0_ = f32[8,80,512]{2,1,0:T(8,128)S(1)} custom-call(bf16[8,128,512]{2,1,0:T(8,128)(2,1)S(1)} %get-tuple-element.46.q_ref, bf16[8,512,128]{2,1,0:T(8,128)(2,1)S(1)} %get-tuple-element.47.k_ref, bf16[8,80,512]{2,1,0:T(8,128)(2,1)S(1)} %get-tuple-element.48.v_ref), custom_call_target="tpu_custom_call" | custom-call | flops 1073741824 | bytes 4194304 | tf_op jit(solution)/shard_map/pallas_call | solution.py:173
  28.5 0.0 collective-permute-done.5.refs_1_
  28.5 0.0 collective-permute-done.6.refs_2_
  28.5 2.7 %collective-permute-done.7.refs_3_ = bf16[576,128]{1,0:T(8,128)(2,1)S(1)} collective-permute-done((bf16[576,128]{1,0:T(8,128)(2,1)S(1)}, bf16[576,128]{1,0:T(8,128)(2,1)S(1)}, u32[]{:S(2)}, u32[]{:S(2)}) %collective-permute-start.7) | collective-permute-done | bytes 147488 | tf_op jit(solution)/shard_map/ppermute | solution.py:41
  31.2 2.3 %shard_map.66 = (bf16[8,256,128]{2,1,0:T(8,128)(2,1)S(1)}, bf16[8,80,256]{2,1,0:T(8,128)(2,1)S(1)}) custom-call(s32[2]{0:T(128)S(1)} %and_select_fusion.order_ref, f32[3,1152]{1,0:T(4,128)S(1)} %copy-done.2, bf16[3,576,1152]{2,1,0:T(8,128)(2,1)S(1)} %bitcast.18, bf16[576,128]{1,0:T(8,128)(2,1)S(1)} %broadcast_select_fusion.4.refs_0_, ...), custom_call_target="tpu_custom_call" | custom-call | flops 679477248 | bytes 3702784 | tf_op jit(solution)/shard_map/pallas_call | solution.py:111
  33.6 2.6 %collective-permute-start.8 = (bf16[8,256,128]{2,1,0:T(8,128)(2,1)S(1)}, bf16[8,256,128]{2,1,0:T(8,128)(2,1)S(1)}, u32[]{:S(2)}, u32[]{:S(2)}) collective-permute-start(bf16[8,256,128]{2,1,0:T(8,128)(2,1)S(1)} %get-tuple-element.50.k_ref), channel_id=1, source_target_pairs={{0,2},{2,0},{4,6},{6,4},{8,10},{10,8},{12,14},{14,12},{16,18},{18,... | collective-permute-start | bytes 1572872 | tf_op jit(solution)/shard_map/ppermute | solution.py:31
  36.2 0.1 collective-permute-start.9
  36.3 1.3 %shard_map.67.state_ref = f32[8,80,512]{2,1,0:T(8,128)S(1)} custom-call(bf16[8,128,512]{2,1,0:T(8,128)(2,1)S(1)} %get-tuple-element.46.q_ref, bf16[8,256,128]{2,1,0:T(8,128)(2,1)S(1)} %get-tuple-element.50.k_ref, bf16[8,80,256]{2,1,0:T(8,128)(2,1)S(1)} %get-tuple-element.51.v_ref, f32[8,80,512]{2,1,0:T(8,128)S(1)} %shard_map.65.refs_0_), custom_call_target="tpu_custom_call" | custom-call | flops 1073741824 | bytes 4194304 | tf_op jit(solution)/shard_map/pallas_call | solution.py:173
  37.6 0.6 collective-permute-done.9.refs_1_
  38.2 0.0 collective-permute-done.8.refs_0_
  38.2 3.3 %shard_map.68 = (f32[576,256]{1,0:T(8,128)S(1)}, f32[576,256]{1,0:T(8,128)}, bf16[1,576,256]{2,1,0:T(8,128)(2,1)S(1)}, bf16[1,576,256]{2,1,0:T(8,128)(2,1)S(1)}) custom-call(s32[1]{0:T(128)} %bitcast.1.me_ref, f32[3,1152]{1,0:T(4,128)S(1)} %copy-done.2, bf16[576,512]{1,0:T(8,128)(2,1)S(1)} %bitcast.23, bf16[8,128,512]{2,1,0:T(8,128)(2,1)S(1)} %get-tuple-element.46.q_ref, ...), custom_call_target="tpu_custom_call" | custom-call | flops 1753219072 | bytes 5521408 | tf_op jit(solution)/shard_map/pallas_call | solution.py:258
  41.5 0.0 copy-start.3
  41.6 0.9 %collective-permute-start.10 = (bf16[576,256]{1,0:T(8,128)(2,1)S(1)}, bf16[576,256]{1,0:T(8,128)(2,1)S(1)}, u32[]{:S(2)}, u32[]{:S(2)}) collective-permute-start(bf16[576,256]{1,0:T(8,128)(2,1)S(1)} %bitcast.27), channel_id=1, source_target_pairs={{0,1},{1,0},{2,3},{3,2},{4,5},{5,4},{6,7},{7,6},{8,9},{9,8},{10,11... | collective-permute-start | bytes 884744 | tf_op jit(solution)/shard_map/ppermute | solution.py:41
  42.4 0.7 %collective-permute-start.11 = (bf16[576,256]{1,0:T(8,128)(2,1)S(1)}, bf16[576,256]{1,0:T(8,128)(2,1)S(1)}, u32[]{:S(2)}, u32[]{:S(2)}) collective-permute-start(bf16[576,256]{1,0:T(8,128)(2,1)S(1)} %bitcast.26), channel_id=1, source_target_pairs={{0,1},{1,0},{2,3},{3,2},{4,5},{5,4},{6,7},{7,6},{8,9},{9,8},{10,11... | collective-permute-start | bytes 884744 | tf_op jit(solution)/shard_map/ppermute | solution.py:41
  43.2 6.7 %collective-permute-done.10 = bf16[576,256]{1,0:T(8,128)(2,1)S(1)} collective-permute-done((bf16[576,256]{1,0:T(8,128)(2,1)S(1)}, bf16[576,256]{1,0:T(8,128)(2,1)S(1)}, u32[]{:S(2)}, u32[]{:S(2)}) %collective-permute-start.10) | collective-permute-done | bytes 294944 | tf_op jit(solution)/shard_map/ppermute | solution.py:41
  49.8 0.1 add_convert_fusion.1.hidden_ref
  49.9 2.1 %collective-permute-start.14 = (bf16[576,256]{1,0:T(8,128)(2,1)S(1)}, bf16[576,256]{1,0:T(8,128)(2,1)S(1)}, u32[]{:S(2)}, u32[]{:S(2)}) collective-permute-start(bf16[576,256]{1,0:T(8,128)(2,1)S(1)} %add_convert_fusion.1.hidden_ref), channel_id=1, source_target_pairs={{0,2},{2,0},{4,6},{6,4},{8,10},{10,8},{12,14},{14,12},{16,18},{18,... | collective-permute-start | bytes 884744 | tf_op jit(solution)/shard_map/ppermute | solution.py:31
  52.0 1.4 %collective-permute-start.15 = (bf16[576,256]{1,0:T(8,128)(2,1)S(1)}, bf16[576,256]{1,0:T(8,128)(2,1)S(1)}, u32[]{:S(2)}, u32[]{:S(2)}) collective-permute-start(bf16[576,256]{1,0:T(8,128)(2,1)S(1)} %add_convert_fusion.1.hidden_ref), channel_id=1, source_target_pairs={{2,4},{4,2},{6,8},{8,6},{10,12},{12,10},{14,16},{16,14},{18,20},{2... | collective-permute-start | bytes 884744 | tf_op jit(solution)/shard_map/ppermute | solution.py:390
  53.4 0.2 copy.14
  53.6 2.6 %collective-permute-done.11 = bf16[576,256]{1,0:T(8,128)(2,1)S(1)} collective-permute-done((bf16[576,256]{1,0:T(8,128)(2,1)S(1)}, bf16[576,256]{1,0:T(8,128)(2,1)S(1)}, u32[]{:S(2)}, u32[]{:S(2)}) %collective-permute-start.11) | collective-permute-done | bytes 294944 | tf_op jit(solution)/shard_map/ppermute | solution.py:41
  56.2 0.1 add_convert_fusion.hidden_ref
  56.2 1.3 %collective-permute-start.12 = (bf16[576,256]{1,0:T(8,128)(2,1)S(1)}, bf16[576,256]{1,0:T(8,128)(2,1)S(1)}, u32[]{:S(2)}, u32[]{:S(2)}) collective-permute-start(bf16[576,256]{1,0:T(8,128)(2,1)S(1)} %add_convert_fusion.hidden_ref), channel_id=1, source_target_pairs={{0,2},{2,0},{4,6},{6,4},{8,10},{10,8},{12,14},{14,12},{16,18},{18,... | collective-permute-start | bytes 884744 | tf_op jit(solution)/shard_map/ppermute | solution.py:31
  57.5 2.2 %collective-permute-start.13 = (bf16[576,256]{1,0:T(8,128)(2,1)S(1)}, bf16[576,256]{1,0:T(8,128)(2,1)S(1)}, u32[]{:S(2)}, u32[]{:S(2)}) collective-permute-start(bf16[576,256]{1,0:T(8,128)(2,1)S(1)} %add_convert_fusion.hidden_ref), channel_id=1, source_target_pairs={{2,4},{4,2},{6,8},{8,6},{10,12},{12,10},{14,16},{16,14},{18,20},{2... | collective-permute-start | bytes 884744 | tf_op jit(solution)/shard_map/ppermute | solution.py:390
  59.7 0.0 collective-permute-done.14.near_ref
  59.7 4.8 %collective-permute-done.15.far_ref = bf16[576,256]{1,0:T(8,128)(2,1)S(1)} collective-permute-done((bf16[576,256]{1,0:T(8,128)(2,1)S(1)}, bf16[576,256]{1,0:T(8,128)(2,1)S(1)}, u32[]{:S(2)}, u32[]{:S(2)}) %collective-permute-start.15) | collective-permute-done | bytes 294944 | tf_op jit(solution)/shard_map/ppermute | solution.py:390
  64.5 1.1 %shard_map.69.refs_0_ = bf16[576,512]{1,0:T(8,128)(2,1)} custom-call(f32[576,3]{1,0:T(8,128)S(1)} %bitcast.24, bf16[576,256]{1,0:T(8,128)(2,1)S(1)} %add_convert_fusion.1.hidden_ref, bf16[576,256]{1,0:T(8,128)(2,1)S(1)} %collective-permute-done.14.near_ref, bf16[576,256]{1,0:T(8,128)(2,1)S(1)} %collective-permute-done.15.far_ref), custom_call_target="tpu_custom_call" | custom-call | flops 10000000000 | bytes 1179648 | tf_op jit(solution)/shard_map/pallas_call | solution.py:300
  65.6 0.0 collective-permute-done.12.near_ref
  65.6 2.1 %collective-permute-done.13.far_ref = bf16[576,256]{1,0:T(8,128)(2,1)S(1)} collective-permute-done((bf16[576,256]{1,0:T(8,128)(2,1)S(1)}, bf16[576,256]{1,0:T(8,128)(2,1)S(1)}, u32[]{:S(2)}, u32[]{:S(2)}) %collective-permute-start.13) | collective-permute-done | bytes 294944 | tf_op jit(solution)/shard_map/ppermute | solution.py:390
  67.6 1.1 %shard_map.70 = bf16[576,512]{1,0:T(8,128)(2,1)} custom-call(f32[576,3]{1,0:T(8,128)S(1)} %bitcast.25, bf16[576,256]{1,0:T(8,128)(2,1)S(1)} %add_convert_fusion.hidden_ref, bf16[576,256]{1,0:T(8,128)(2,1)S(1)} %collective-permute-done.12.near_ref, bf16[576,256]{1,0:T(8,128)(2,1)S(1)} %collective-permute-done.13.far_ref, ...), custom_call_target="tpu_custom_call", output_to_operand_aliasing={{}: (4, {})} | custom-call | flops 10000000000 | bytes 1179648 | tf_op jit(solution)/shard_map/pallas_call | solution.py:300
  (16 shorter events, 0.2 us)
Async XLA Ops:
  1.1 2.7 %collective-permute-start.1 = (bf16[576,256]{1,0:T(8,128)(2,1)S(1)}, bf16[576,256]{1,0:T(8,128)(2,1)S(1)}, u32[]{:S(2)}, u32[]{:S(2)}) collective-permute-start(bf16[576,256]{1,0:T(8,128)(2,1)S(1)} %get-tuple-element.40), channel_id=1, source_target_pairs={{0,2},{2,0},{4,6},{6,4},{8,10},{10,8},{12,14},{14,12},{16,18},{18,... | collective-permute-start | bytes 884744 | tf_op jit(solution)/shard_map/ppermute | solution.py:31
  1.8 15.1 %collective-permute-start.3 = (bf16[576,512]{1,0:T(8,128)(2,1)}, bf16[576,512]{1,0:T(8,128)(2,1)S(1)}, u32[]{:S(2)}, u32[]{:S(2)}) collective-permute-start(bf16[576,512]{1,0:T(8,128)(2,1)} %bitcast.21), channel_id=1, source_target_pairs={{0,1},{1,0},{2,3},{3,2},{4,5},{5,4},{6,7},{7,6},{8,9},{9,8},{10,11... | collective-permute-start | bytes 1769480 | tf_op jit(solution)/shard_map/ppermute | solution.py:41
  3.9 5.3 %collective-permute-start = (bf16[576,128]{1,0:T(8,128)(2,1)S(1)}, bf16[576,128]{1,0:T(8,128)(2,1)}, u32[]{:S(2)}, u32[]{:S(2)}) collective-permute-start(bf16[576,128]{1,0:T(8,128)(2,1)S(1)} %broadcast_select_fusion), channel_id=1, source_target_pairs={{0,4},{2,6},{4,0},{6,2},{8,12},{10,14},{12,8},{14,10},{16,20},{18,... | collective-permute-start | bytes 442376 | tf_op jit(solution)/shard_map/cond/branch_1_fun/ppermute | solution.py:31
  9.2 4.4 %collective-permute-start.2 = (bf16[576,128]{1,0:T(8,128)(2,1)S(1)}, bf16[576,128]{1,0:T(8,128)(2,1)S(1)}, u32[]{:S(2)}, u32[]{:S(2)}) collective-permute-start(bf16[576,128]{1,0:T(8,128)(2,1)S(1)} %select_select_fusion), channel_id=1, source_target_pairs={{0,8},{2,10},{4,12},{6,14},{8,0},{10,2},{12,4},{14,6},{16,24},{18,... | collective-permute-start | bytes 442376 | tf_op jit(solution)/shard_map/ppermute | solution.py:31
  9.4 7.5 %copy-start.1 = (bf16[1,512,576]{1,2,0:T(8,128)(2,1)S(1)}, bf16[1,512,576]{1,2,0:T(8,128)(2,1)}, u32[]{:S(2)}) copy-start(bf16[1,512,576]{1,2,0:T(8,128)(2,1)} %param.8) | copy-start | bytes 1769476
  9.4 7.5 %copy-start.2 = (f32[3,1152]{1,0:T(4,128)S(1)}, f32[3,1152]{1,0:T(4,128)}, u32[]{:S(2)}) copy-start(f32[3,1152]{1,0:T(4,128)} %modulation_ref.5) | copy-start | bytes 41476
  13.6 8.8 %collective-permute-start.4 = (bf16[576,128]{1,0:T(8,128)(2,1)S(1)}, bf16[576,128]{1,0:T(8,128)(2,1)S(1)}, u32[]{:S(2)}, u32[]{:S(2)}) collective-permute-start(bf16[576,128]{1,0:T(8,128)(2,1)S(1)} %broadcast_select_fusion.5), channel_id=1, source_target_pairs={{0,16},{2,18},{4,20},{6,22},{8,24},{10,26},{12,28},{14,30},{16,0},... | collective-permute-start | bytes 442376 | tf_op jit(solution)/shard_map/ppermute | solution.py:31
  22.4 6.1 %collective-permute-start.5 = (bf16[576,128]{1,0:T(8,128)(2,1)S(1)}, bf16[576,128]{1,0:T(8,128)(2,1)S(1)}, u32[]{:S(2)}, u32[]{:S(2)}) collective-permute-start(bf16[576,128]{1,0:T(8,128)(2,1)S(1)} %broadcast_select_fusion.4.refs_0_), channel_id=1, source_target_pairs={{0,1},{1,0},{2,3},{3,2},{4,5},{5,4},{6,7},{7,6},{8,9},{9,8},{10,11... | collective-permute-start | bytes 442376 | tf_op jit(solution)/shard_map/ppermute | solution.py:41
  23.3 5.2 %collective-permute-start.6 = (bf16[576,128]{1,0:T(8,128)(2,1)S(1)}, bf16[576,128]{1,0:T(8,128)(2,1)S(1)}, u32[]{:S(2)}, u32[]{:S(2)}) collective-permute-start(bf16[576,128]{1,0:T(8,128)(2,1)S(1)} %broadcast_select_fusion.4.refs_0_), channel_id=1, source_target_pairs={{0,4},{1,5},{2,6},{3,7},{4,0},{5,1},{6,2},{7,3},{8,12},{9,13},{10,... | collective-permute-start | bytes 442376 | tf_op jit(solution)/shard_map/ppermute | solution.py:41
  25.0 6.2 %collective-permute-start.7 = (bf16[576,128]{1,0:T(8,128)(2,1)S(1)}, bf16[576,128]{1,0:T(8,128)(2,1)S(1)}, u32[]{:S(2)}, u32[]{:S(2)}) collective-permute-start(bf16[576,128]{1,0:T(8,128)(2,1)S(1)} %broadcast_select_fusion.4.refs_0_), channel_id=1, source_target_pairs={{0,5},{1,4},{2,7},{3,6},{4,1},{5,0},{6,3},{7,2},{8,13},{9,12},{10,... | collective-permute-start | bytes 442376 | tf_op jit(solution)/shard_map/ppermute | solution.py:41
  25.7 5.5 %copy-start = (bf16[3,1152,576]{1,2,0:T(8,128)(2,1)S(1)}, bf16[3,1152,576]{1,2,0:T(8,128)(2,1)}, u32[]{:S(2)}) copy-start(bf16[3,1152,576]{1,2,0:T(8,128)(2,1)} %param.10) | copy-start | bytes 11943940
  33.6 4.6 %collective-permute-start.8 = (bf16[8,256,128]{2,1,0:T(8,128)(2,1)S(1)}, bf16[8,256,128]{2,1,0:T(8,128)(2,1)S(1)}, u32[]{:S(2)}, u32[]{:S(2)}) collective-permute-start(bf16[8,256,128]{2,1,0:T(8,128)(2,1)S(1)} %get-tuple-element.50.k_ref), channel_id=1, source_target_pairs={{0,2},{2,0},{4,6},{6,4},{8,10},{10,8},{12,14},{14,12},{16,18},{18,... | collective-permute-start | bytes 1572872 | tf_op jit(solution)/shard_map/ppermute | solution.py:31
  36.2 2.0 %collective-permute-start.9 = (bf16[8,80,256]{2,1,0:T(8,128)(2,1)S(1)}, bf16[8,80,256]{2,1,0:T(8,128)(2,1)S(1)}, u32[]{:S(2)}, u32[]{:S(2)}) collective-permute-start(bf16[8,80,256]{2,1,0:T(8,128)(2,1)S(1)} %get-tuple-element.51.v_ref), channel_id=1, source_target_pairs={{0,2},{2,0},{4,6},{6,4},{8,10},{10,8},{12,14},{14,12},{16,18},{18,... | collective-permute-start | bytes 983048 | tf_op jit(solution)/shard_map/ppermute | solution.py:31
  38.2 4.2 %copy-start.4 = (f32[3,576]{1,0:T(4,128)S(1)}, f32[3,576]{1,0:T(4,128)}, u32[]{:S(2)}) copy-start(f32[3,576]{1,0:T(4,128)} %param.12) | copy-start | bytes 20740
  41.5 14.6 %copy-start.3 = (f32[576,256]{1,0:T(8,128)S(1)}, f32[576,256]{1,0:T(8,128)}, u32[]{:S(2)}) copy-start(f32[576,256]{1,0:T(8,128)} %get-tuple-element.57) | copy-start | bytes 1769476
  41.6 8.3 %collective-permute-start.10 = (bf16[576,256]{1,0:T(8,128)(2,1)S(1)}, bf16[576,256]{1,0:T(8,128)(2,1)S(1)}, u32[]{:S(2)}, u32[]{:S(2)}) collective-permute-start(bf16[576,256]{1,0:T(8,128)(2,1)S(1)} %bitcast.27), channel_id=1, source_target_pairs={{0,1},{1,0},{2,3},{3,2},{4,5},{5,4},{6,7},{7,6},{8,9},{9,8},{10,11... | collective-permute-start | bytes 884744 | tf_op jit(solution)/shard_map/ppermute | solution.py:41
  42.4 13.7 %collective-permute-start.11 = (bf16[576,256]{1,0:T(8,128)(2,1)S(1)}, bf16[576,256]{1,0:T(8,128)(2,1)S(1)}, u32[]{:S(2)}, u32[]{:S(2)}) collective-permute-start(bf16[576,256]{1,0:T(8,128)(2,1)S(1)} %bitcast.26), channel_id=1, source_target_pairs={{0,1},{1,0},{2,3},{3,2},{4,5},{5,4},{6,7},{7,6},{8,9},{9,8},{10,11... | collective-permute-start | bytes 884744 | tf_op jit(solution)/shard_map/ppermute | solution.py:41
  49.9 9.8 %collective-permute-start.14 = (bf16[576,256]{1,0:T(8,128)(2,1)S(1)}, bf16[576,256]{1,0:T(8,128)(2,1)S(1)}, u32[]{:S(2)}, u32[]{:S(2)}) collective-permute-start(bf16[576,256]{1,0:T(8,128)(2,1)S(1)} %add_convert_fusion.1.hidden_ref), channel_id=1, source_target_pairs={{0,2},{2,0},{4,6},{6,4},{8,10},{10,8},{12,14},{14,12},{16,18},{18,... | collective-permute-start | bytes 884744 | tf_op jit(solution)/shard_map/ppermute | solution.py:31
  52.0 12.5 %collective-permute-start.15 = (bf16[576,256]{1,0:T(8,128)(2,1)S(1)}, bf16[576,256]{1,0:T(8,128)(2,1)S(1)}, u32[]{:S(2)}, u32[]{:S(2)}) collective-permute-start(bf16[576,256]{1,0:T(8,128)(2,1)S(1)} %add_convert_fusion.1.hidden_ref), channel_id=1, source_target_pairs={{2,4},{4,2},{6,8},{8,6},{10,12},{12,10},{14,16},{16,14},{18,20},{2... | collective-permute-start | bytes 884744 | tf_op jit(solution)/shard_map/ppermute | solution.py:390
  56.2 9.4 %collective-permute-start.12 = (bf16[576,256]{1,0:T(8,128)(2,1)S(1)}, bf16[576,256]{1,0:T(8,128)(2,1)S(1)}, u32[]{:S(2)}, u32[]{:S(2)}) collective-permute-start(bf16[576,256]{1,0:T(8,128)(2,1)S(1)} %add_convert_fusion.hidden_ref), channel_id=1, source_target_pairs={{0,2},{2,0},{4,6},{6,4},{8,10},{10,8},{12,14},{14,12},{16,18},{18,... | collective-permute-start | bytes 884744 | tf_op jit(solution)/shard_map/ppermute | solution.py:31
  57.5 10.1 %collective-permute-start.13 = (bf16[576,256]{1,0:T(8,128)(2,1)S(1)}, bf16[576,256]{1,0:T(8,128)(2,1)S(1)}, u32[]{:S(2)}, u32[]{:S(2)}) collective-permute-start(bf16[576,256]{1,0:T(8,128)(2,1)S(1)} %add_convert_fusion.hidden_ref), channel_id=1, source_target_pairs={{2,4},{4,2},{6,8},{8,6},{10,12},{12,10},{14,16},{16,14},{18,20},{2... | collective-permute-start | bytes 884744 | tf_op jit(solution)/shard_map/ppermute | solution.py:390

commit v5 on v4

--- a/solution.py
+++ b/solution.py
@@ -229,8 +229,8 @@
             )
         attended[head * HS : (head + 1) * HS, :] = total[:HS] / total[HS : HS + 1]
 
+    gate = as_columns(modulation_ref)[:, 2:3]
     flash(heads, score, weigh, collect)
-    gate = as_columns(modulation_ref)[:, 2:3]
     me = me_ref[0]
     terms[...] = gate * jnp.dot(
         w_ref[...], attended[...].astype(jnp.bfloat16), preferred_element_type=jnp.float32

time: 68.9 us -> 68.9 us (level)
  no operation moved by 1% of the time
where the time goes in v5:
time: 68.9 us; the launch traced here: 68.7 us
  waiting for transfers between devices  29 us (42%)
  starting transfers between devices  18.2 us (26%)
  Pallas kernels  16.9 us (25%)
  local copies, waits for them, and re-layouts  2.34 us (3%)
  other arithmetic  1.38 us (2%)
  between operations  0.84 us (1%)
    ppermute x6, waiting for transfers between devices, shifted(): return lax.ppermute(block, ('tm', 'head'), route)  15.2 us
    ppermute x8, starting transfers between devices, exchanged(): return lax.ppermute(block, 'tm', [(i, i ^ bit) for i in range(count)])  8.46 us
    pallas_call x2, Pallas kernels, project(): pl.pallas_call(functools.partial(project_kernel, len(blocks), parts, with...  7.33 us
    ppermute x8, waiting for transfers between devices, exchanged(): return lax.ppermute(block, 'tm', [(i, i ^ bit) for i in range(count)])  6.94 us
    ppermute x2, waiting for transfers between devices, local(): lax.ppermute(hidden, ('tm', 'head'), odd)  6.84 us
    ppermute x6, starting transfers between devices, shifted(): return lax.ppermute(block, ('tm', 'head'), route)  6.22 us
    pallas_call x2, Pallas kernels, attend_block(): pl.pallas_call(block_kernel, out_shape=jax.ShapeDtypeStruct((heads, VALUE...  4.07 us
    ppermute x2, starting transfers between devices, local(): lax.ppermute(hidden, ('tm', 'head'), odd)  3.55 us
  transfers between devices with their start and end apart: 16, of which 10 were waited for; matrix products, arithmetic and copies ran while one was open for 4% of the time, Pallas kernels for 15%

profile of v5, /device:TPU:25, one launch (start us, length us, event | category | flops | bytes accessed | tf_op | source)
XLA Modules:
  0.0 68.7 jit_solution(5726315042457584959)
XLA Ops:
  0.0 1.1 %broadcast_select_fusion.1 = (bf16[576,256]{1,0:T(8,128)(2,1)S(1)}, bf16[576,256]{1,0:T(8,128)(2,1)S(1)}) fusion(pred[]{:T(512)S(6)} %eq.41, bf16[576,512]{1,0:T(8,128)(2,1)} %bitcast.20), kind=kLoop, calls=%fused_computation.3 | loop fusion | flops 294912 | bytes 1179649 | tf_op jit(solution)/shard_map/jit(_where)/select_n | solution.py:340
  1.1 0.7 %collective-permute-start.1 = (bf16[576,256]{1,0:T(8,128)(2,1)S(1)}, bf16[576,256]{1,0:T(8,128)(2,1)S(1)}, u32[]{:S(2)}, u32[]{:S(2)}) collective-permute-start(bf16[576,256]{1,0:T(8,128)(2,1)S(1)} %get-tuple-element.40), channel_id=1, source_target_pairs={{0,2},{2,0},{4,6},{6,4},{8,10},{10,8},{12,14},{14,12},{16,18},{18,... | collective-permute-start | bytes 884744 | tf_op jit(solution)/shard_map/ppermute | solution.py:31
  1.8 1.3 %collective-permute-start.3 = (bf16[576,512]{1,0:T(8,128)(2,1)}, bf16[576,512]{1,0:T(8,128)(2,1)S(1)}, u32[]{:S(2)}, u32[]{:S(2)}) collective-permute-start(bf16[576,512]{1,0:T(8,128)(2,1)} %bitcast.21), channel_id=1, source_target_pairs={{0,1},{1,0},{2,3},{3,2},{4,5},{5,4},{6,7},{7,6},{8,9},{9,8},{10,11... | collective-permute-start | bytes 1769480 | tf_op jit(solution)/shard_map/ppermute | solution.py:41
  3.8 0.0 collective-permute-done.1
  3.8 5.3 %conditional.1 = (bf16[576,128]{1,0:T(8,128)(2,1)}) conditional(s32[]{:T(128)} %bitcast.9, () %tuple.23, (pred[]{:T(512)}, bf16[576,128]{1,0:T(8,128)(2,1)S(1)}, bf16[576,128]{1,0:T(8,128)(2,1)S(1)}) %tuple.24), branch_computations={%region_0.1_spmd, %region_1.2_spmd} | conditional | flops 73728 | bytes 1032241 | solution.py:345
  3.9 1.3 %collective-permute-start = (bf16[576,128]{1,0:T(8,128)(2,1)S(1)}, bf16[576,128]{1,0:T(8,128)(2,1)}, u32[]{:S(2)}, u32[]{:S(2)}) collective-permute-start(bf16[576,128]{1,0:T(8,128)(2,1)S(1)} %broadcast_select_fusion), channel_id=1, source_target_pairs={{0,4},{2,6},{4,0},{6,2},{8,12},{10,14},{12,8},{14,10},{16,20},{18,... | collective-permute-start | bytes 442376 | tf_op jit(solution)/shard_map/cond/branch_1_fun/ppermute | solution.py:31
  5.2 4.0 %collective-permute-done = bf16[576,128]{1,0:T(8,128)(2,1)} collective-permute-done((bf16[576,128]{1,0:T(8,128)(2,1)S(1)}, bf16[576,128]{1,0:T(8,128)(2,1)}, u32[]{:S(2)}, u32[]{:S(2)}) %collective-permute-start) | collective-permute-done | bytes 147488 | tf_op jit(solution)/shard_map/cond/branch_1_fun/ppermute | solution.py:31
  9.2 0.2 collective-permute-start.2
  9.4 0.0 copy-start.2
  9.4 2.1 %copy.15 = bf16[576,1152]{0,1:T(8,128)(2,1)S(1)} copy(bf16[576,1152]{1,0:T(8,128)(2,1)} %param.11) | data formatting | bytes 2654208 | tf_op jit(solution)/shard_map/optimization_barrier | solution.py:315
  11.6 1.9 %collective-permute-done.2 = bf16[576,128]{1,0:T(8,128)(2,1)S(1)} collective-permute-done((bf16[576,128]{1,0:T(8,128)(2,1)S(1)}, bf16[576,128]{1,0:T(8,128)(2,1)S(1)}, u32[]{:S(2)}, u32[]{:S(2)}) %collective-permute-start.2) | collective-permute-done | bytes 147488 | tf_op jit(solution)/shard_map/ppermute | solution.py:31
  13.6 0.1 collective-permute-start.4
  13.7 3.3 %collective-permute-done.3.refs_1_ = bf16[576,512]{1,0:T(8,128)(2,1)S(1)} collective-permute-done((bf16[576,512]{1,0:T(8,128)(2,1)}, bf16[576,512]{1,0:T(8,128)(2,1)S(1)}, u32[]{:S(2)}, u32[]{:S(2)}) %collective-permute-start.3) | collective-permute-done | bytes 589856 | tf_op jit(solution)/shard_map/ppermute | solution.py:41
  17.0 0.0 copy-done.1
  17.0 5.0 %shard_map.64 = (bf16[8,128,512]{2,1,0:T(8,128)(2,1)S(1)}, bf16[8,512,128]{2,1,0:T(8,128)(2,1)S(1)}, bf16[8,80,512]{2,1,0:T(8,128)(2,1)S(1)}) custom-call(s32[2]{0:T(128)S(1)} %and_select_fusion.order_ref, f32[3,1152]{1,0:T(4,128)S(1)} %copy-done.2, bf16[3,576,1152]{2,1,0:T(8,128)(2,1)} %bitcast.17, bf16[576,512]{1,0:T(8,128)(2,1)S(1)} %bitcast.22, ...), custom_call_target="tpu_custom_call" | custom-call | flops 2038431744 | bytes 7127040 | tf_op jit(solution)/shard_map/pallas_call | solution.py:111
  21.9 0.4 collective-permute-done.4
  22.4 0.9 %collective-permute-start.5 = (bf16[576,128]{1,0:T(8,128)(2,1)S(1)}, bf16[576,128]{1,0:T(8,128)(2,1)S(1)}, u32[]{:S(2)}, u32[]{:S(2)}) collective-permute-start(bf16[576,128]{1,0:T(8,128)(2,1)S(1)} %broadcast_select_fusion.4.refs_0_), channel_id=1, source_target_pairs={{0,1},{1,0},{2,3},{3,2},{4,5},{5,4},{6,7},{7,6},{8,9},{9,8},{10,11... | collective-permute-start | bytes 442376 | tf_op jit(solution)/shard_map/ppermute | solution.py:41
  23.3 1.7 %collective-permute-start.6 = (bf16[576,128]{1,0:T(8,128)(2,1)S(1)}, bf16[576,128]{1,0:T(8,128)(2,1)S(1)}, u32[]{:S(2)}, u32[]{:S(2)}) collective-permute-start(bf16[576,128]{1,0:T(8,128)(2,1)S(1)} %broadcast_select_fusion.4.refs_0_), channel_id=1, source_target_pairs={{0,4},{1,5},{2,6},{3,7},{4,0},{5,1},{6,2},{7,3},{8,12},{9,13},{10,... | collective-permute-start | bytes 442376 | tf_op jit(solution)/shard_map/ppermute | solution.py:41
  25.0 0.7 %collective-permute-start.7 = (bf16[576,128]{1,0:T(8,128)(2,1)S(1)}, bf16[576,128]{1,0:T(8,128)(2,1)S(1)}, u32[]{:S(2)}, u32[]{:S(2)}) collective-permute-start(bf16[576,128]{1,0:T(8,128)(2,1)S(1)} %broadcast_select_fusion.4.refs_0_), channel_id=1, source_target_pairs={{0,5},{1,4},{2,7},{3,6},{4,1},{5,0},{6,3},{7,2},{8,13},{9,12},{10,... | collective-permute-start | bytes 442376 | tf_op jit(solution)/shard_map/ppermute | solution.py:41
  25.7 2.8 %shard_map.65.refs_0_ = f32[8,80,512]{2,1,0:T(8,128)S(1)} custom-call(bf16[8,128,512]{2,1,0:T(8,128)(2,1)S(1)} %get-tuple-element.46.q_ref, bf16[8,512,128]{2,1,0:T(8,128)(2,1)S(1)} %get-tuple-element.47.k_ref, bf16[8,80,512]{2,1,0:T(8,128)(2,1)S(1)} %get-tuple-element.48.v_ref), custom_call_target="tpu_custom_call" | custom-call | flops 1073741824 | bytes 4194304 | tf_op jit(solution)/shard_map/pallas_call | solution.py:173
  28.5 0.0 collective-permute-done.5.refs_1_
  28.5 0.0 collective-permute-done.6.refs_2_
  28.5 2.7 %collective-permute-done.7.refs_3_ = bf16[576,128]{1,0:T(8,128)(2,1)S(1)} collective-permute-done((bf16[576,128]{1,0:T(8,128)(2,1)S(1)}, bf16[576,128]{1,0:T(8,128)(2,1)S(1)}, u32[]{:S(2)}, u32[]{:S(2)}) %collective-permute-start.7) | collective-permute-done | bytes 147488 | tf_op jit(solution)/shard_map/ppermute | solution.py:41
  31.2 2.3 %shard_map.66 = (bf16[8,256,128]{2,1,0:T(8,128)(2,1)S(1)}, bf16[8,80,256]{2,1,0:T(8,128)(2,1)S(1)}) custom-call(s32[2]{0:T(128)S(1)} %and_select_fusion.order_ref, f32[3,1152]{1,0:T(4,128)S(1)} %copy-done.2, bf16[3,576,1152]{2,1,0:T(8,128)(2,1)S(1)} %bitcast.18, bf16[576,128]{1,0:T(8,128)(2,1)S(1)} %broadcast_select_fusion.4.refs_0_, ...), custom_call_target="tpu_custom_call" | custom-call | flops 679477248 | bytes 3702784 | tf_op jit(solution)/shard_map/pallas_call | solution.py:111
  33.6 2.6 %collective-permute-start.8 = (bf16[8,256,128]{2,1,0:T(8,128)(2,1)S(1)}, bf16[8,256,128]{2,1,0:T(8,128)(2,1)S(1)}, u32[]{:S(2)}, u32[]{:S(2)}) collective-permute-start(bf16[8,256,128]{2,1,0:T(8,128)(2,1)S(1)} %get-tuple-element.50.k_ref), channel_id=1, source_target_pairs={{0,2},{2,0},{4,6},{6,4},{8,10},{10,8},{12,14},{14,12},{16,18},{18,... | collective-permute-start | bytes 1572872 | tf_op jit(solution)/shard_map/ppermute | solution.py:31
  36.2 0.1 collective-permute-start.9
  36.3 1.3 %shard_map.67.state_ref = f32[8,80,512]{2,1,0:T(8,128)S(1)} custom-call(bf16[8,128,512]{2,1,0:T(8,128)(2,1)S(1)} %get-tuple-element.46.q_ref, bf16[8,256,128]{2,1,0:T(8,128)(2,1)S(1)} %get-tuple-element.50.k_ref, bf16[8,80,256]{2,1,0:T(8,128)(2,1)S(1)} %get-tuple-element.51.v_ref, f32[8,80,512]{2,1,0:T(8,128)S(1)} %shard_map.65.refs_0_), custom_call_target="tpu_custom_call" | custom-call | flops 1073741824 | bytes 4194304 | tf_op jit(solution)/shard_map/pallas_call | solution.py:173
  37.6 0.6 collective-permute-done.9.refs_1_
  38.2 0.0 collective-permute-done.8.refs_0_
  38.2 3.3 %shard_map.68 = (f32[576,256]{1,0:T(8,128)S(1)}, f32[576,256]{1,0:T(8,128)}, bf16[1,576,256]{2,1,0:T(8,128)(2,1)S(1)}, bf16[1,576,256]{2,1,0:T(8,128)(2,1)S(1)}) custom-call(s32[1]{0:T(128)} %bitcast.1.me_ref, f32[3,1152]{1,0:T(4,128)S(1)} %copy-done.2, bf16[576,512]{1,0:T(8,128)(2,1)S(1)} %bitcast.23, bf16[8,128,512]{2,1,0:T(8,128)(2,1)S(1)} %get-tuple-element.46.q_ref, ...), custom_call_target="tpu_custom_call" | custom-call | flops 1753219072 | bytes 5521408 | tf_op jit(solution)/shard_map/pallas_call | solution.py:258
  41.5 0.0 copy-start.3
  41.6 0.9 %collective-permute-start.10 = (bf16[576,256]{1,0:T(8,128)(2,1)S(1)}, bf16[576,256]{1,0:T(8,128)(2,1)S(1)}, u32[]{:S(2)}, u32[]{:S(2)}) collective-permute-start(bf16[576,256]{1,0:T(8,128)(2,1)S(1)} %bitcast.27), channel_id=1, source_target_pairs={{0,1},{1,0},{2,3},{3,2},{4,5},{5,4},{6,7},{7,6},{8,9},{9,8},{10,11... | collective-permute-start | bytes 884744 | tf_op jit(solution)/shard_map/ppermute | solution.py:41
  42.4 0.7 %collective-permute-start.11 = (bf16[576,256]{1,0:T(8,128)(2,1)S(1)}, bf16[576,256]{1,0:T(8,128)(2,1)S(1)}, u32[]{:S(2)}, u32[]{:S(2)}) collective-permute-start(bf16[576,256]{1,0:T(8,128)(2,1)S(1)} %bitcast.26), channel_id=1, source_target_pairs={{0,1},{1,0},{2,3},{3,2},{4,5},{5,4},{6,7},{7,6},{8,9},{9,8},{10,11... | collective-permute-start | bytes 884744 | tf_op jit(solution)/shard_map/ppermute | solution.py:41
  43.2 6.7 %collective-permute-done.10 = bf16[576,256]{1,0:T(8,128)(2,1)S(1)} collective-permute-done((bf16[576,256]{1,0:T(8,128)(2,1)S(1)}, bf16[576,256]{1,0:T(8,128)(2,1)S(1)}, u32[]{:S(2)}, u32[]{:S(2)}) %collective-permute-start.10) | collective-permute-done | bytes 294944 | tf_op jit(solution)/shard_map/ppermute | solution.py:41
  49.8 0.1 add_convert_fusion.1.hidden_ref
  49.9 2.1 %collective-permute-start.14 = (bf16[576,256]{1,0:T(8,128)(2,1)S(1)}, bf16[576,256]{1,0:T(8,128)(2,1)S(1)}, u32[]{:S(2)}, u32[]{:S(2)}) collective-permute-start(bf16[576,256]{1,0:T(8,128)(2,1)S(1)} %add_convert_fusion.1.hidden_ref), channel_id=1, source_target_pairs={{0,2},{2,0},{4,6},{6,4},{8,10},{10,8},{12,14},{14,12},{16,18},{18,... | collective-permute-start | bytes 884744 | tf_op jit(solution)/shard_map/ppermute | solution.py:31
  52.0 1.4 %collective-permute-start.15 = (bf16[576,256]{1,0:T(8,128)(2,1)S(1)}, bf16[576,256]{1,0:T(8,128)(2,1)S(1)}, u32[]{:S(2)}, u32[]{:S(2)}) collective-permute-start(bf16[576,256]{1,0:T(8,128)(2,1)S(1)} %add_convert_fusion.1.hidden_ref), channel_id=1, source_target_pairs={{2,4},{4,2},{6,8},{8,6},{10,12},{12,10},{14,16},{16,14},{18,20},{2... | collective-permute-start | bytes 884744 | tf_op jit(solution)/shard_map/ppermute | solution.py:390
  53.4 0.2 copy.14
  53.6 2.6 %collective-permute-done.11 = bf16[576,256]{1,0:T(8,128)(2,1)S(1)} collective-permute-done((bf16[576,256]{1,0:T(8,128)(2,1)S(1)}, bf16[576,256]{1,0:T(8,128)(2,1)S(1)}, u32[]{:S(2)}, u32[]{:S(2)}) %collective-permute-start.11) | collective-permute-done | bytes 294944 | tf_op jit(solution)/shard_map/ppermute | solution.py:41
  56.2 0.1 add_convert_fusion.hidden_ref
  56.2 1.3 %collective-permute-start.12 = (bf16[576,256]{1,0:T(8,128)(2,1)S(1)}, bf16[576,256]{1,0:T(8,128)(2,1)S(1)}, u32[]{:S(2)}, u32[]{:S(2)}) collective-permute-start(bf16[576,256]{1,0:T(8,128)(2,1)S(1)} %add_convert_fusion.hidden_ref), channel_id=1, source_target_pairs={{0,2},{2,0},{4,6},{6,4},{8,10},{10,8},{12,14},{14,12},{16,18},{18,... | collective-permute-start | bytes 884744 | tf_op jit(solution)/shard_map/ppermute | solution.py:31
  57.5 2.2 %collective-permute-start.13 = (bf16[576,256]{1,0:T(8,128)(2,1)S(1)}, bf16[576,256]{1,0:T(8,128)(2,1)S(1)}, u32[]{:S(2)}, u32[]{:S(2)}) collective-permute-start(bf16[576,256]{1,0:T(8,128)(2,1)S(1)} %add_convert_fusion.hidden_ref), channel_id=1, source_target_pairs={{2,4},{4,2},{6,8},{8,6},{10,12},{12,10},{14,16},{16,14},{18,20},{2... | collective-permute-start | bytes 884744 | tf_op jit(solution)/shard_map/ppermute | solution.py:390
  59.7 0.0 collective-permute-done.14.near_ref
  59.7 4.8 %collective-permute-done.15.far_ref = bf16[576,256]{1,0:T(8,128)(2,1)S(1)} collective-permute-done((bf16[576,256]{1,0:T(8,128)(2,1)S(1)}, bf16[576,256]{1,0:T(8,128)(2,1)S(1)}, u32[]{:S(2)}, u32[]{:S(2)}) %collective-permute-start.15) | collective-permute-done | bytes 294944 | tf_op jit(solution)/shard_map/ppermute | solution.py:390
  64.5 1.1 %shard_map.69.refs_0_ = bf16[576,512]{1,0:T(8,128)(2,1)} custom-call(f32[576,3]{1,0:T(8,128)S(1)} %bitcast.24, bf16[576,256]{1,0:T(8,128)(2,1)S(1)} %add_convert_fusion.1.hidden_ref, bf16[576,256]{1,0:T(8,128)(2,1)S(1)} %collective-permute-done.14.near_ref, bf16[576,256]{1,0:T(8,128)(2,1)S(1)} %collective-permute-done.15.far_ref), custom_call_target="tpu_custom_call" | custom-call | flops 10000000000 | bytes 1179648 | tf_op jit(solution)/shard_map/pallas_call | solution.py:300
  65.6 0.0 collective-permute-done.12.near_ref
  65.6 2.1 %collective-permute-done.13.far_ref = bf16[576,256]{1,0:T(8,128)(2,1)S(1)} collective-permute-done((bf16[576,256]{1,0:T(8,128)(2,1)S(1)}, bf16[576,256]{1,0:T(8,128)(2,1)S(1)}, u32[]{:S(2)}, u32[]{:S(2)}) %collective-permute-start.13) | collective-permute-done | bytes 294944 | tf_op jit(solution)/shard_map/ppermute | solution.py:390
  67.6 1.1 %shard_map.70 = bf16[576,512]{1,0:T(8,128)(2,1)} custom-call(f32[576,3]{1,0:T(8,128)S(1)} %bitcast.25, bf16[576,256]{1,0:T(8,128)(2,1)S(1)} %add_convert_fusion.hidden_ref, bf16[576,256]{1,0:T(8,128)(2,1)S(1)} %collective-permute-done.12.near_ref, bf16[576,256]{1,0:T(8,128)(2,1)S(1)} %collective-permute-done.13.far_ref, ...), custom_call_target="tpu_custom_call", output_to_operand_aliasing={{}: (4, {})} | custom-call | flops 10000000000 | bytes 1179648 | tf_op jit(solution)/shard_map/pallas_call | solution.py:300
  (16 shorter events, 0.2 us)
Async XLA Ops:
  1.1 2.7 %collective-permute-start.1 = (bf16[576,256]{1,0:T(8,128)(2,1)S(1)}, bf16[576,256]{1,0:T(8,128)(2,1)S(1)}, u32[]{:S(2)}, u32[]{:S(2)}) collective-permute-start(bf16[576,256]{1,0:T(8,128)(2,1)S(1)} %get-tuple-element.40), channel_id=1, source_target_pairs={{0,2},{2,0},{4,6},{6,4},{8,10},{10,8},{12,14},{14,12},{16,18},{18,... | collective-permute-start | bytes 884744 | tf_op jit(solution)/shard_map/ppermute | solution.py:31
  1.8 15.1 %collective-permute-start.3 = (bf16[576,512]{1,0:T(8,128)(2,1)}, bf16[576,512]{1,0:T(8,128)(2,1)S(1)}, u32[]{:S(2)}, u32[]{:S(2)}) collective-permute-start(bf16[576,512]{1,0:T(8,128)(2,1)} %bitcast.21), channel_id=1, source_target_pairs={{0,1},{1,0},{2,3},{3,2},{4,5},{5,4},{6,7},{7,6},{8,9},{9,8},{10,11... | collective-permute-start | bytes 1769480 | tf_op jit(solution)/shard_map/ppermute | solution.py:41
  3.9 5.3 %collective-permute-start = (bf16[576,128]{1,0:T(8,128)(2,1)S(1)}, bf16[576,128]{1,0:T(8,128)(2,1)}, u32[]{:S(2)}, u32[]{:S(2)}) collective-permute-start(bf16[576,128]{1,0:T(8,128)(2,1)S(1)} %broadcast_select_fusion), channel_id=1, source_target_pairs={{0,4},{2,6},{4,0},{6,2},{8,12},{10,14},{12,8},{14,10},{16,20},{18,... | collective-permute-start | bytes 442376 | tf_op jit(solution)/shard_map/cond/branch_1_fun/ppermute | solution.py:31
  9.2 4.4 %collective-permute-start.2 = (bf16[576,128]{1,0:T(8,128)(2,1)S(1)}, bf16[576,128]{1,0:T(8,128)(2,1)S(1)}, u32[]{:S(2)}, u32[]{:S(2)}) collective-permute-start(bf16[576,128]{1,0:T(8,128)(2,1)S(1)} %select_select_fusion), channel_id=1, source_target_pairs={{0,8},{2,10},{4,12},{6,14},{8,0},{10,2},{12,4},{14,6},{16,24},{18,... | collective-permute-start | bytes 442376 | tf_op jit(solution)/shard_map/ppermute | solution.py:31
  9.4 7.5 %copy-start.1 = (bf16[1,512,576]{1,2,0:T(8,128)(2,1)S(1)}, bf16[1,512,576]{1,2,0:T(8,128)(2,1)}, u32[]{:S(2)}) copy-start(bf16[1,512,576]{1,2,0:T(8,128)(2,1)} %param.8) | copy-start | bytes 1769476
  9.4 7.5 %copy-start.2 = (f32[3,1152]{1,0:T(4,128)S(1)}, f32[3,1152]{1,0:T(4,128)}, u32[]{:S(2)}) copy-start(f32[3,1152]{1,0:T(4,128)} %modulation_ref.5) | copy-start | bytes 41476
  13.6 8.8 %collective-permute-start.4 = (bf16[576,128]{1,0:T(8,128)(2,1)S(1)}, bf16[576,128]{1,0:T(8,128)(2,1)S(1)}, u32[]{:S(2)}, u32[]{:S(2)}) collective-permute-start(bf16[576,128]{1,0:T(8,128)(2,1)S(1)} %broadcast_select_fusion.5), channel_id=1, source_target_pairs={{0,16},{2,18},{4,20},{6,22},{8,24},{10,26},{12,28},{14,30},{16,0},... | collective-permute-start | bytes 442376 | tf_op jit(solution)/shard_map/ppermute | solution.py:31
  22.4 6.1 %collective-permute-start.5 = (bf16[576,128]{1,0:T(8,128)(2,1)S(1)}, bf16[576,128]{1,0:T(8,128)(2,1)S(1)}, u32[]{:S(2)}, u32[]{:S(2)}) collective-permute-start(bf16[576,128]{1,0:T(8,128)(2,1)S(1)} %broadcast_select_fusion.4.refs_0_), channel_id=1, source_target_pairs={{0,1},{1,0},{2,3},{3,2},{4,5},{5,4},{6,7},{7,6},{8,9},{9,8},{10,11... | collective-permute-start | bytes 442376 | tf_op jit(solution)/shard_map/ppermute | solution.py:41
  23.3 5.2 %collective-permute-start.6 = (bf16[576,128]{1,0:T(8,128)(2,1)S(1)}, bf16[576,128]{1,0:T(8,128)(2,1)S(1)}, u32[]{:S(2)}, u32[]{:S(2)}) collective-permute-start(bf16[576,128]{1,0:T(8,128)(2,1)S(1)} %broadcast_select_fusion.4.refs_0_), channel_id=1, source_target_pairs={{0,4},{1,5},{2,6},{3,7},{4,0},{5,1},{6,2},{7,3},{8,12},{9,13},{10,... | collective-permute-start | bytes 442376 | tf_op jit(solution)/shard_map/ppermute | solution.py:41
  25.0 6.2 %collective-permute-start.7 = (bf16[576,128]{1,0:T(8,128)(2,1)S(1)}, bf16[576,128]{1,0:T(8,128)(2,1)S(1)}, u32[]{:S(2)}, u32[]{:S(2)}) collective-permute-start(bf16[576,128]{1,0:T(8,128)(2,1)S(1)} %broadcast_select_fusion.4.refs_0_), channel_id=1, source_target_pairs={{0,5},{1,4},{2,7},{3,6},{4,1},{5,0},{6,3},{7,2},{8,13},{9,12},{10,... | collective-permute-start | bytes 442376 | tf_op jit(solution)/shard_map/ppermute | solution.py:41
  25.7 5.5 %copy-start = (bf16[3,1152,576]{1,2,0:T(8,128)(2,1)S(1)}, bf16[3,1152,576]{1,2,0:T(8,128)(2,1)}, u32[]{:S(2)}) copy-start(bf16[3,1152,576]{1,2,0:T(8,128)(2,1)} %param.10) | copy-start | bytes 11943940
  33.6 4.6 %collective-permute-start.8 = (bf16[8,256,128]{2,1,0:T(8,128)(2,1)S(1)}, bf16[8,256,128]{2,1,0:T(8,128)(2,1)S(1)}, u32[]{:S(2)}, u32[]{:S(2)}) collective-permute-start(bf16[8,256,128]{2,1,0:T(8,128)(2,1)S(1)} %get-tuple-element.50.k_ref), channel_id=1, source_target_pairs={{0,2},{2,0},{4,6},{6,4},{8,10},{10,8},{12,14},{14,12},{16,18},{18,... | collective-permute-start | bytes 1572872 | tf_op jit(solution)/shard_map/ppermute | solution.py:31
  36.2 2.0 %collective-permute-start.9 = (bf16[8,80,256]{2,1,0:T(8,128)(2,1)S(1)}, bf16[8,80,256]{2,1,0:T(8,128)(2,1)S(1)}, u32[]{:S(2)}, u32[]{:S(2)}) collective-permute-start(bf16[8,80,256]{2,1,0:T(8,128)(2,1)S(1)} %get-tuple-element.51.v_ref), channel_id=1, source_target_pairs={{0,2},{2,0},{4,6},{6,4},{8,10},{10,8},{12,14},{14,12},{16,18},{18,... | collective-permute-start | bytes 983048 | tf_op jit(solution)/shard_map/ppermute | solution.py:31
  38.2 4.2 %copy-start.4 = (f32[3,576]{1,0:T(4,128)S(1)}, f32[3,576]{1,0:T(4,128)}, u32[]{:S(2)}) copy-start(f32[3,576]{1,0:T(4,128)} %param.12) | copy-start | bytes 20740
  41.5 14.6 %copy-start.3 = (f32[576,256]{1,0:T(8,128)S(1)}, f32[576,256]{1,0:T(8,128)}, u32[]{:S(2)}) copy-start(f32[576,256]{1,0:T(8,128)} %get-tuple-element.57) | copy-start | bytes 1769476
  41.6 8.3 %collective-permute-start.10 = (bf16[576,256]{1,0:T(8,128)(2,1)S(1)}, bf16[576,256]{1,0:T(8,128)(2,1)S(1)}, u32[]{:S(2)}, u32[]{:S(2)}) collective-permute-start(bf16[576,256]{1,0:T(8,128)(2,1)S(1)} %bitcast.27), channel_id=1, source_target_pairs={{0,1},{1,0},{2,3},{3,2},{4,5},{5,4},{6,7},{7,6},{8,9},{9,8},{10,11... | collective-permute-start | bytes 884744 | tf_op jit(solution)/shard_map/ppermute | solution.py:41
  42.4 13.7 %collective-permute-start.11 = (bf16[576,256]{1,0:T(8,128)(2,1)S(1)}, bf16[576,256]{1,0:T(8,128)(2,1)S(1)}, u32[]{:S(2)}, u32[]{:S(2)}) collective-permute-start(bf16[576,256]{1,0:T(8,128)(2,1)S(1)} %bitcast.26), channel_id=1, source_target_pairs={{0,1},{1,0},{2,3},{3,2},{4,5},{5,4},{6,7},{7,6},{8,9},{9,8},{10,11... | collective-permute-start | bytes 884744 | tf_op jit(solution)/shard_map/ppermute | solution.py:41
  49.9 9.8 %collective-permute-start.14 = (bf16[576,256]{1,0:T(8,128)(2,1)S(1)}, bf16[576,256]{1,0:T(8,128)(2,1)S(1)}, u32[]{:S(2)}, u32[]{:S(2)}) collective-permute-start(bf16[576,256]{1,0:T(8,128)(2,1)S(1)} %add_convert_fusion.1.hidden_ref), channel_id=1, source_target_pairs={{0,2},{2,0},{4,6},{6,4},{8,10},{10,8},{12,14},{14,12},{16,18},{18,... | collective-permute-start | bytes 884744 | tf_op jit(solution)/shard_map/ppermute | solution.py:31
  52.0 12.5 %collective-permute-start.15 = (bf16[576,256]{1,0:T(8,128)(2,1)S(1)}, bf16[576,256]{1,0:T(8,128)(2,1)S(1)}, u32[]{:S(2)}, u32[]{:S(2)}) collective-permute-start(bf16[576,256]{1,0:T(8,128)(2,1)S(1)} %add_convert_fusion.1.hidden_ref), channel_id=1, source_target_pairs={{2,4},{4,2},{6,8},{8,6},{10,12},{12,10},{14,16},{16,14},{18,20},{2... | collective-permute-start | bytes 884744 | tf_op jit(solution)/shard_map/ppermute | solution.py:390
  56.2 9.4 %collective-permute-start.12 = (bf16[576,256]{1,0:T(8,128)(2,1)S(1)}, bf16[576,256]{1,0:T(8,128)(2,1)S(1)}, u32[]{:S(2)}, u32[]{:S(2)}) collective-permute-start(bf16[576,256]{1,0:T(8,128)(2,1)S(1)} %add_convert_fusion.hidden_ref), channel_id=1, source_target_pairs={{0,2},{2,0},{4,6},{6,4},{8,10},{10,8},{12,14},{14,12},{16,18},{18,... | collective-permute-start | bytes 884744 | tf_op jit(solution)/shard_map/ppermute | solution.py:31
  57.5 10.1 %collective-permute-start.13 = (bf16[576,256]{1,0:T(8,128)(2,1)S(1)}, bf16[576,256]{1,0:T(8,128)(2,1)S(1)}, u32[]{:S(2)}, u32[]{:S(2)}) collective-permute-start(bf16[576,256]{1,0:T(8,128)(2,1)S(1)} %add_convert_fusion.hidden_ref), channel_id=1, source_target_pairs={{2,4},{4,2},{6,8},{8,6},{10,12},{12,10},{14,16},{16,14},{18,20},{2... | collective-permute-start | bytes 884744 | tf_op jit(solution)/shard_map/ppermute | solution.py:390
